TPU v7x, 512 devices: a whole 4x8x8 slice. The times are simulated.
512 devices in a mesh: gx: 16 (over y_hi, z), gy: 4 (over y_lo), gz: 8 (over x, core).
Axes of the slice: x: 4, y: 8 (y_hi: 2, y_lo: 4; y = y_hi * 4 + y_lo), z: 8, core: 2. Of those that a mesh axis runs over, the one named last changes fastest.
Arguments:
- gas_old: float32 [7, 32, 32, 1024], P(None, 'gx', 'gy', 'gz'), may hold values from -6 to 6
- diffusion: float32 [7], replicated, may hold values from 1 to 8
- stiffness: float32 [7], replicated, may hold values from 0.5 to 2
- weights: bfloat16 [8192, 128, 128], P(('gx', 'gy', 'gz')), may hold values from 0 to 0.015625
- velocity: bfloat16 [8192, 3, 128], P(('gx', 'gy', 'gz')), may hold values from -6 to 6
- rates: bfloat16 [8192, 128], P(('gx', 'gy', 'gz')), may hold values from 0.5 to 5
- destination: int32 [8192, 1], P(('gx', 'gy', 'gz')), may hold values from 0 to 15; in each aligned block of 16 rows (0 to 15, 16 to 31, ...) at most 2 rows name the same one
- tile_ids: int32 [8192], P(('gx', 'gy', 'gz')), may hold values from 0 to 15
Outputs:
- gas_new: float32 [7, 32, 32, 1024], P(None, 'gx', 'gy', 'gz')
- velocity_new: float32 [8192, 3, 128], P(('gx', 'gy', 'gz'))
Inputs may be any that keep to these rules, and one draw needn't show every extreme that they name: `destination`: the blocks held by one device name any one index of gx at most 2 times, and some device's blocks name some index exactly 2 times.
All inputs are finite; a program needn't handle non-finite values.
Results may differ from a plain program's by a relative error of at most 0.0018.
Values may be sent and summed in bfloat16 or wider, within the bound.
No kernel may reach another device: no remote copies, remote signals or barrier semaphores. Data moves between devices by JAX's collectives and lax.ppermute only.
A program may use at most 64 MiB of HBM per device.

v0:
```python
import jax
import jax.numpy as jnp
from jax import lax
from jax.sharding import PartitionSpec as P

NEWTON = 2
CGS = 3


def with_halo(block, sides, width):
    for axis, dim in sides:
        count = lax.axis_size(axis)
        forward = [(i, i + 1) for i in range(count - 1)]
        backward = [(target, source) for source, target in forward]
        low = lax.ppermute(
            lax.slice_in_dim(block, block.shape[dim] - width, None, axis=dim), axis, forward
        )
        high = lax.ppermute(lax.slice_in_dim(block, 0, width, axis=dim), axis, backward)
        block = jnp.concatenate([low, block, high], axis=dim)
    return block


def parcel_terms(weights, tiles, velocity, rates):
    wide = weights.astype(jnp.float32)
    gas_at = jnp.einsum("bpc,bfc->bfp", wide, tiles, precision=lax.Precision.HIGHEST)
    forces = rates[:, None, :] * (gas_at[:, 1:4] - velocity)
    evapor = 0.2 * rates / (1.0 + jnp.exp(gas_at[:, 5]))
    work = jnp.sum(forces * velocity, axis=1)
    rows = [evapor]
    for comp in range(3):
        rows.append(-forces[:, comp] + evapor * velocity[:, comp])
    rows.append(-work + evapor * gas_at[:, 4])
    rows.append(evapor)
    rows.append(evapor * gas_at[:, 6])
    rows.append(rates)
    sources = jnp.stack(rows, axis=1)
    deposit = jnp.einsum("bpc,bfp->bfc", wide, sources, precision=lax.Precision.HIGHEST)
    return (deposit, velocity + 0.2 * forces)


def neighbours(field):
    padded = with_halo(field, (("gx", 1), ("gy", 2), ("gz", 3)), 1)
    total = padded[:, 2:, 1:-1, 1:-1] + padded[:, :-2, 1:-1, 1:-1]
    total = total + padded[:, 1:-1, 2:, 1:-1] + padded[:, 1:-1, :-2, 1:-1]
    return total + padded[:, 1:-1, 1:-1, 2:] + padded[:, 1:-1, 1:-1, :-2]


def inner(left, right):
    local = jnp.sum(left * right, axis=(1, 2, 3))
    return lax.psum(local, ("gx", "gy", "gz"))[:, None, None, None]


def body(gas_old, diffusion, stiffness, weights, velocity, rates, destination, tile_ids):
    fields, size_x, size_y, size_z = gas_old.shape
    count = tile_ids.shape[0]
    peers = lax.axis_size("gx")
    capacity = max(2, (2 * count + peers - 1) // peers)
    slots_all = peers * capacity
    target_gx = destination[:, 0]
    order = jnp.arange(count, dtype=jnp.int32)
    earlier = order[:, None] > order[None, :]
    same = target_gx[:, None] == target_gx[None, :]
    ranked = jnp.sum((earlier & same).astype(jnp.int32), axis=1)
    slot = target_gx * capacity + ranked
    tiles_view = gas_old.reshape(fields, -1, 128)
    tile_total = tiles_view.shape[1]
    send_w = jnp.zeros((slots_all, 128, 128), jnp.bfloat16).at[slot].set(weights)
    send_v = jnp.zeros((slots_all, 3, 128), jnp.bfloat16).at[slot].set(velocity)
    send_r = jnp.zeros((slots_all, 128), jnp.bfloat16).at[slot].set(rates)
    send_t = jnp.zeros((slots_all,), jnp.bfloat16).at[slot].set(tile_ids.astype(jnp.bfloat16))
    got_w, got_v, got_r, got_t = (
        lax.all_to_all(send_w, "gx", split_axis=0, concat_axis=0, tiled=True),
        lax.all_to_all(send_v, "gx", split_axis=0, concat_axis=0, tiled=True),
        lax.all_to_all(send_r, "gx", split_axis=0, concat_axis=0, tiled=True),
        lax.all_to_all(send_t, "gx", split_axis=0, concat_axis=0, tiled=True),
    )
    got_ids = got_t.astype(jnp.int32)
    tiles = jnp.take(tiles_view, got_ids, axis=1).transpose(1, 0, 2)
    deposit, moved = parcel_terms(
        got_w, tiles, got_v.astype(jnp.float32), got_r.astype(jnp.float32)
    )
    back = lax.all_to_all(moved, "gx", split_axis=0, concat_axis=0, tiled=True)
    velocity_new = back[slot]
    source = jnp.zeros((fields + 1, tile_total, 128), jnp.float32)
    source = source.at[:, got_ids].add(deposit.transpose(1, 0, 2))
    source = source.reshape(fields + 1, size_x, size_y, size_z)
    index = jnp.arange(fields, dtype=jnp.int32)
    moment = ((index >= 1) & (index <= 3)).astype(jnp.float32)[:, None, None, None]
    damping = 1.0 + 0.5 * moment * source[fields][None]
    target = gas_old + 0.5 * source[:fields]
    coeff = diffusion[:, None, None, None]
    beta = stiffness[:, None, None, None]
    state = gas_old
    for newton in range(NEWTON):
        bent = jnp.tanh(state)
        resid = damping * state + beta * bent + coeff * (6.0 * state - neighbours(state)) - target
        diag = damping + beta * (1.0 - bent * bent) + 6.0 * coeff
        rvec = -resid
        direction = rvec
        step = jnp.zeros_like(state)
        norm_now = inner(rvec, rvec)
        for inner_it in range(CGS):
            image = diag * direction - coeff * neighbours(direction)
            alpha = norm_now / inner(direction, image)
            step = step + alpha * direction
            if inner_it + 1 < CGS:
                rvec = rvec - alpha * image
                norm_next = inner(rvec, rvec)
                direction = rvec + norm_next / norm_now * direction
                norm_now = norm_next
        state = state + step
    return (state, velocity_new)


def solution(mesh):
    return jax.shard_map(
        body,
        mesh=mesh,
        in_specs=(
            P(None, "gx", "gy", "gz"),
            P(),
            P(),
            P(("gx", "gy", "gz"), None, None),
            P(("gx", "gy", "gz"), None, None),
            P(("gx", "gy", "gz"), None),
            P(("gx", "gy", "gz"), None),
            P(("gx", "gy", "gz")),
        ),
        out_specs=(P(None, "gx", "gy", "gz"), P(("gx", "gy", "gz"), None, None)),
        check_vma=False,
    )
```

profile of v0, /device:TPU:1, one launch (start us, length us, event | category | flops | bytes accessed | tf_op | source)
XLA Modules:
  0.0 1329.0 jit_solution(16083485110300411714)
XLA Ops:
  3.5 16.2 %all-to-all-start = ((bf16[16,2,1]{1,2,0:T(2,128)(2,1)}), bf16[16,2,1]{1,2,0:T(2,128)(2,1)S(1)}, u32[]{:S(2)}, u32[]{:S(2)}) async-start(bf16[16,2,1]{1,2,0:T(2,128)(2,1)} %all_to_all.28), calls=%async_computation | async-start | bytes 16384 | tf_op jit(solution)/shard_map/all_to_all | solution.py:75
  21.1 9.8 all-to-all-done
  37.1 8.2 all-to-all-done.1
  45.3 3.5 all-to-all-start.3
  52.7 7.3 all-to-all-done.3
  60.0 4.2 all-to-all-start.2
  69.2 11.6 collective-permute-done
  82.1 4.0 collective-permute-start.3
  86.7 4.0 collective-permute-done.2
  90.9 7.9 collective-permute-start.5
  108.5 6.3 collective-permute-start.7
  117.1 4.5 collective-permute-start.9
  122.7 5.3 collective-permute-start.11
  131.0 4.4 collective-permute-done.10
  135.6 116.3 %all-reduce.1 = (f32[7]{0:T(128)S(1)}, f32[7]{0:T(128)S(1)}) all-reduce(f32[7]{0:T(128)S(1)} %get-tuple-element.13, f32[7]{0:T(128)S(1)} %get-tuple-element.12), channel_id=1, replica_groups=mesh['gx'=16,'gy'=4,'gz'=8] {'gx','gy','gz'}, use_global_device_ids=true, to_apply=%region_8.9 | all-reduce | flops 14 | bytes 112 | tf_op jit(solution)/shard_map/psum | solution.py:50
  252.1 95.5 %psum.86 = f32[7]{0:T(128)S(1)} all-reduce(f32[7]{0:T(128)S(1)} %get-tuple-element.29), channel_id=1, replica_groups=mesh['gx'=16,'gy'=4,'gz'=8] {'gx','gy','gz'}, use_global_device_ids=true, to_apply=%region_12.13 | all-reduce | flops 7 | bytes 56 | tf_op jit(solution)/shard_map/psum | solution.py:50
  349.0 4.0 collective-permute-start.13
  355.3 4.0 collective-permute-start.15
  360.3 5.6 collective-permute-start.17
  368.9 4.4 collective-permute-done.16
  373.6 105.5 %psum.87 = f32[7]{0:T(128)S(1)} all-reduce(f32[7]{0:T(128)S(1)} %get-tuple-element.27), channel_id=1, replica_groups=mesh['gx'=16,'gy'=4,'gz'=8] {'gx','gy','gz'}, use_global_device_ids=true, to_apply=%region_14.15 | all-reduce | flops 7 | bytes 56 | tf_op jit(solution)/shard_map/psum | solution.py:50
  479.3 95.3 %psum.88 = f32[7]{0:T(128)S(1)} all-reduce(f32[7]{0:T(128)S(1)} %multiply_reduce_fusion.6), channel_id=1, replica_groups=mesh['gx'=16,'gy'=4,'gz'=8] {'gx','gy','gz'}, use_global_device_ids=true, to_apply=%region_16.17 | all-reduce | flops 7 | bytes 56 | tf_op jit(solution)/shard_map/psum | solution.py:50
  576.0 4.0 collective-permute-start.19
  582.3 4.0 collective-permute-start.21
  587.3 5.8 collective-permute-start.23
  595.9 4.6 collective-permute-done.22
  600.7 104.9 %psum.89 = f32[7]{0:T(128)S(1)} all-reduce(f32[7]{0:T(128)S(1)} %fusion.41), channel_id=1, replica_groups=mesh['gx'=16,'gy'=4,'gz'=8] {'gx','gy','gz'}, use_global_device_ids=true, to_apply=%region_18.19 | all-reduce | flops 7 | bytes 56 | tf_op jit(solution)/shard_map/psum | solution.py:50
  707.1 4.0 collective-permute-start.25
  713.4 4.0 collective-permute-start.27
  718.4 6.5 collective-permute-start.29
  727.8 4.4 collective-permute-done.28
  733.7 4.6 collective-permute-start.31
  740.6 4.5 collective-permute-start.33
  752.5 4.4 collective-permute-done.34
  757.2 112.9 %all-reduce = (f32[7]{0:T(128)S(1)}, f32[7]{0:T(128)S(1)}) all-reduce(f32[7]{0:T(128)S(1)} %get-tuple-element.11, f32[7]{0:T(128)S(1)} %get-tuple-element.10), channel_id=1, replica_groups=mesh['gx'=16,'gy'=4,'gz'=8] {'gx','gy','gz'}, use_global_device_ids=true, to_apply=%region_20.21 | all-reduce | flops 14 | bytes 112 | tf_op jit(solution)/shard_map/psum | solution.py:50
  870.3 94.5 %psum.92 = f32[7]{0:T(128)S(1)} all-reduce(f32[7]{0:T(128)S(1)} %get-tuple-element.22), channel_id=1, replica_groups=mesh['gx'=16,'gy'=4,'gz'=8] {'gx','gy','gz'}, use_global_device_ids=true, to_apply=%region_24.25 | all-reduce | flops 7 | bytes 56 | tf_op jit(solution)/shard_map/psum | solution.py:50
  966.2 4.0 collective-permute-start.37
  972.5 4.0 collective-permute-start.39
  977.5 5.6 collective-permute-start.41
  986.1 4.4 collective-permute-done.40
  990.7 105.2 %psum.93 = f32[7]{0:T(128)S(1)} all-reduce(f32[7]{0:T(128)S(1)} %get-tuple-element.20), channel_id=1, replica_groups=mesh['gx'=16,'gy'=4,'gz'=8] {'gx','gy','gz'}, use_global_device_ids=true, to_apply=%region_26.27 | all-reduce | flops 7 | bytes 56 | tf_op jit(solution)/shard_map/psum | solution.py:50
  1096.2 95.3 %psum.94 = f32[7]{0:T(128)S(1)} all-reduce(f32[7]{0:T(128)S(1)} %multiply_reduce_fusion.1), channel_id=1, replica_groups=mesh['gx'=16,'gy'=4,'gz'=8] {'gx','gy','gz'}, use_global_device_ids=true, to_apply=%region_28.29 | all-reduce | flops 7 | bytes 56 | tf_op jit(solution)/shard_map/psum | solution.py:50
  1192.9 4.0 collective-permute-start.43
  1199.2 4.0 collective-permute-start.45
  1203.2 14.6 %all-to-all-start.4 = ((f32[32,3,128]{2,1,0:T(4,128)}), f32[32,3,128]{2,1,0:T(4,128)S(1)}, u32[]{:S(2)}, u32[]{:S(2)}) async-start(f32[32,3,128]{2,1,0:T(4,128)} %get-tuple-element.18), calls=%async_computation.4 | async-start | bytes 131072 | tf_op jit(solution)/shard_map/all_to_all | solution.py:82
  1218.0 5.6 collective-permute-start.47
  1225.6 3.5 all-to-all-done.4
  1232.1 96.2 %psum.95 = f32[7]{0:T(128)S(1)} all-reduce(f32[7]{0:T(128)S(1)} %fusion.9), channel_id=1, replica_groups=mesh['gx'=16,'gy'=4,'gz'=8] {'gx','gy','gz'}, use_global_device_ids=true, to_apply=%region_30.31 | all-reduce | flops 7 | bytes 56 | tf_op jit(solution)/shard_map/psum | solution.py:50
  (184 shorter events, 90.0 us)
Async XLA Ops:
  3.5 27.4 %all-to-all-start = ((bf16[16,2,1]{1,2,0:T(2,128)(2,1)}), bf16[16,2,1]{1,2,0:T(2,128)(2,1)S(1)}, u32[]{:S(2)}, u32[]{:S(2)}) async-start(bf16[16,2,1]{1,2,0:T(2,128)(2,1)} %all_to_all.28), calls=%async_computation | async-start | bytes 16384 | tf_op jit(solution)/shard_map/all_to_all | solution.py:75
  30.9 14.5 %all-to-all-start.1 = ((bf16[16,2,128]{2,1,0:T(2,128)(2,1)}), bf16[16,2,128]{2,1,0:T(2,128)(2,1)S(1)}, u32[]{:S(2)}, u32[]{:S(2)}) async-start(bf16[16,2,128]{2,1,0:T(2,128)(2,1)} %bitcast.4), calls=%async_computation.1 | async-start | bytes 16384 | tf_op jit(solution)/shard_map/all_to_all | solution.py:74
  45.3 14.7 %all-to-all-start.3 = ((bf16[32,3,128]{2,1,0:T(4,128)(2,1)}), bf16[32,3,128]{2,1,0:T(4,128)(2,1)S(1)}, u32[]{:S(2)}, u32[]{:S(2)}) async-start(bf16[32,3,128]{2,1,0:T(4,128)(2,1)} %scatter_fusion.1), calls=%async_computation.3 | async-start | bytes 65536 | tf_op jit(solution)/shard_map/all_to_all | solution.py:73
  60.0 40.7 %all-to-all-start.2 = ((bf16[32,128,128]{2,1,0:T(8,128)(2,1)}), bf16[32,128,128]{2,1,0:T(8,128)(2,1)S(1)}, u32[]{:S(2)}, u32[]{:S(2)}) async-start(bf16[32,128,128]{2,1,0:T(8,128)(2,1)} %scatter_fusion), calls=%async_computation.2 | async-start | bytes 2097152 | tf_op jit(solution)/shard_map/all_to_all | solution.py:72
  67.5 13.3 collective-permute-start
  80.8 9.9 collective-permute-start.2
  82.1 8.6 collective-permute-start.3
  90.9 15.4 %collective-permute-start.5 = (f32[7,4,10,1]{3,2,1,0:T(8,128)S(1)}, f32[7,4,10,1]{3,2,1,0:T(8,128)S(1)}, u32[]{:S(2)}, u32[]{:S(2)}) collective-permute-start(f32[7,4,10,1]{3,2,1,0:T(8,128)S(1)} %get-tuple-element.51), channel_id=1, source_target_pairs={{0,1},{1,2},{2,3},{3,4},{4,5},{5,6},{6,7},{8,9},{9,10},{10,11},{11... | collective-permute-start | bytes 3368 | tf_op jit(solution)/shard_map/ppermute | solution.py:15
  98.8 7.5 collective-permute-start.4
  107.2 7.6 collective-permute-start.6
  108.5 7.2 collective-permute-start.7
  115.8 5.9 collective-permute-start.8
  117.1 5.4 collective-permute-start.9
  122.7 8.3 collective-permute-start.11
  128.0 7.3 collective-permute-start.10
  347.7 5.3 collective-permute-start.12
  349.0 5.0 collective-permute-start.13
  354.0 5.3 collective-permute-start.14
  360.3 8.6 collective-permute-start.17
  366.0 7.3 collective-permute-start.16
  574.7 5.3 collective-permute-start.18
  576.0 5.0 collective-permute-start.19
  581.0 5.3 collective-permute-start.20
  587.3 8.6 collective-permute-start.23
  593.1 7.3 collective-permute-start.22
  705.8 5.3 collective-permute-start.24
  707.1 5.0 collective-permute-start.25
  712.1 5.3 collective-permute-start.26
  718.4 9.5 collective-permute-start.29
  724.9 7.3 collective-permute-start.28
  732.4 5.9 collective-permute-start.30
  733.7 5.5 collective-permute-start.31
  739.3 5.9 collective-permute-start.32
  740.6 5.4 collective-permute-start.33
  746.1 6.4 collective-permute-start.35
  749.6 7.3 collective-permute-start.34
  964.9 5.3 collective-permute-start.36
  966.2 5.0 collective-permute-start.37
  971.2 5.3 collective-permute-start.38
  977.5 8.6 collective-permute-start.41
  983.1 7.3 collective-permute-start.40
  1191.6 5.3 collective-permute-start.42
  1192.9 5.0 collective-permute-start.43
  1197.9 19.9 %collective-permute-start.44 = (f32[7,4,1,128]{3,2,1,0:T(1,128)S(1)}, f32[7,4,1,128]{3,2,1,0:T(1,128)S(1)}, u32[]{:S(2)}, u32[]{:S(2)}) collective-permute-start(f32[7,4,1,128]{3,2,1,0:T(1,128)S(1)} %get-tuple-element.56), channel_id=1, source_target_pairs={{8,0},{16,8},{24,16},{9,1},{17,9},{25,17},{10,2},{18,10},{26,18},{... | collective-permute-start | bytes 43016 | tf_op jit(solution)/shard_map/ppermute | solution.py:18
  1199.2 18.6 %collective-permute-start.45 = (f32[7,4,1,128]{3,2,1,0:T(1,128)S(1)}, f32[7,4,1,128]{3,2,1,0:T(1,128)S(1)}, u32[]{:S(2)}, u32[]{:S(2)}) collective-permute-start(f32[7,4,1,128]{3,2,1,0:T(1,128)S(1)} %get-tuple-element.55), channel_id=1, source_target_pairs={{0,8},{8,16},{16,24},{1,9},{9,17},{17,25},{2,10},{10,18},{18,26},{... | collective-permute-start | bytes 43016 | tf_op jit(solution)/shard_map/ppermute | solution.py:15
  1203.2 25.9 %all-to-all-start.4 = ((f32[32,3,128]{2,1,0:T(4,128)}), f32[32,3,128]{2,1,0:T(4,128)S(1)}, u32[]{:S(2)}, u32[]{:S(2)}) async-start(f32[32,3,128]{2,1,0:T(4,128)} %get-tuple-element.18), calls=%async_computation.4 | async-start | bytes 131072 | tf_op jit(solution)/shard_map/all_to_all | solution.py:82
  1218.0 11.7 collective-permute-start.47
  1223.6 7.6 collective-permute-start.46
  (12 other events, 54.2 us)
where the time goes:
time: 1330 us
  blocking collectives  1020 us (77%)
  starting transfers between devices  191 us (14%)
  waiting for transfers between devices  90.2 us (7%)
  local copies, waits for them, and re-layouts  14.5 us (1%)
    psum x10, blocking collectives, inner(): return lax.psum(local, ('gx', 'gy', 'gz'))[:, None, None, None]  1020 us
    ppermute x24, starting transfers between devices, with_halo(): lax.ppermute(lax.slice_in_dim(block, block.shape[dim] - width, None, axis...  113 us
    ppermute x24, waiting for transfers between devices, with_halo(): lax.ppermute(lax.slice_in_dim(block, 0, width, axis=dim), axis, backward)  43.8 us
    ppermute x24, starting transfers between devices, with_halo(): lax.ppermute(lax.slice_in_dim(block, 0, width, axis=dim), axis, backward)  36 us
  transfers between devices with their start and end apart: 53, of which 32 were waited for; matrix products, arithmetic and copies ran while one was open for 1% of the time, Pallas kernels for 0%

commit v1 on v0

v1 whole, which is shorter than its diff:
```python
import jax
import jax.numpy as jnp
from jax import lax
from jax.experimental import pallas as pl
from jax.experimental.pallas import tpu as pltpu
from jax.sharding import Mesh, PartitionSpec as P

F32 = jnp.float32
BF16 = jnp.bfloat16
FIELDS = 7
BLOCKS = 16
LANES = 128
NQ = 8
HALO = 8
CHUNK = 16
LIMIT = 48 * 1024 * 1024


def split(value):
    high = value.astype(BF16)
    low = (value - high.astype(F32)).astype(BF16)
    return high, low


def dot_nt(left, right):
    return lax.dot_general(left, right, (((1,), (1,)), ((), ())), preferred_element_type=F32)


def dot_nn(left, right):
    return lax.dot_general(left, right, (((1,), (0,)), ((), ())), preferred_element_type=F32)


def iota(shape, dim):
    return lax.broadcasted_iota(jnp.int32, shape, dim)


def parcel_kernel(
    dest, tile, gathered, gas, weights, velocity, rates, send, moved, tiles_buf, at_buf, source_buf, dep_buf
):
    tiles_buf[...] = jnp.zeros_like(tiles_buf)
    for b in range(BLOCKS):
        owner = dest[b]
        line = tile[b]
        for f in range(6):
            tiles_buf[b, pl.ds(f, 1), :] = gathered[owner, f, pl.ds(line, 1), :].astype(F32)
    for b in range(BLOCKS):
        high, low = split(tiles_buf[b])
        both = jnp.concatenate([high, low], axis=0)
        value = dot_nt(both, weights[b])
        at_buf[:, b, :] = value[:8] + value[8:]
    rate = rates[...].astype(F32)
    speed = velocity[...].astype(F32)
    evapor = 0.2 * rate / (1.0 + jnp.exp(at_buf[4]))
    work = jnp.zeros_like(rate)
    source_buf[:, 0, :] = evapor
    for k in range(3):
        vel = speed[:, k, :]
        force = rate * (at_buf[k] - vel)
        moved[:, k, :] = vel + 0.2 * force
        work = work + force * vel
        source_buf[:, 1 + k, :] = evapor * vel - force
    source_buf[:, 4, :] = evapor * at_buf[3] - work
    source_buf[:, 5, :] = evapor
    source_buf[:, 6, :] = evapor * at_buf[5]
    source_buf[:, 7, :] = rate
    for b in range(BLOCKS):
        high, low = split(source_buf[b])
        both = jnp.concatenate([high, low], axis=0)
        value = dot_nn(both, weights[b])
        dep_buf[:, b, :] = value[:8] + value[8:]
    lane = iota((8, LANES), 1)
    row = iota((8, LANES), 0)
    spot = jnp.zeros((8, LANES), F32)
    for b in range(BLOCKS):
        code = (tile[b] % 8) * 32 + dest[b] * 2 + tile[b] // 8
        mark = (row == b % 8) & ((lane // 64) == b // 8)
        spot = jnp.where(mark, code.astype(F32), spot)
    part = (lane % 64) // 16
    upper = lane >= 64
    for c in range(8):
        third = jnp.where(
            upper,
            pltpu.roll(dep_buf[7, 8:16], (96 - 16 * c) % LANES, 1),
            pltpu.roll(dep_buf[7, 0:8], (32 - 16 * c) % LANES, 1),
        )
        tail = jnp.where(part == 2, third, spot)
        for f in range(8):
            src = min(f, FIELDS - 1)
            first = jnp.where(
                upper,
                pltpu.roll(gas[src, 8:16], (64 - 16 * c) % LANES, 1),
                pltpu.roll(gas[src, 0:8], (-16 * c) % LANES, 1),
            )
            second = jnp.where(
                upper,
                pltpu.roll(dep_buf[src, 8:16], (80 - 16 * c) % LANES, 1),
                pltpu.roll(dep_buf[src, 0:8], (16 - 16 * c) % LANES, 1),
            )
            index = ((c // 4) * 8 + f) * 4 + c % 4
            send[index] = jnp.where(part == 0, first, jnp.where(part == 1, second, tail))


def expand_kernel(where, got, base):
    moment = ((where[0] >= 1) & (where[0] <= 3)).astype(F32)
    target = iota((256, 256), 0)
    k = iota((256, 256), 1)
    inner = k % 128
    perm = (target == (inner % 8) * 32 + (inner // 8) * 2 + k // 128).astype(F32).astype(BF16)
    gases = []
    for j in range(4):
        rows = got[:, j].reshape(LANES, LANES)
        flip = rows.T
        spot = jnp.concatenate([flip[48:49], flip[112:113]], axis=1).astype(jnp.int32)
        onehot = (target == spot).astype(F32).astype(BF16)
        dep = jnp.concatenate([flip[16:48], flip[80:112]], axis=1)
        high, low = split(dep)
        value = dot_nt(jnp.concatenate([high, low], axis=0), onehot)
        value = value[:32] + value[32:]
        gas = jnp.concatenate([flip[0:16], flip[64:80]], axis=1)
        high, low = split(gas)
        held = dot_nt(jnp.concatenate([high, low], axis=0), perm)
        held = held[:16] + held[16:]
        area = slice(j * 256, (j + 1) * 256)
        base[0, :, area] = held
        base[1, :, area] = held + 0.5 * value[:16]
        base[2, :, area] = 1.0 + 0.5 * moment * value[16:]


def gather_neighbours(blocks):
    shape = blocks[0].shape
    lane = iota(shape, 1)
    place = lane % 32
    ups = [pltpu.roll(v, 32, 1) for v in blocks]
    downs = [pltpu.roll(v, LANES - 32, 1) for v in blocks]
    zero = jnp.zeros(shape, F32)
    out = []
    for q in range(NQ):
        v = blocks[q]
        total = jnp.where(place == 0, 0.0, pltpu.roll(v, 1, 1))
        total = total + jnp.where(place == 31, 0.0, pltpu.roll(v, LANES - 1, 1))
        total = total + jnp.where(lane < 32, ups[q - 1] if q > 0 else zero, ups[q])
        total = total + jnp.where(lane >= 96, downs[q + 1] if q < NQ - 1 else zero, downs[q])
        total = total + pltpu.roll(v, 1, 0) + pltpu.roll(v, shape[0] - 1, 0)
        out.append(total)
    return out


def newton_terms(q, rhs, damp, diffusion, stiffness, mask):
    around = gather_neighbours(q)
    residual = []
    extra = []
    scale = 1.0 / (6.0 * diffusion)
    for n in range(NQ):
        bent = jnp.tanh(q[n])
        residual.append(
            mask * (rhs[n] - damp[n] * q[n] - stiffness * bent + diffusion * (around[n] - 6.0 * q[n]))
        )
        extra.append((damp[n] - 1.0 + stiffness * (0.5 - bent * bent)) * scale)

    def apply(v):
        near = gather_neighbours(v)
        return [mask * (extra[n] * v[n] - near[n] * (1.0 / 6.0)) for n in range(NQ)]

    one = apply(residual)
    two = apply(one)
    three = apply(two)
    rows = []
    for left, right in (
        (residual, residual), (residual, one), (one, one), (one, two), (two, two), (two, three)
    ):
        total = jnp.zeros((CHUNK, LANES), F32)
        for n in range(NQ):
            total = total + left[n][HALO:HALO + CHUNK] * right[n][HALO:HALO + CHUNK]
        rows.append(jnp.sum(total, axis=0, keepdims=True))
    rows.append(jnp.zeros((2, LANES), F32))
    table = jnp.sum(jnp.concatenate(rows, axis=0), axis=1, keepdims=True)
    pick = iota((8, LANES), 0) == iota((8, LANES), 1)
    line = jnp.sum(jnp.where(pick, table, 0.0), axis=0, keepdims=True)
    return residual, one, two, line


def coefficients(m, diffusion, stiffness):
    s = 6.0 * diffusion
    t = 6.0 * diffusion + 1.0 + 0.5 * stiffness
    alpha = m[0] / (t * m[0] + s * m[1])
    a = 1.0 - alpha * t
    b = -alpha * s
    next_norm = a * a * m[0] + 2.0 * a * b * m[1] + b * b * m[2]
    step0 = alpha
    p = a + next_norm / m[0]
    i0 = t * p
    i1 = t * b + s * p
    i2 = s * b
    curve = p * (i0 * m[0] + i1 * m[1] + i2 * m[2]) + b * (i0 * m[1] + i1 * m[2] + i2 * m[3])
    alpha = next_norm / curve
    step0 = step0 + alpha * p
    step1 = alpha * b
    c0 = a - alpha * i0
    c1 = b - alpha * i1
    c2 = -alpha * i2
    last_norm = (
        c0 * (c0 * m[0] + c1 * m[1] + c2 * m[2])
        + c1 * (c0 * m[1] + c1 * m[2] + c2 * m[3])
        + c2 * (c0 * m[2] + c1 * m[3] + c2 * m[4])
    )
    ratio = last_norm / next_norm
    e0 = c0 + ratio * p
    e1 = c1 + ratio * b
    e2 = c2
    i0 = t * e0
    i1 = t * e1 + s * e0
    i2 = t * e2 + s * e1
    i3 = s * e2
    curve = (
        e0 * (i0 * m[0] + i1 * m[1] + i2 * m[2] + i3 * m[3])
        + e1 * (i0 * m[1] + i1 * m[2] + i2 * m[3] + i3 * m[4])
        + e2 * (i0 * m[2] + i1 * m[3] + i2 * m[4] + i3 * m[5])
    )
    alpha = last_norm / curve
    return step0 + alpha * e0, step1 + alpha * e1, alpha * e2


def load(lower, base, upper, index):
    whole = jnp.concatenate([lower[index], base[index], upper[index]], axis=0)
    return [whole[:, n * LANES:(n + 1) * LANES] for n in range(NQ)]


def plane_mask(where):
    plane = iota((CHUNK + 2 * HALO, LANES), 0)
    outside = ((plane < HALO) & (where[1] == 0)) | ((plane >= HALO + CHUNK) & (where[1] == 63))
    return jnp.where(outside, 0.0, 1.0).astype(F32)


def first_kernel(where, diffusion, stiffness, lower, base, upper, basis, sums):
    field = jnp.minimum(where[0], FIELDS - 1)
    d = diffusion[field]
    beta = stiffness[field]
    q = load(lower, base, upper, 0)
    rhs = load(lower, base, upper, 1)
    damp = load(lower, base, upper, 2)
    zero, one, two, line = newton_terms(q, rhs, damp, jnp.full((1, 1), d), beta, plane_mask(where))
    for n in range(NQ):
        area = slice(n * LANES, (n + 1) * LANES)
        basis[0, :, area] = zero[n]
        basis[1, :, area] = one[n]
        basis[2, :, area] = two[n]
    sums[...] = jnp.broadcast_to(line[None], sums.shape)


def second_kernel(where, diffusion, stiffness, lower, base, upper, basis, got, send, state_buf):
    field = jnp.minimum(where[0], FIELDS - 1)
    d = jnp.full((1, 1), diffusion[field])
    beta = jnp.full((1, 1), stiffness[field])
    row = jnp.sum(got[...], axis=0)
    lane = iota((1, LANES), 1)
    m = [jnp.sum(jnp.where(lane == k, row, 0.0), axis=1, keepdims=True) for k in range(6)]
    k0, k1, k2 = coefficients(m, d, beta)
    q = load(lower, base, upper, 0)
    rhs = load(lower, base, upper, 1)
    damp = load(lower, base, upper, 2)
    state = []
    for n in range(NQ):
        area = slice(n * LANES, (n + 1) * LANES)
        state.append(q[n] + k0 * basis[0, :, area] + k1 * basis[1, :, area] + k2 * basis[2, :, area])
    zero, one, two, line = newton_terms(state, rhs, damp, d, beta, plane_mask(where))
    for n in range(NQ):
        area = slice(n * LANES, (n + 1) * LANES)
        for a, held in enumerate((state, zero, one, two)):
            state_buf[a * CHUNK:(a + 1) * CHUNK, area] = held[n][HALO:HALO + CHUNK]
    out = iota((LANES, 256), 0)
    k = iota((LANES, 256), 1)
    origin = (out % 8) * 32 + (out // 8) * 2
    perms = [(k == origin + x).astype(F32).astype(BF16) for x in range(2)]
    for j in range(4):
        high, low = split(state_buf[:, j * 256:(j + 1) * 256])
        sides = [dot_nt(perm, high) + dot_nt(perm, low) for perm in perms]
        send[:, j, 0:8, :] = jnp.concatenate(sides, axis=1).reshape(16, 8, LANES)
    send[:, :, 8:16, :] = jnp.broadcast_to(line[None, None], (16, 4, 8, LANES))


def collect_kernel(got, sums):
    first = iota((8, LANES), 0)
    table = jnp.zeros((8, LANES), F32)
    for f in range(8):
        total = jnp.zeros((8, LANES), F32)
        for l in range(2):
            for y in range(4):
                total = total + got[(l * 8 + f) * 4 + y, 8:16, :]
        table = jnp.where(first == f, total, table)
    sums[...] = jnp.broadcast_to(table[None], sums.shape)


def final_kernel(diffusion, stiffness, got, sums, out):
    table = jnp.sum(sums[...], axis=0)
    lane = iota((8, LANES), 1)
    row = iota((8, 1), 0)
    m = [jnp.sum(jnp.where(lane == k, table, 0.0), axis=1, keepdims=True) for k in range(6)]
    d = jnp.ones((8, 1), F32)
    beta = jnp.ones((8, 1), F32)
    for f in range(FIELDS):
        d = jnp.where(row == f, diffusion[f], d)
        beta = jnp.where(row == f, stiffness[f], beta)
    k0, k1, k2 = coefficients(m, d, beta)
    part = (lane % 64) // 16
    scale = jnp.where(part == 0, 1.0, jnp.where(part == 1, k0, jnp.where(part == 2, k1, k2)))
    for f in range(FIELDS):
        factor = scale[f:f + 1]
        low = jnp.zeros((8, LANES), F32)
        high = jnp.zeros((8, LANES), F32)
        for c in range(8):
            index = ((c // 4) * 8 + f) * 4 + c % 4
            value = got[index, 0:8, :] * factor
            value = value + pltpu.roll(value, 16, 1)
            value = value + pltpu.roll(value, 32, 1)
            here = (lane // 16) == c
            low = jnp.where(here, pltpu.roll(value, (16 * (c - 3)) % LANES, 1), low)
            high = jnp.where(here, pltpu.roll(value, (16 * (c - 7)) % LANES, 1), high)
        out[f, 0:8, :] = low
        out[f, 8:16, :] = high


def call(kernel, shapes, spaces, args, scratch=()):
    single = not isinstance(shapes, (list, tuple))
    listed = [shapes] if single else shapes
    result = pl.pallas_call(
        kernel,
        out_shape=listed,
        in_specs=[pl.BlockSpec(memory_space=pltpu.SMEM if s == "s" else pltpu.VMEM) for s in spaces],
        out_specs=[pl.BlockSpec(memory_space=pltpu.VMEM) for _ in listed],
        scratch_shapes=list(scratch),
        compiler_params=pltpu.CompilerParams(vmem_limit_bytes=LIMIT),
    )(*args)
    return result[0] if single else result


def shaped(*dims):
    return jax.ShapeDtypeStruct(dims, F32)


def chain():
    def device(f, place):
        gz, c = divmod(place, 8)
        l, gy = divmod(c, 4)
        return ((l * 8 + f) * 4 + gy) * 8 + gz

    return [(device(f, place), device(f, place + 1)) for f in range(8) for place in range(63)]


ALL = ("l", "f", "gy", "gz")
GX = ("l", "f")
PLANE = ("l", "f", "gy")
GROUP = ("l", "gy", "gz")


def exchange(value, axes):
    return lax.all_to_all(value, axes, 0, 0, tiled=True)


def body(gas_old, diffusion, stiffness, weights, velocity, rates, destination, tile_ids):
    place = lax.axis_index("gz") * 8 + lax.axis_index("l") * 4 + lax.axis_index("gy")
    where = jnp.stack([lax.axis_index("f"), place]).astype(jnp.int32)
    gas = gas_old.reshape(FIELDS, BLOCKS, LANES)
    gathered = exchange(jnp.broadcast_to(gas[None, 1:], (16, 6, BLOCKS, LANES)), GX)
    send, moved = call(
        parcel_kernel,
        [shaped(64, 8, LANES), shaped(BLOCKS, 3, LANES)],
        "ssvvvvv",
        (destination[:, 0], tile_ids, gathered, gas, weights, velocity, rates),
        [pltpu.VMEM((BLOCKS, 8, LANES), F32), pltpu.VMEM((8, BLOCKS, LANES), F32),
         pltpu.VMEM((BLOCKS, 8, LANES), F32), pltpu.VMEM((8, BLOCKS, LANES), F32)],
    )
    got = exchange(send, PLANE).reshape(16, 4, 8, LANES)
    base = call(expand_kernel, shaped(3, CHUNK, 1024), "sv", (where, got))
    forward = chain()
    backward = [(b, a) for a, b in forward]
    lower = lax.ppermute(base[:, HALO:], ALL, forward)
    upper = lax.ppermute(base[:, :HALO], ALL, backward)
    basis, sums = call(
        first_kernel,
        [shaped(3, CHUNK + 2 * HALO, 1024), shaped(64, 1, LANES)],
        "sssvvv",
        (where, diffusion, stiffness, lower, base, upper),
    )
    sums = exchange(sums, GROUP)
    send = call(
        second_kernel,
        shaped(16, 4, 16, LANES),
        "sssvvvvv",
        (where, diffusion, stiffness, lower, base, upper, basis, sums),
        [pltpu.VMEM((4 * CHUNK, 1024), F32)],
    )
    got = exchange(send.reshape(64, 16, LANES), PLANE)
    sums = call(collect_kernel, shaped(8, 8, LANES), "v", (got,))
    sums = exchange(sums, "gz")
    out = call(final_kernel, shaped(FIELDS, BLOCKS, LANES), "ssvv", (diffusion, stiffness, got, sums))
    return out.reshape(gas_old.shape), moved


def solution(mesh):
    fine = Mesh(mesh.devices.reshape(2, 8, 4, 8), ALL)
    blocks = ("l", "f", "gy", "gz")
    return jax.shard_map(
        body,
        mesh=fine,
        in_specs=(
            P(None, GX, "gy", "gz"),
            P(),
            P(),
            P(blocks, None, None),
            P(blocks, None, None),
            P(blocks, None),
            P(blocks, None),
            P(blocks),
        ),
        out_specs=(P(None, GX, "gy", "gz"), P(blocks, None, None)),
        check_vma=False,
    )
```

time: 1330 us -> 138 us (0.10)
  blocking collectives: 1020 us -> 43.7 us
  starting transfers between devices: 191 us -> 42.4 us
  waiting for transfers between devices: 90.2 us -> 38.6 us
    psum x10 -> x0, blocking collectives: 1020 us -> none  [inner(): return lax.psum(local, ('gx', 'gy', 'gz'))[:, None, None, None]]
    ppermute x48 -> x2, starting transfers between devices: 149 us -> 6.77 us  [the longest x1 4.41 us: body(): upper = lax.ppermute(base[:, :HALO], ALL, backward)]
    ppermute x48 -> x2, waiting for transfers between devices: 61.4 us -> 1.62 us  [the longest x1 1.26 us: body(): upper = lax.ppermute(base[:, :HALO], ALL, backward)]
    all_to_all x0 -> x2, blocking collectives: none -> 43.7 us  [exchange(): return lax.all_to_all(value, axes, 0, 0, tiled=True)]
    all_to_all x5 -> x3, waiting for transfers between devices: 28.8 us -> 37 us  [exchange(): return lax.all_to_all(value, axes, 0, 0, tiled=True)]
    all_to_all x5 -> x3, starting transfers between devices: 41.9 us -> 35.7 us  [exchange(): return lax.all_to_all(value, axes, 0, 0, tiled=True)]
  transfers between devices with their start and end apart: 53 -> 5, of which waited for: 32 -> 5; matrix products, arithmetic and copies ran while one was open for 1% -> 1% of each run, Pallas kernels for 0% -> 0%
where the time goes in v1:
time: 138 us; the launch traced here: 137 us
  blocking collectives  43.7 us (32%)
  starting transfers between devices  42.4 us (31%)
  waiting for transfers between devices  38.6 us (28%)
  Pallas kernels  8.46 us (6%)
  local copies, waits for them, and re-layouts  3.09 us (2%)
    all_to_all x2, blocking collectives, exchange(): return lax.all_to_all(value, axes, 0, 0, tiled=True)  43.7 us
    all_to_all x3, waiting for transfers between devices, exchange(): return lax.all_to_all(value, axes, 0, 0, tiled=True)  37 us
    all_to_all x3, starting transfers between devices, exchange(): return lax.all_to_all(value, axes, 0, 0, tiled=True)  35.7 us
    pallas_call x6, Pallas kernels, call(): pl.pallas_call(kernel, out_shape=listed, in_specs=[pl.BlockSpec(memory_sp...  8.46 us
    ppermute x1, starting transfers between devices, body(): upper = lax.ppermute(base[:, :HALO], ALL, backward)  4.41 us
  transfers between devices with their start and end apart: 5, of which 5 were waited for; matrix products, arithmetic and copies ran while one was open for 1% of the time, Pallas kernels for 0%

profile of v1, /device:TPU:1, one launch (start us, length us, event | category | flops | bytes accessed | tf_op | source)
XLA Modules:
  0.0 137.2 jit_solution(12903615912701573759)
XLA Ops:
  0.6 0.8 slice_bitcast_fusion
  1.4 1.0 broadcast_in_dim.9
  2.4 0.0 copy-start.7
  2.4 0.0 copy-start
  2.4 0.0 copy-start.1
  2.4 16.4 %all-to-all-start = ((f32[16,6,16,128]{3,2,1,0:T(8,128)}), f32[16,6,16,128]{3,2,1,0:T(8,128)S(1)}, u32[]{:S(2)}, u32[]{:S(2)}) async-start(f32[16,6,16,128]{3,2,1,0:T(8,128)} %broadcast_in_dim.9), calls=%async_computation | async-start | bytes 1572864 | tf_op jit(solution)/shard_map/all_to_all | solution.py:356
  18.8 0.0 copy-done.7
  18.8 0.0 copy-start.4
  18.8 20.3 %all-to-all-done.gathered = f32[16,6,16,128]{3,2,1,0:T(8,128)S(1)} async-done(((f32[16,6,16,128]{3,2,1,0:T(8,128)}), f32[16,6,16,128]{3,2,1,0:T(8,128)S(1)}, u32[]{:S(2)}, u32[]{:S(2)}) %all-to-all-start) | async-done | bytes 786464 | tf_op jit(solution)/shard_map/all_to_all | solution.py:356
  39.2 0.0 copy-start.5
  39.2 0.0 copy-start.6
  39.2 0.0 copy-done
  39.2 0.0 copy-done.1
  39.2 0.0 copy-done.4
  39.2 0.6 copy-done.5
  39.8 0.0 copy-done.6
  39.8 2.0 %shard_map.95 = (f32[64,8,128]{2,1,0:T(8,128)}, f32[16,3,128]{2,1,0:T(4,128)S(1)}) custom-call(s32[16]{0:T(128)S(1)} %bitcast.12, s32[16]{0:T(128)S(1)} %copy-done.6, f32[16,6,16,128]{3,2,1,0:T(8,128)S(1)} %all-to-all-done.gathered, f32[7,16,128]{2,1,0:T(8,128)S(1)} %bitcast.11, bf16[16,128,128]{2,1,0:T(8,128)(2,1)S(1)} %copy-done, ...), custom_call_target="tpu_custom_call" | custom-call | tf_op jit(solution)/shard_map/pallas_call | solution.py:325
  41.9 12.9 %all-to-all-start.1 = ((f32[64,8,128]{2,1,0:T(8,128)}), f32[64,8,128]{2,1,0:T(8,128)S(1)}, u32[]{:S(2)}, u32[]{:S(2)}) async-start(f32[64,8,128]{2,1,0:T(8,128)} %get-tuple-element.6), calls=%async_computation.1 | async-start | bytes 524288 | tf_op jit(solution)/shard_map/all_to_all | solution.py:356
  54.8 0.1 pad_add_fusion.where
  54.9 12.6 %all-to-all-done.1 = f32[64,8,128]{2,1,0:T(8,128)S(1)} async-done(((f32[64,8,128]{2,1,0:T(8,128)}), f32[64,8,128]{2,1,0:T(8,128)S(1)}, u32[]{:S(2)}, u32[]{:S(2)}) %all-to-all-start.1) | async-done | bytes 262176 | tf_op jit(solution)/shard_map/all_to_all | solution.py:356
  67.5 1.0 shard_map.96.base
  68.5 0.0 copy-start.2
  68.5 0.0 copy-start.3
  68.5 2.4 %collective-permute-start = (f32[3,8,1024]{2,1,0:T(8,128)S(1)}, f32[3,8,1024]{2,1,0:T(8,128)S(1)}, u32[]{:S(2)}, u32[]{:S(2)}) collective-permute-start(f32[3,8,1024]{2,1,0:T(8,128)S(1)} %get-tuple-element.13), channel_id=1, source_target_pairs={{0,8},{8,16},{16,24},{24,256},{256,264},{264,272},{272,280},{280,1... | collective-permute-start | bytes 294920 | tf_op jit(solution)/shard_map/ppermute | solution.py:376
  70.9 4.4 %collective-permute-start.1 = (f32[3,8,1024]{2,1,0:T(8,128)S(1)}, f32[3,8,1024]{2,1,0:T(8,128)S(1)}, u32[]{:S(2)}, u32[]{:S(2)}) collective-permute-start(f32[3,8,1024]{2,1,0:T(8,128)S(1)} %get-tuple-element.12), channel_id=1, source_target_pairs={{8,0},{16,8},{24,16},{256,24},{264,256},{272,264},{280,272},{1,280... | collective-permute-start | bytes 294920 | tf_op jit(solution)/shard_map/ppermute | solution.py:377
  75.3 0.4 collective-permute-done.lower
  75.7 1.3 collective-permute-done.1.upper
  77.0 0.0 copy-done.2
  77.0 0.0 copy-done.3
  77.0 1.3 shard_map.97
  78.3 22.1 %all_to_all.25.got = f32[64,1,128]{2,1,0:T(1,128)S(1)} all-to-all(f32[64,1,128]{2,1,0:T(1,128)S(1)} %get-tuple-element.8), channel_id=1, replica_groups=mesh['l'=2,'f'=8,'gy'=4,'gz'=8] {'l','gy','gz'}, dimensions={0} | all-to-all | bytes 65536 | tf_op jit(solution)/shard_map/all_to_all | solution.py:356
  100.3 1.8 %shard_map.98 = f32[16,4,16,128]{3,2,1,0:T(8,128)S(1)} custom-call(s32[2]{0:T(128)S(1)} %pad_add_fusion.where, f32[7]{0:T(128)S(1)} %copy-done.2, f32[7]{0:T(128)S(1)} %copy-done.3, f32[3,8,1024]{2,1,0:T(8,128)S(1)} %collective-permute-done.lower, f32[3,16,1024]{2,1,0:T(8,128)S(1)} %shard_map.96.base, f32[3,8,1024]{2,1,0:T(8,128)S(1)} %collective-permute-done.1.upper, ...), custom_call_target="tpu_custom_call" | custom-call | tf_op jit(solution)/shard_map/pallas_call | solution.py:325
  102.1 21.7 %all_to_all.26.got = f32[64,16,128]{2,1,0:T(8,128)S(1)} all-to-all(f32[64,16,128]{2,1,0:T(8,128)S(1)} %bitcast.9), channel_id=1, replica_groups=mesh['l'=2,'f'=8,'gy'=4,'gz'=8] {'l','f','gy'}, dimensions={0} | all-to-all | bytes 1048576 | tf_op jit(solution)/shard_map/all_to_all | solution.py:356
  123.8 0.6 shard_map.99
  124.5 6.4 %all-to-all-start.4 = ((f32[8,8,128]{2,1,0:T(8,128)}), f32[8,8,128]{2,1,0:T(8,128)S(1)}, u32[]{:S(2)}, u32[]{:S(2)}) async-start(f32[8,8,128]{2,1,0:T(8,128)} %shard_map.99), calls=%async_computation.4 | async-start | bytes 65536 | tf_op jit(solution)/shard_map/all_to_all | solution.py:356
  130.8 0.6 copy.11
  131.5 4.1 %all-to-all-done.4.sums = f32[8,8,128]{2,1,0:T(8,128)S(1)} async-done(((f32[8,8,128]{2,1,0:T(8,128)}), f32[8,8,128]{2,1,0:T(8,128)S(1)}, u32[]{:S(2)}, u32[]{:S(2)}) %all-to-all-start.4) | async-done | bytes 32800 | tf_op jit(solution)/shard_map/all_to_all | solution.py:356
  135.6 1.6 %shard_map.100 = f32[7,16,128]{2,1,0:T(8,128)} custom-call(f32[7]{0:T(128)S(1)} %copy-done.2, f32[7]{0:T(128)S(1)} %copy-done.3, f32[64,16,128]{2,1,0:T(8,128)S(1)} %all_to_all.26.got, f32[8,8,128]{2,1,0:T(8,128)S(1)} %all-to-all-done.4.sums), custom_call_target="tpu_custom_call" | custom-call | tf_op jit(solution)/shard_map/pallas_call | solution.py:325
  (2 shorter events, 0.0 us)
Async XLA Ops:
  2.4 16.4 %copy-start.7 = (bf16[16,3,128]{2,0,1:T(8,128)(2,1)S(1)}, bf16[16,3,128]{2,0,1:T(8,128)(2,1)}, u32[]{:S(2)}) copy-start(bf16[16,3,128]{2,0,1:T(8,128)(2,1)} %param.12) | copy-start | bytes 36868
  2.4 36.8 %copy-start = (bf16[16,128,128]{2,1,0:T(8,128)(2,1)S(1)}, bf16[16,128,128]{2,1,0:T(8,128)(2,1)}, u32[]{:S(2)}) copy-start(bf16[16,128,128]{2,1,0:T(8,128)(2,1)} %weights.1) | copy-start | bytes 1572868
  2.4 36.8 %copy-start.1 = (f32[7,2,8,128]{3,2,1,0:T(8,128)S(1)}, f32[7,2,8,128]{3,2,1,0:T(8,128)}, u32[]{:S(2)}) copy-start(f32[7,2,8,128]{3,2,1,0:T(8,128)} %param.8) | copy-start | bytes 172036
  2.4 36.8 %all-to-all-start = ((f32[16,6,16,128]{3,2,1,0:T(8,128)}), f32[16,6,16,128]{3,2,1,0:T(8,128)S(1)}, u32[]{:S(2)}, u32[]{:S(2)}) async-start(f32[16,6,16,128]{3,2,1,0:T(8,128)} %broadcast_in_dim.9), calls=%async_computation | async-start | bytes 1572864 | tf_op jit(solution)/shard_map/all_to_all | solution.py:356
  18.8 20.4 %copy-start.4 = (bf16[16,128]{1,0:T(8,128)(2,1)S(1)}, bf16[16,128]{1,0:T(8,128)(2,1)}, u32[]{:S(2)}) copy-start(bf16[16,128]{1,0:T(8,128)(2,1)} %rates.1) | copy-start | bytes 12292
  39.2 0.7 copy-start.5
  39.2 0.7 copy-start.6
  41.9 25.6 %all-to-all-start.1 = ((f32[64,8,128]{2,1,0:T(8,128)}), f32[64,8,128]{2,1,0:T(8,128)S(1)}, u32[]{:S(2)}, u32[]{:S(2)}) async-start(f32[64,8,128]{2,1,0:T(8,128)} %get-tuple-element.6), calls=%async_computation.1 | async-start | bytes 524288 | tf_op jit(solution)/shard_map/all_to_all | solution.py:356
  68.5 8.4 %copy-start.2 = (f32[7]{0:T(128)S(1)}, f32[7]{0:T(128)}, u32[]{:S(2)}) copy-start(f32[7]{0:T(128)} %diffusion.5) | copy-start | bytes 88
  68.5 8.4 %copy-start.3 = (f32[7]{0:T(128)S(1)}, f32[7]{0:T(128)}, u32[]{:S(2)}) copy-start(f32[7]{0:T(128)} %stiffness.5) | copy-start | bytes 88
  68.5 7.1 %collective-permute-start = (f32[3,8,1024]{2,1,0:T(8,128)S(1)}, f32[3,8,1024]{2,1,0:T(8,128)S(1)}, u32[]{:S(2)}, u32[]{:S(2)}) collective-permute-start(f32[3,8,1024]{2,1,0:T(8,128)S(1)} %get-tuple-element.13), channel_id=1, source_target_pairs={{0,8},{8,16},{16,24},{24,256},{256,264},{264,272},{272,280},{280,1... | collective-permute-start | bytes 294920 | tf_op jit(solution)/shard_map/ppermute | solution.py:376
  70.9 6.0 %collective-permute-start.1 = (f32[3,8,1024]{2,1,0:T(8,128)S(1)}, f32[3,8,1024]{2,1,0:T(8,128)S(1)}, u32[]{:S(2)}, u32[]{:S(2)}) collective-permute-start(f32[3,8,1024]{2,1,0:T(8,128)S(1)} %get-tuple-element.12), channel_id=1, source_target_pairs={{8,0},{16,8},{24,16},{256,24},{264,256},{272,264},{280,272},{1,280... | collective-permute-start | bytes 294920 | tf_op jit(solution)/shard_map/ppermute | solution.py:377
  124.5 11.1 %all-to-all-start.4 = ((f32[8,8,128]{2,1,0:T(8,128)}), f32[8,8,128]{2,1,0:T(8,128)S(1)}, u32[]{:S(2)}, u32[]{:S(2)}) async-start(f32[8,8,128]{2,1,0:T(8,128)} %shard_map.99), calls=%async_computation.4 | async-start | bytes 65536 | tf_op jit(solution)/shard_map/all_to_all | solution.py:356

commit v2 on v1

--- a/solution.py
+++ b/solution.py
@@ -54,9 +54,9 @@
     work = jnp.zeros_like(rate)
     source_buf[:, 0, :] = evapor
     for k in range(3):
-        vel = speed[:, k, :]
+        vel = speed[k]
         force = rate * (at_buf[k] - vel)
-        moved[:, k, :] = vel + 0.2 * force
+        moved[k] = vel + 0.2 * force
         work = work + force * vel
         source_buf[:, 1 + k, :] = evapor * vel - force
     source_buf[:, 4, :] = evapor * at_buf[3] - work
@@ -359,13 +359,14 @@
 def body(gas_old, diffusion, stiffness, weights, velocity, rates, destination, tile_ids):
     place = lax.axis_index("gz") * 8 + lax.axis_index("l") * 4 + lax.axis_index("gy")
     where = jnp.stack([lax.axis_index("f"), place]).astype(jnp.int32)
+    gas_old, where = lax.optimization_barrier((gas_old, where))
     gas = gas_old.reshape(FIELDS, BLOCKS, LANES)
     gathered = exchange(jnp.broadcast_to(gas[None, 1:], (16, 6, BLOCKS, LANES)), GX)
     send, moved = call(
         parcel_kernel,
-        [shaped(64, 8, LANES), shaped(BLOCKS, 3, LANES)],
+        [shaped(64, 8, LANES), shaped(3, BLOCKS, LANES)],
         "ssvvvvv",
-        (destination[:, 0], tile_ids, gathered, gas, weights, velocity, rates),
+        (destination[:, 0], tile_ids, gathered, gas, weights, velocity.transpose(1, 0, 2), rates),
         [pltpu.VMEM((BLOCKS, 8, LANES), F32), pltpu.VMEM((8, BLOCKS, LANES), F32),
          pltpu.VMEM((BLOCKS, 8, LANES), F32), pltpu.VMEM((8, BLOCKS, LANES), F32)],
     )
@@ -393,7 +394,7 @@
     sums = call(collect_kernel, shaped(8, 8, LANES), "v", (got,))
     sums = exchange(sums, "gz")
     out = call(final_kernel, shaped(FIELDS, BLOCKS, LANES), "ssvv", (diffusion, stiffness, got, sums))
-    return out.reshape(gas_old.shape), moved
+    return out.reshape(gas_old.shape), moved.transpose(1, 0, 2)
 
 
 def solution(mesh):

time: 138 us -> 133 us (0.964)
  blocking collectives: 43.7 us -> 111 us
  starting transfers between devices: 42.4 us -> 6.75 us
  waiting for transfers between devices: 38.6 us -> 5.57 us
  local copies, waits for them, and re-layouts: 3.09 us -> 1.58 us
    all_to_all x2 -> x5, blocking collectives: 43.7 us -> 111 us  [exchange(): return lax.all_to_all(value, axes, 0, 0, tiled=True)]
    all_to_all x3 -> x0, waiting for transfers between devices: 37 us -> none  [exchange(): return lax.all_to_all(value, axes, 0, 0, tiled=True)]
    all_to_all x3 -> x0, starting transfers between devices: 35.7 us -> none  [exchange(): return lax.all_to_all(value, axes, 0, 0, tiled=True)]
    ppermute x1, waiting for transfers between devices: 0.36 us -> 5.57 us  [body(): lower = lax.ppermute(base[:, HALO:], ALL, forward)]
  transfers between devices with their start and end apart: 5 -> 2, of which waited for: 5 -> 1; matrix products, arithmetic and copies ran while one was open for 1% -> 0% of each run, Pallas kernels for 0% -> 0%
where the time goes in v2:
time: 133 us
  blocking collectives  111 us (83%)
  Pallas kernels  7.63 us (6%)
  starting transfers between devices  6.75 us (5%)
  waiting for transfers between devices  5.57 us (4%)
  local copies, waits for them, and re-layouts  1.58 us (1%)
    all_to_all x5, blocking collectives, exchange(): return lax.all_to_all(value, axes, 0, 0, tiled=True)  111 us
    pallas_call x6, Pallas kernels, call(): pl.pallas_call(kernel, out_shape=listed, in_specs=[pl.BlockSpec(memory_sp...  7.63 us
    ppermute x1, waiting for transfers between devices, body(): lower = lax.ppermute(base[:, HALO:], ALL, forward)  5.57 us
    ppermute x1, starting transfers between devices, body(): upper = lax.ppermute(base[:, :HALO], ALL, backward)  4.83 us
  transfers between devices with their start and end apart: 2, of which 1 were waited for; matrix products, arithmetic and copies ran while one was open for 0% of the time, Pallas kernels for 0%

profile of v2, /device:TPU:1, one launch (start us, length us, event | category | flops | bytes accessed | tf_op | source)
XLA Modules:
  0.0 132.9 jit_solution(3786296908169090062)
XLA Ops:
  0.6 0.1 pad_add_fusion.where
  0.7 0.8 slice_bitcast_fusion
  1.5 0.1 broadcast_in_dim.9
  1.6 0.0 copy-start
  1.6 0.0 copy-start.1
  1.6 0.0 copy-start.2
  1.6 36.6 %all_to_all.25.gathered = f32[16,6,16,128]{3,2,1,0:T(8,128)S(1)} all-to-all(f32[16,6,16,128]{3,2,1,0:T(8,128)S(1)} %broadcast_in_dim.9), channel_id=1, replica_groups=mesh['l'=2,'f'=8,'gy'=4,'gz'=8] {'l','f'}, dimensions={0} | all-to-all | bytes 1572864 | tf_op jit(solution)/shard_map/all_to_all | solution.py:356
  38.3 0.0 copy-start.5
  38.3 0.0 copy-start.6
  38.3 0.0 copy-start.7
  38.3 0.0 copy-done
  38.3 0.0 copy-done.1
  38.3 0.0 copy-done.2
  38.3 0.7 copy-done.5
  39.0 0.0 copy-done.6
  39.0 0.0 copy-done.7
  39.0 1.8 %shard_map.95 = (f32[64,8,128]{2,1,0:T(8,128)S(1)}, f32[3,16,128]{2,1,0:T(8,128)}) custom-call(s32[16]{0:T(128)S(1)} %bitcast.15, s32[16]{0:T(128)S(1)} %copy-done.7, f32[16,6,16,128]{3,2,1,0:T(8,128)S(1)} %all_to_all.25.gathered, f32[7,16,128]{2,1,0:T(8,128)S(1)} %bitcast.13, bf16[16,128,128]{2,1,0:T(8,128)(2,1)S(1)} %copy-done, ...), custom_call_target="tpu_custom_call" | custom-call | tf_op jit(solution)/shard_map/pallas_call | solution.py:325
  40.8 23.7 %all_to_all.26 = f32[64,8,128]{2,1,0:T(8,128)S(1)} all-to-all(f32[64,8,128]{2,1,0:T(8,128)S(1)} %get-tuple-element.10), channel_id=1, replica_groups=mesh['l'=2,'f'=8,'gy'=4,'gz'=8] {'l','f','gy'}, dimensions={0} | all-to-all | bytes 524288 | tf_op jit(solution)/shard_map/all_to_all | solution.py:356
  64.5 1.0 shard_map.96.base
  65.6 0.0 copy-start.3
  65.6 0.0 copy-start.4
  65.6 4.8 %collective-permute-start.1 = (f32[3,8,1024]{2,1,0:T(8,128)S(1)}, f32[3,8,1024]{2,1,0:T(8,128)S(1)}, u32[]{:S(2)}, u32[]{:S(2)}) collective-permute-start(f32[3,8,1024]{2,1,0:T(8,128)S(1)} %get-tuple-element.14), channel_id=1, source_target_pairs={{8,0},{16,8},{24,16},{256,24},{264,256},{272,264},{280,272},{1,280... | collective-permute-start | bytes 294920 | tf_op jit(solution)/shard_map/ppermute | solution.py:378
  70.4 1.9 %collective-permute-start = (f32[3,8,1024]{2,1,0:T(8,128)S(1)}, f32[3,8,1024]{2,1,0:T(8,128)S(1)}, u32[]{:S(2)}, u32[]{:S(2)}) collective-permute-start(f32[3,8,1024]{2,1,0:T(8,128)S(1)} %get-tuple-element.15), channel_id=1, source_target_pairs={{0,8},{8,16},{16,24},{24,256},{256,264},{264,272},{272,280},{280,1... | collective-permute-start | bytes 294920 | tf_op jit(solution)/shard_map/ppermute | solution.py:377
  72.4 0.0 collective-permute-done.1.upper
  72.4 5.6 %collective-permute-done.lower = f32[3,8,1024]{2,1,0:T(8,128)S(1)} collective-permute-done((f32[3,8,1024]{2,1,0:T(8,128)S(1)}, f32[3,8,1024]{2,1,0:T(8,128)S(1)}, u32[]{:S(2)}, u32[]{:S(2)}) %collective-permute-start) | collective-permute-done | bytes 98336 | tf_op jit(solution)/shard_map/ppermute | solution.py:377
  77.9 0.0 copy-done.3
  77.9 0.0 copy-done.4
  78.0 1.3 shard_map.97
  79.3 18.3 %all_to_all.27.got = f32[64,1,128]{2,1,0:T(1,128)S(1)} all-to-all(f32[64,1,128]{2,1,0:T(1,128)S(1)} %get-tuple-element.12), channel_id=1, replica_groups=mesh['l'=2,'f'=8,'gy'=4,'gz'=8] {'l','gy','gz'}, dimensions={0} | all-to-all | bytes 65536 | tf_op jit(solution)/shard_map/all_to_all | solution.py:356
  97.6 1.8 %shard_map.98 = f32[16,4,16,128]{3,2,1,0:T(8,128)S(1)} custom-call(s32[2]{0:T(128)S(1)} %pad_add_fusion.where, f32[7]{0:T(128)S(1)} %copy-done.3, f32[7]{0:T(128)S(1)} %copy-done.4, f32[3,8,1024]{2,1,0:T(8,128)S(1)} %collective-permute-done.lower, f32[3,16,1024]{2,1,0:T(8,128)S(1)} %shard_map.96.base, f32[3,8,1024]{2,1,0:T(8,128)S(1)} %collective-permute-done.1.upper, ...), custom_call_target="tpu_custom_call" | custom-call | tf_op jit(solution)/shard_map/pallas_call | solution.py:325
  99.4 21.7 %all_to_all.28.got = f32[64,16,128]{2,1,0:T(8,128)S(1)} all-to-all(f32[64,16,128]{2,1,0:T(8,128)S(1)} %bitcast.11), channel_id=1, replica_groups=mesh['l'=2,'f'=8,'gy'=4,'gz'=8] {'l','f','gy'}, dimensions={0} | all-to-all | bytes 1048576 | tf_op jit(solution)/shard_map/all_to_all | solution.py:356
  121.1 10.2 %all_to_all.29.sums = f32[8,8,128]{2,1,0:T(8,128)S(1)} all-to-all(f32[8,8,128]{2,1,0:T(8,128)S(1)} %shard_map.99), channel_id=1, replica_groups=mesh['l'=2,'f'=8,'gy'=4,'gz'=8] {'gz'}, dimensions={0} | all-to-all | bytes 65536 | tf_op jit(solution)/shard_map/all_to_all | solution.py:356
  131.3 1.6 %shard_map.100 = f32[7,16,128]{2,1,0:T(8,128)} custom-call(f32[7]{0:T(128)S(1)} %copy-done.3, f32[7]{0:T(128)S(1)} %copy-done.4, f32[64,16,128]{2,1,0:T(8,128)S(1)} %all_to_all.28.got, f32[8,8,128]{2,1,0:T(8,128)S(1)} %all_to_all.29.sums), custom_call_target="tpu_custom_call" | custom-call | tf_op jit(solution)/shard_map/pallas_call | solution.py:325
  (2 shorter events, 0.0 us)
Async XLA Ops:
  1.6 36.7 %copy-start = (bf16[16,128,128]{2,1,0:T(8,128)(2,1)S(1)}, bf16[16,128,128]{2,1,0:T(8,128)(2,1)}, u32[]{:S(2)}) copy-start(bf16[16,128,128]{2,1,0:T(8,128)(2,1)} %weights.1) | copy-start | bytes 1572868
  1.6 36.7 %copy-start.1 = (f32[7,2,8,128]{3,2,1,0:T(8,128)S(1)}, f32[7,2,8,128]{3,2,1,0:T(8,128)}, u32[]{:S(2)}) copy-start(f32[7,2,8,128]{3,2,1,0:T(8,128)} %param.8) | copy-start | bytes 172036
  1.6 36.7 %copy-start.2 = (bf16[16,3,128]{2,0,1:T(8,128)(2,1)S(1)}, bf16[16,3,128]{2,0,1:T(8,128)(2,1)}, u32[]{:S(2)}) copy-start(bf16[16,3,128]{2,0,1:T(8,128)(2,1)} %param.12) | copy-start | bytes 36868
  38.3 0.7 copy-start.5
  38.3 0.7 copy-start.6
  38.3 0.7 copy-start.7
  65.6 12.4 %copy-start.3 = (f32[7]{0:T(128)S(1)}, f32[7]{0:T(128)}, u32[]{:S(2)}) copy-start(f32[7]{0:T(128)} %diffusion.5) | copy-start | bytes 88
  65.6 12.4 %copy-start.4 = (f32[7]{0:T(128)S(1)}, f32[7]{0:T(128)}, u32[]{:S(2)}) copy-start(f32[7]{0:T(128)} %stiffness.5) | copy-start | bytes 88
  65.6 6.8 %collective-permute-start.1 = (f32[3,8,1024]{2,1,0:T(8,128)S(1)}, f32[3,8,1024]{2,1,0:T(8,128)S(1)}, u32[]{:S(2)}, u32[]{:S(2)}) collective-permute-start(f32[3,8,1024]{2,1,0:T(8,128)S(1)} %get-tuple-element.14), channel_id=1, source_target_pairs={{8,0},{16,8},{24,16},{256,24},{264,256},{272,264},{280,272},{1,280... | collective-permute-start | bytes 294920 | tf_op jit(solution)/shard_map/ppermute | solution.py:378
  70.4 7.5 %collective-permute-start = (f32[3,8,1024]{2,1,0:T(8,128)S(1)}, f32[3,8,1024]{2,1,0:T(8,128)S(1)}, u32[]{:S(2)}, u32[]{:S(2)}) collective-permute-start(f32[3,8,1024]{2,1,0:T(8,128)S(1)} %get-tuple-element.15), channel_id=1, source_target_pairs={{0,8},{8,16},{16,24},{24,256},{256,264},{264,272},{272,280},{280,1... | collective-permute-start | bytes 294920 | tf_op jit(solution)/shard_map/ppermute | solution.py:377

commit v3 on v2

--- a/solution.py
+++ b/solution.py
@@ -7,6 +7,7 @@
 
 F32 = jnp.float32
 BF16 = jnp.bfloat16
+F16 = jnp.float16
 FIELDS = 7
 BLOCKS = 16
 LANES = 128
@@ -35,14 +36,15 @@
 
 
 def parcel_kernel(
-    dest, tile, gathered, gas, weights, velocity, rates, send, moved, tiles_buf, at_buf, source_buf, dep_buf
+    dest, tile, gathered, gas, weights, velocity, rates, send, moved,
+    tiles_buf, at_buf, source_buf, dep_buf
 ):
     tiles_buf[...] = jnp.zeros_like(tiles_buf)
     for b in range(BLOCKS):
         owner = dest[b]
         line = tile[b]
         for f in range(6):
-            tiles_buf[b, pl.ds(f, 1), :] = gathered[owner, f, pl.ds(line, 1), :].astype(F32)
+            tiles_buf[b, pl.ds(f, 1), :] = gathered[owner, f, pl.ds(line, 1), :]
     for b in range(BLOCKS):
         high, low = split(tiles_buf[b])
         both = jnp.concatenate([high, low], axis=0)
@@ -68,62 +70,45 @@
         both = jnp.concatenate([high, low], axis=0)
         value = dot_nn(both, weights[b])
         dep_buf[:, b, :] = value[:8] + value[8:]
-    lane = iota((8, LANES), 1)
-    row = iota((8, LANES), 0)
-    spot = jnp.zeros((8, LANES), F32)
+    lane = iota((BLOCKS, LANES), 1)
+    row = iota((BLOCKS, LANES), 0)
+    spot = jnp.zeros((BLOCKS, LANES), F32)
     for b in range(BLOCKS):
         code = (tile[b] % 8) * 32 + dest[b] * 2 + tile[b] // 8
-        mark = (row == b % 8) & ((lane // 64) == b // 8)
-        spot = jnp.where(mark, code.astype(F32), spot)
-    part = (lane % 64) // 16
-    upper = lane >= 64
+        spot = jnp.where(row == b, code.astype(F32), spot)
+    part = lane // 32
     for c in range(8):
-        third = jnp.where(
-            upper,
-            pltpu.roll(dep_buf[7, 8:16], (96 - 16 * c) % LANES, 1),
-            pltpu.roll(dep_buf[7, 0:8], (32 - 16 * c) % LANES, 1),
-        )
-        tail = jnp.where(part == 2, third, spot)
+        start = 16 * c - HALO
+        tail = jnp.where(part == 2, pltpu.roll(dep_buf[7], (64 - start) % LANES, 1), spot)
         for f in range(8):
             src = min(f, FIELDS - 1)
-            first = jnp.where(
-                upper,
-                pltpu.roll(gas[src, 8:16], (64 - 16 * c) % LANES, 1),
-                pltpu.roll(gas[src, 0:8], (-16 * c) % LANES, 1),
-            )
-            second = jnp.where(
-                upper,
-                pltpu.roll(dep_buf[src, 8:16], (80 - 16 * c) % LANES, 1),
-                pltpu.roll(dep_buf[src, 0:8], (16 - 16 * c) % LANES, 1),
-            )
+            first = pltpu.roll(gas[src], (-start) % LANES, 1)
+            second = pltpu.roll(dep_buf[src], (32 - start) % LANES, 1)
             index = ((c // 4) * 8 + f) * 4 + c % 4
             send[index] = jnp.where(part == 0, first, jnp.where(part == 1, second, tail))
 
 
-def expand_kernel(where, got, base):
+def expand_kernel(where, got, base, edge):
     moment = ((where[0] >= 1) & (where[0] <= 3)).astype(F32)
     target = iota((256, 256), 0)
     k = iota((256, 256), 1)
-    inner = k % 128
-    perm = (target == (inner % 8) * 32 + (inner // 8) * 2 + k // 128).astype(F32).astype(BF16)
-    gases = []
+    perm = (target == (k % 8) * 32 + (k // 16) * 2 + (k % 16) // 8).astype(F32).astype(BF16)
     for j in range(4):
-        rows = got[:, j].reshape(LANES, LANES)
-        flip = rows.T
-        spot = jnp.concatenate([flip[48:49], flip[112:113]], axis=1).astype(jnp.int32)
+        flip = got[:, j].reshape(256, LANES).T
+        spot = flip[96:97].astype(jnp.int32)
         onehot = (target == spot).astype(F32).astype(BF16)
-        dep = jnp.concatenate([flip[16:48], flip[80:112]], axis=1)
-        high, low = split(dep)
+        high, low = split(flip[32:96])
         value = dot_nt(jnp.concatenate([high, low], axis=0), onehot)
-        value = value[:32] + value[32:]
-        gas = jnp.concatenate([flip[0:16], flip[64:80]], axis=1)
-        high, low = split(gas)
+        value = value[:64] + value[64:]
+        high, low = split(flip[0:32])
         held = dot_nt(jnp.concatenate([high, low], axis=0), perm)
-        held = held[:16] + held[16:]
+        held = held[:32] + held[32:]
         area = slice(j * 256, (j + 1) * 256)
         base[0, :, area] = held
-        base[1, :, area] = held + 0.5 * value[:16]
-        base[2, :, area] = 1.0 + 0.5 * moment * value[16:]
+        base[1, :, area] = held + 0.5 * value[:32]
+        base[2, :, area] = 1.0 + 0.5 * moment * value[32:]
+    last = jnp.full((1, 1, 1), where[1] % 8) == 7
+    edge[...] = jnp.where(last, base[:, HALO + CHUNK - HALO:HALO + CHUNK], base[:, HALO:2 * HALO])
 
 
 def gather_neighbours(blocks):
@@ -220,9 +205,17 @@
     return step0 + alpha * e0, step1 + alpha * e1, alpha * e2
 
 
-def load(lower, base, upper, index):
-    whole = jnp.concatenate([lower[index], base[index], upper[index]], axis=0)
-    return [whole[:, n * LANES:(n + 1) * LANES] for n in range(NQ)]
+def load(where, base, border, index):
+    c = where[1] % 8
+    plane = iota((CHUNK + 2 * HALO, LANES), 0)
+    swap = ((plane < HALO) & (c == 0)) | ((plane >= HALO + CHUNK) & (c == 7))
+    out = []
+    for n in range(NQ):
+        area = slice(n * LANES, (n + 1) * LANES)
+        given = border[index, :, area]
+        given = jnp.concatenate([given, given, given, given], axis=0)
+        out.append(jnp.where(swap, given, base[index, :, area]))
+    return out
 
 
 def plane_mask(where):
@@ -231,13 +224,13 @@
     return jnp.where(outside, 0.0, 1.0).astype(F32)
 
 
-def first_kernel(where, diffusion, stiffness, lower, base, upper, basis, sums):
+def first_kernel(where, diffusion, stiffness, base, border, basis, sums):
     field = jnp.minimum(where[0], FIELDS - 1)
     d = diffusion[field]
     beta = stiffness[field]
-    q = load(lower, base, upper, 0)
-    rhs = load(lower, base, upper, 1)
-    damp = load(lower, base, upper, 2)
+    q = load(where, base, border, 0)
+    rhs = load(where, base, border, 1)
+    damp = load(where, base, border, 2)
     zero, one, two, line = newton_terms(q, rhs, damp, jnp.full((1, 1), d), beta, plane_mask(where))
     for n in range(NQ):
         area = slice(n * LANES, (n + 1) * LANES)
@@ -247,7 +240,7 @@
     sums[...] = jnp.broadcast_to(line[None], sums.shape)
 
 
-def second_kernel(where, diffusion, stiffness, lower, base, upper, basis, got, send, state_buf):
+def second_kernel(where, diffusion, stiffness, base, border, basis, got, send, state_buf):
     field = jnp.minimum(where[0], FIELDS - 1)
     d = jnp.full((1, 1), diffusion[field])
     beta = jnp.full((1, 1), stiffness[field])
@@ -255,39 +248,72 @@
     lane = iota((1, LANES), 1)
     m = [jnp.sum(jnp.where(lane == k, row, 0.0), axis=1, keepdims=True) for k in range(6)]
     k0, k1, k2 = coefficients(m, d, beta)
-    q = load(lower, base, upper, 0)
-    rhs = load(lower, base, upper, 1)
-    damp = load(lower, base, upper, 2)
+    q = load(where, base, border, 0)
+    rhs = load(where, base, border, 1)
+    damp = load(where, base, border, 2)
     state = []
     for n in range(NQ):
         area = slice(n * LANES, (n + 1) * LANES)
         state.append(q[n] + k0 * basis[0, :, area] + k1 * basis[1, :, area] + k2 * basis[2, :, area])
     zero, one, two, line = newton_terms(state, rhs, damp, d, beta, plane_mask(where))
+    inner = slice(HALO, HALO + CHUNK)
+    powers = []
+    for group in ((state,), (zero, one, two)):
+        top = jnp.zeros((CHUNK, LANES), F32)
+        for held in group:
+            for n in range(NQ):
+                top = jnp.maximum(top, jnp.abs(held[n][inner]))
+        powers.append(power_of(jnp.max(jnp.max(top, axis=0, keepdims=True), axis=1, keepdims=True)))
+    scales = [jnp.exp2(-power) for power in powers]
     for n in range(NQ):
         area = slice(n * LANES, (n + 1) * LANES)
         for a, held in enumerate((state, zero, one, two)):
-            state_buf[a * CHUNK:(a + 1) * CHUNK, area] = held[n][HALO:HALO + CHUNK]
+            state_buf[a * CHUNK:(a + 1) * CHUNK, area] = held[n][inner] * scales[min(a, 1)]
+    power = power_of(jnp.max(jnp.abs(line), axis=1, keepdims=True))
+    scaled = line * jnp.exp2(-power) * 1024.0
+    first = shorten(scaled)
+    rest = scaled - first
+    lane = iota((8, LANES), 1)
+    extra = jnp.where(lane < 64, pltpu.roll(jnp.broadcast_to(first, (8, LANES)), 32, 1),
+                      pltpu.roll(jnp.broadcast_to(rest, (8, LANES)), 96, 1))
+    for spot, value in ((48, powers[0]), (49, powers[1]), (50, power)):
+        extra = jnp.where(lane == spot, value, extra)
     out = iota((LANES, 256), 0)
     k = iota((LANES, 256), 1)
     origin = (out % 8) * 32 + (out // 8) * 2
     perms = [(k == origin + x).astype(F32).astype(BF16) for x in range(2)]
+    wide = (lane % 64) < 32
     for j in range(4):
         high, low = split(state_buf[:, j * 256:(j + 1) * 256])
         sides = [dot_nt(perm, high) + dot_nt(perm, low) for perm in perms]
-        send[:, j, 0:8, :] = jnp.concatenate(sides, axis=1).reshape(16, 8, LANES)
-    send[:, :, 8:16, :] = jnp.broadcast_to(line[None, None], (16, 4, 8, LANES))
+        value = jnp.concatenate(sides, axis=1).reshape(16, 8, LANES)
+        upper = shorten(value)
+        send[:, j, 0:8, :] = upper
+        send[:, j, 8:16, :] = jnp.where(wide[None], value - upper, extra[None])
+
+
+def shorten(value):
+    spread = value * 8193.0
+    return spread - (spread - value)
+
+
+def power_of(top):
+    return jnp.clip(jnp.ceil(jnp.log2(top)), -60.0, 120.0)
 
 
 def collect_kernel(got, sums):
     first = iota((8, LANES), 0)
+    lane = iota((8, LANES), 1)
     table = jnp.zeros((8, LANES), F32)
     for f in range(8):
         total = jnp.zeros((8, LANES), F32)
         for l in range(2):
             for y in range(4):
-                total = total + got[(l * 8 + f) * 4 + y, 8:16, :]
+                part = got[(l * 8 + f) * 4 + y, 8:16, :]
+                power = jnp.sum(jnp.where(lane == 50, part, 0.0), axis=1, keepdims=True)
+                total = total + (part + pltpu.roll(part, 64, 1)) * (jnp.exp2(power) * (1.0 / 1024.0))
         table = jnp.where(first == f, total, table)
-    sums[...] = jnp.broadcast_to(table[None], sums.shape)
+    sums[...] = jnp.broadcast_to(pltpu.roll(table, 96, 1)[None], sums.shape)
 
 
 def final_kernel(diffusion, stiffness, got, sums, out):
@@ -303,13 +329,18 @@
     k0, k1, k2 = coefficients(m, d, beta)
     part = (lane % 64) // 16
     scale = jnp.where(part == 0, 1.0, jnp.where(part == 1, k0, jnp.where(part == 2, k1, k2)))
+    wide = part < 2
     for f in range(FIELDS):
         factor = scale[f:f + 1]
         low = jnp.zeros((8, LANES), F32)
         high = jnp.zeros((8, LANES), F32)
         for c in range(8):
             index = ((c // 4) * 8 + f) * 4 + c % 4
-            value = got[index, 0:8, :] * factor
+            under = got[index, 8:16, :]
+            power0 = jnp.sum(jnp.where(lane == 48, under, 0.0), axis=1, keepdims=True)
+            power1 = jnp.sum(jnp.where(lane == 49, under, 0.0), axis=1, keepdims=True)
+            value = got[index, 0:8, :] + jnp.where(wide, under, 0.0)
+            value = value * factor * jnp.exp2(jnp.where(part == 0, power0, power1))
             value = value + pltpu.roll(value, 16, 1)
             value = value + pltpu.roll(value, 32, 1)
             here = (lane // 16) == c
@@ -337,13 +368,12 @@
     return jax.ShapeDtypeStruct(dims, F32)
 
 
-def chain():
-    def device(f, place):
-        gz, c = divmod(place, 8)
-        l, gy = divmod(c, 4)
-        return ((l * 8 + f) * 4 + gy) * 8 + gz
-
-    return [(device(f, place), device(f, place + 1)) for f in range(8) for place in range(63)]
+def borders():
+    def device(f, c, gz):
+        return (((c // 4) * 8 + f) * 4 + c % 4) * 8 + gz
+
+    pairs = [(device(f, 7, gz), device(f, 0, gz + 1)) for f in range(8) for gz in range(7)]
+    return pairs + [(b, a) for a, b in pairs]
 
 
 ALL = ("l", "f", "gy", "gz")
@@ -354,6 +384,10 @@
 
 def exchange(value, axes):
     return lax.all_to_all(value, axes, 0, 0, tiled=True)
+
+
+def exchange_short(value, axes):
+    return exchange(value.astype(F16), axes).astype(F32)
 
 
 def body(gas_old, diffusion, stiffness, weights, velocity, rates, destination, tile_ids):
@@ -361,36 +395,35 @@
     where = jnp.stack([lax.axis_index("f"), place]).astype(jnp.int32)
     gas_old, where = lax.optimization_barrier((gas_old, where))
     gas = gas_old.reshape(FIELDS, BLOCKS, LANES)
-    gathered = exchange(jnp.broadcast_to(gas[None, 1:], (16, 6, BLOCKS, LANES)), GX)
+    gathered = exchange_short(jnp.broadcast_to(gas[None, 1:], (16, 6, BLOCKS, LANES)), GX)
     send, moved = call(
         parcel_kernel,
-        [shaped(64, 8, LANES), shaped(3, BLOCKS, LANES)],
+        [shaped(64, BLOCKS, LANES), shaped(3, BLOCKS, LANES)],
         "ssvvvvv",
         (destination[:, 0], tile_ids, gathered, gas, weights, velocity.transpose(1, 0, 2), rates),
         [pltpu.VMEM((BLOCKS, 8, LANES), F32), pltpu.VMEM((8, BLOCKS, LANES), F32),
          pltpu.VMEM((BLOCKS, 8, LANES), F32), pltpu.VMEM((8, BLOCKS, LANES), F32)],
     )
-    got = exchange(send, PLANE).reshape(16, 4, 8, LANES)
-    base = call(expand_kernel, shaped(3, CHUNK, 1024), "sv", (where, got))
-    forward = chain()
-    backward = [(b, a) for a, b in forward]
-    lower = lax.ppermute(base[:, HALO:], ALL, forward)
-    upper = lax.ppermute(base[:, :HALO], ALL, backward)
+    got = exchange_short(send, PLANE).reshape(16, 4, BLOCKS, LANES)
+    base, edge = call(
+        expand_kernel, [shaped(3, CHUNK + 2 * HALO, 1024), shaped(3, HALO, 1024)], "sv", (where, got)
+    )
+    border = lax.ppermute(edge, ALL, borders())
     basis, sums = call(
         first_kernel,
         [shaped(3, CHUNK + 2 * HALO, 1024), shaped(64, 1, LANES)],
-        "sssvvv",
-        (where, diffusion, stiffness, lower, base, upper),
+        "sssvv",
+        (where, diffusion, stiffness, base, border),
     )
     sums = exchange(sums, GROUP)
     send = call(
         second_kernel,
         shaped(16, 4, 16, LANES),
-        "sssvvvvv",
-        (where, diffusion, stiffness, lower, base, upper, basis, sums),
+        "sssvvvv",
+        (where, diffusion, stiffness, base, border, basis, sums),
         [pltpu.VMEM((4 * CHUNK, 1024), F32)],
     )
-    got = exchange(send.reshape(64, 16, LANES), PLANE)
+    got = exchange_short(send.reshape(64, 16, LANES), PLANE)
     sums = call(collect_kernel, shaped(8, 8, LANES), "v", (got,))
     sums = exchange(sums, "gz")
     out = call(final_kernel, shaped(FIELDS, BLOCKS, LANES), "ssvv", (diffusion, stiffness, got, sums))

time: 133 us -> 126 us (0.947)
  blocking collectives: 111 us -> 96.4 us
  Pallas kernels: 7.63 us -> 19.1 us
  waiting for transfers between devices: 5.57 us -> 2.29 us
  starting transfers between devices: 6.75 us -> 4.9 us
    all_to_all x5, blocking collectives: 111 us -> 96.4 us  [exchange(): return lax.all_to_all(value, axes, 0, 0, tiled=True)]
    pallas_call x6, Pallas kernels: 7.63 us -> 19.1 us  [call(): pl.pallas_call(kernel, out_shape=listed, in_specs=[pl.BlockSpec(memory_sp...]
    ppermute x2 -> x1, waiting for transfers between devices: 5.57 us -> 2.29 us  [body(): border = lax.ppermute(edge, ALL, borders())]
    ppermute x2 -> x1, starting transfers between devices: 6.75 us -> 4.9 us  [body(): border = lax.ppermute(edge, ALL, borders())]
  transfers between devices with their start and end apart: 2 -> 1, of which waited for: 1 -> 1; matrix products, arithmetic and copies ran while one was open for 0% -> 0% of each run, Pallas kernels for 0% -> 0%
where the time goes in v3:
time: 126 us
  blocking collectives  96.4 us (77%)
  Pallas kernels  19.1 us (15%)
  starting transfers between devices  4.9 us (4%)
  waiting for transfers between devices  2.29 us (2%)
    all_to_all x5, blocking collectives, exchange(): return lax.all_to_all(value, axes, 0, 0, tiled=True)  96.4 us
    pallas_call x6, Pallas kernels, call(): pl.pallas_call(kernel, out_shape=listed, in_specs=[pl.BlockSpec(memory_sp...  19.1 us
    ppermute x1, starting transfers between devices, body(): border = lax.ppermute(edge, ALL, borders())  4.9 us
  transfers between devices with their start and end apart: 1, of which 1 were waited for; matrix products, arithmetic and copies ran while one was open for 0% of the time, Pallas kernels for 0%

profile of v3, /device:TPU:1, one launch (start us, length us, event | category | flops | bytes accessed | tf_op | source)
XLA Modules:
  0.0 125.5 jit_solution(17791386140189917761)
XLA Ops:
  0.6 0.1 pad_add_fusion.where
  0.7 0.8 fusion
  1.5 0.1 broadcast_in_dim.2
  1.6 28.8 %all_to_all.25 = f16[16,6,16,128]{3,2,1,0:T(8,128)(2,1)S(1)} all-to-all(f16[16,6,16,128]{3,2,1,0:T(8,128)(2,1)S(1)} %broadcast_in_dim.2), channel_id=1, replica_groups=mesh['l'=2,'f'=8,'gy'=4,'gz'=8] {'l','f'}, dimensions={0} | all-to-all | bytes 786432 | tf_op jit(solution)/shard_map/all_to_all | solution.py:386
  30.4 0.0 copy-start
  30.4 0.0 copy-start.1
  30.4 0.0 copy-start.2
  30.4 0.1 convert_element_type.22.gathered
  30.5 0.0 copy-start.5
  30.5 0.0 copy-start.6
  30.5 0.0 copy-start.7
  30.5 0.9 copy-done
  31.5 0.0 copy-done.1
  31.5 0.0 copy-done.2
  31.5 0.0 copy-done.5
  31.5 0.0 copy-done.6
  31.5 0.0 copy-done.7
  31.5 1.9 %shard_map.95 = (f32[64,16,128]{2,1,0:T(8,128)S(1)}, f32[3,16,128]{2,1,0:T(8,128)}) custom-call(s32[16]{0:T(128)S(1)} %bitcast.14, s32[16]{0:T(128)S(1)} %copy-done.7, f32[16,6,16,128]{3,2,1,0:T(8,128)S(1)} %convert_element_type.22.gathered, f32[7,16,128]{2,1,0:T(8,128)S(1)} %bitcast.12, bf16[16,128,128]{2,1,0:T(8,128)(2,1)S(1)} %copy-done, ...), custom_call_target="tpu_custom_call" | custom-call | tf_op jit(solution)/shard_map/pallas_call | solution.py:356
  33.5 22.3 %all_to_all.26 = f16[64,16,128]{2,1,0:T(8,128)(2,1)S(1)} all-to-all(f16[64,16,128]{2,1,0:T(8,128)(2,1)S(1)} %convert_element_type.23), channel_id=1, replica_groups=mesh['l'=2,'f'=8,'gy'=4,'gz'=8] {'l','f','gy'}, dimensions={0} | all-to-all | bytes 524288 | tf_op jit(solution)/shard_map/all_to_all | solution.py:386
  55.8 1.1 shard_map.96
  56.9 0.0 copy-start.3
  56.9 0.0 copy-start.4
  56.9 4.9 %collective-permute-start = (f32[3,8,1024]{2,1,0:T(8,128)S(1)}, f32[3,8,1024]{2,1,0:T(8,128)S(1)}, u32[]{:S(2)}, u32[]{:S(2)}) collective-permute-start(f32[3,8,1024]{2,1,0:T(8,128)S(1)} %get-tuple-element.14), channel_id=1, source_target_pairs={{280,1},{281,2},{282,3},{283,4},{284,5},{285,6},{286,7},{312,33},{... | collective-permute-start | bytes 294920 | tf_op jit(solution)/shard_map/ppermute | solution.py:411
  61.8 2.3 %collective-permute-done.border = f32[3,8,1024]{2,1,0:T(8,128)S(1)} collective-permute-done((f32[3,8,1024]{2,1,0:T(8,128)S(1)}, f32[3,8,1024]{2,1,0:T(8,128)S(1)}, u32[]{:S(2)}, u32[]{:S(2)}) %collective-permute-start) | collective-permute-done | bytes 98336 | tf_op jit(solution)/shard_map/ppermute | solution.py:411
  64.1 0.0 copy-done.3
  64.1 0.0 copy-done.4
  64.1 1.3 %shard_map.97 = (f32[3,32,1024]{2,1,0:T(8,128)S(1)}, f32[64,1,128]{2,1,0:T(1,128)S(1)}) custom-call(s32[2]{0:T(128)S(1)} %pad_add_fusion.where, f32[7]{0:T(128)S(1)} %copy-done.3, f32[7]{0:T(128)S(1)} %copy-done.4, f32[3,32,1024]{2,1,0:T(8,128)S(1)} %get-tuple-element.13.base, f32[3,8,1024]{2,1,0:T(8,128)S(1)} %collective-permute-done.border), custom_call_target="tpu_custom_call" | custom-call | tf_op jit(solution)/shard_map/pallas_call | solution.py:356
  65.4 18.3 %all_to_all.27.got = f32[64,1,128]{2,1,0:T(1,128)S(1)} all-to-all(f32[64,1,128]{2,1,0:T(1,128)S(1)} %get-tuple-element.16), channel_id=1, replica_groups=mesh['l'=2,'f'=8,'gy'=4,'gz'=8] {'l','gy','gz'}, dimensions={0} | all-to-all | bytes 65536 | tf_op jit(solution)/shard_map/all_to_all | solution.py:386
  83.8 1.8 %shard_map.98 = f32[16,4,16,128]{3,2,1,0:T(8,128)S(1)} custom-call(s32[2]{0:T(128)S(1)} %pad_add_fusion.where, f32[7]{0:T(128)S(1)} %copy-done.3, f32[7]{0:T(128)S(1)} %copy-done.4, f32[3,32,1024]{2,1,0:T(8,128)S(1)} %get-tuple-element.13.base, f32[3,8,1024]{2,1,0:T(8,128)S(1)} %collective-permute-done.border, f32[3,32,1024]{2,1,0:T(8,128)S(1)} %get-tuple-element.15.basis, ...), custom_call_target="tpu_custom_call" | custom-call | tf_op jit(solution)/shard_map/pallas_call | solution.py:356
  85.6 17.1 %all_to_all.28 = f16[64,16,128]{2,1,0:T(8,128)(2,1)S(1)} all-to-all(f16[64,16,128]{2,1,0:T(8,128)(2,1)S(1)} %bitcast.16), channel_id=1, replica_groups=mesh['l'=2,'f'=8,'gy'=4,'gz'=8] {'l','f','gy'}, dimensions={0} | all-to-all | bytes 524288 | tf_op jit(solution)/shard_map/all_to_all | solution.py:386
  102.8 0.9 shard_map.99
  103.7 9.8 %all_to_all.29.sums = f32[8,8,128]{2,1,0:T(8,128)S(1)} all-to-all(f32[8,8,128]{2,1,0:T(8,128)S(1)} %shard_map.99), channel_id=1, replica_groups=mesh['l'=2,'f'=8,'gy'=4,'gz'=8] {'gz'}, dimensions={0} | all-to-all | bytes 65536 | tf_op jit(solution)/shard_map/all_to_all | solution.py:386
  113.5 12.0 %shard_map.100 = f32[7,16,128]{2,1,0:T(8,128)} custom-call(f32[7]{0:T(128)S(1)} %copy-done.3, f32[7]{0:T(128)S(1)} %copy-done.4, f32[64,16,128]{2,1,0:T(8,128)S(1)} %convert_element_type.26.got, f32[8,8,128]{2,1,0:T(8,128)S(1)} %all_to_all.29.sums), custom_call_target="tpu_custom_call" | custom-call | tf_op jit(solution)/shard_map/pallas_call | solution.py:356
  (4 shorter events, 0.2 us)
Async XLA Ops:
  30.4 1.0 copy-start
  30.4 1.0 copy-start.1
  30.4 1.0 copy-start.2
  30.5 1.0 copy-start.5
  30.5 1.0 copy-start.6
  30.5 0.9 copy-start.7
  56.9 7.2 %copy-start.3 = (f32[7]{0:T(128)S(1)}, f32[7]{0:T(128)}, u32[]{:S(2)}) copy-start(f32[7]{0:T(128)} %diffusion.5) | copy-start | bytes 88
  56.9 7.2 %copy-start.4 = (f32[7]{0:T(128)S(1)}, f32[7]{0:T(128)}, u32[]{:S(2)}) copy-start(f32[7]{0:T(128)} %stiffness.5) | copy-start | bytes 88
  56.9 7.2 %collective-permute-start = (f32[3,8,1024]{2,1,0:T(8,128)S(1)}, f32[3,8,1024]{2,1,0:T(8,128)S(1)}, u32[]{:S(2)}, u32[]{:S(2)}) collective-permute-start(f32[3,8,1024]{2,1,0:T(8,128)S(1)} %get-tuple-element.14), channel_id=1, source_target_pairs={{280,1},{281,2},{282,3},{283,4},{284,5},{285,6},{286,7},{312,33},{... | collective-permute-start | bytes 294920 | tf_op jit(solution)/shard_map/ppermute | solution.py:411

commit v4 on v3

--- a/solution.py
+++ b/solution.py
@@ -36,7 +36,7 @@
 
 
 def parcel_kernel(
-    dest, tile, gathered, gas, weights, velocity, rates, send, moved,
+    where, dest, tile, gathered, gas, weights, velocity, rates, send, moved,
     tiles_buf, at_buf, source_buf, dep_buf
 ):
     tiles_buf[...] = jnp.zeros_like(tiles_buf)
@@ -84,8 +84,7 @@
             src = min(f, FIELDS - 1)
             first = pltpu.roll(gas[src], (-start) % LANES, 1)
             second = pltpu.roll(dep_buf[src], (32 - start) % LANES, 1)
-            index = ((c // 4) * 8 + f) * 4 + c % 4
-            send[index] = jnp.where(part == 0, first, jnp.where(part == 1, second, tail))
+            send[f * 8 + jnp.where(where[2] == 1, 7 - c, c)] = jnp.where(part == 0, first, jnp.where(part == 1, second, tail))
 
 
 def expand_kernel(where, got, base, edge):
@@ -303,24 +302,20 @@
 
 def collect_kernel(got, sums):
     first = iota((8, LANES), 0)
-    lane = iota((8, LANES), 1)
     table = jnp.zeros((8, LANES), F32)
     for f in range(8):
-        total = jnp.zeros((8, LANES), F32)
-        for l in range(2):
-            for y in range(4):
-                part = got[(l * 8 + f) * 4 + y, 8:16, :]
-                power = jnp.sum(jnp.where(lane == 50, part, 0.0), axis=1, keepdims=True)
-                total = total + (part + pltpu.roll(part, 64, 1)) * (jnp.exp2(power) * (1.0 / 1024.0))
-        table = jnp.where(first == f, total, table)
-    sums[...] = jnp.broadcast_to(pltpu.roll(table, 96, 1)[None], sums.shape)
-
-
-def final_kernel(diffusion, stiffness, got, sums, out):
+        rows = got[f * 8:f * 8 + 8, 8, :]
+        power = jnp.broadcast_to(rows[:, 50:51], rows.shape)
+        rows = (rows + pltpu.roll(rows, 64, 1)) * jnp.exp2(power)
+        table = jnp.where(first == f, jnp.sum(rows, axis=0, keepdims=True), table)
+    sums[...] = jnp.broadcast_to(pltpu.roll(table * (1.0 / 1024.0), 96, 1)[None], sums.shape)
+
+
+def final_kernel(where, diffusion, stiffness, got, sums, out):
     table = jnp.sum(sums[...], axis=0)
     lane = iota((8, LANES), 1)
     row = iota((8, 1), 0)
-    m = [jnp.sum(jnp.where(lane == k, table, 0.0), axis=1, keepdims=True) for k in range(6)]
+    m = [table[:, k:k + 1] for k in range(6)]
     d = jnp.ones((8, 1), F32)
     beta = jnp.ones((8, 1), F32)
     for f in range(FIELDS):
@@ -331,21 +326,22 @@
     scale = jnp.where(part == 0, 1.0, jnp.where(part == 1, k0, jnp.where(part == 2, k1, k2)))
     wide = part < 2
     for f in range(FIELDS):
-        factor = scale[f:f + 1]
+        rows = got[f * 8:f * 8 + 8, 8, :]
+        power = jnp.where(
+            part == 0, jnp.broadcast_to(rows[:, 48:49], rows.shape), jnp.broadcast_to(rows[:, 49:50], rows.shape)
+        )
+        factors = scale[f:f + 1] * jnp.exp2(power)
         low = jnp.zeros((8, LANES), F32)
         high = jnp.zeros((8, LANES), F32)
-        for c in range(8):
-            index = ((c // 4) * 8 + f) * 4 + c % 4
-            under = got[index, 8:16, :]
-            power0 = jnp.sum(jnp.where(lane == 48, under, 0.0), axis=1, keepdims=True)
-            power1 = jnp.sum(jnp.where(lane == 49, under, 0.0), axis=1, keepdims=True)
-            value = got[index, 0:8, :] + jnp.where(wide, under, 0.0)
-            value = value * factor * jnp.exp2(jnp.where(part == 0, power0, power1))
+        for p in range(8):
+            c = jnp.where(where[2] == 1, 7 - p, p)
+            value = got[f * 8 + p, 0:8, :] + jnp.where(wide, got[f * 8 + p, 8:16, :], 0.0)
+            value = value * factors[p:p + 1]
             value = value + pltpu.roll(value, 16, 1)
             value = value + pltpu.roll(value, 32, 1)
             here = (lane // 16) == c
-            low = jnp.where(here, pltpu.roll(value, (16 * (c - 3)) % LANES, 1), low)
-            high = jnp.where(here, pltpu.roll(value, (16 * (c - 7)) % LANES, 1), high)
+            low = jnp.where(here, pltpu.roll(value, (16 * c + 80) % LANES, 1), low)
+            high = jnp.where(here, pltpu.roll(value, (16 * c + 16) % LANES, 1), high)
         out[f, 0:8, :] = low
         out[f, 8:16, :] = high
 
@@ -369,17 +365,19 @@
 
 
 def borders():
-    def device(f, c, gz):
-        return (((c // 4) * 8 + f) * 4 + c % 4) * 8 + gz
-
-    pairs = [(device(f, 7, gz), device(f, 0, gz + 1)) for f in range(8) for gz in range(7)]
-    return pairs + [(b, a) for a, b in pairs]
-
-
-ALL = ("l", "f", "gy", "gz")
-GX = ("l", "f")
-PLANE = ("l", "f", "gy")
-GROUP = ("l", "gy", "gz")
+    pairs = []
+    for f in range(8):
+        for gz in range(7):
+            place = 7 if gz % 2 == 0 else 0
+            first = (f * 8 + place) * 8 + gz
+            pairs += [(first, first + 1), (first + 1, first)]
+    return pairs
+
+
+ALL = ("f", "z", "gy", "gz")
+GX = ("f", "z")
+PLANE = ("f", "z", "gy")
+GROUP = ("z", "gy", "gz")
 
 
 def exchange(value, axes):
@@ -391,16 +389,18 @@
 
 
 def body(gas_old, diffusion, stiffness, weights, velocity, rates, destination, tile_ids):
-    place = lax.axis_index("gz") * 8 + lax.axis_index("l") * 4 + lax.axis_index("gy")
-    where = jnp.stack([lax.axis_index("f"), place]).astype(jnp.int32)
+    odd = lax.axis_index("gz") % 2
+    place = lax.axis_index("z") * 4 + lax.axis_index("gy")
+    place = lax.axis_index("gz") * 8 + jnp.where(odd == 1, 7 - place, place)
+    where = jnp.stack([lax.axis_index("f"), place, odd]).astype(jnp.int32)
     gas_old, where = lax.optimization_barrier((gas_old, where))
     gas = gas_old.reshape(FIELDS, BLOCKS, LANES)
     gathered = exchange_short(jnp.broadcast_to(gas[None, 1:], (16, 6, BLOCKS, LANES)), GX)
     send, moved = call(
         parcel_kernel,
         [shaped(64, BLOCKS, LANES), shaped(3, BLOCKS, LANES)],
-        "ssvvvvv",
-        (destination[:, 0], tile_ids, gathered, gas, weights, velocity.transpose(1, 0, 2), rates),
+        "sssvvvvv",
+        (where, destination[:, 0], tile_ids, gathered, gas, weights, velocity.transpose(1, 0, 2), rates),
         [pltpu.VMEM((BLOCKS, 8, LANES), F32), pltpu.VMEM((8, BLOCKS, LANES), F32),
          pltpu.VMEM((BLOCKS, 8, LANES), F32), pltpu.VMEM((8, BLOCKS, LANES), F32)],
     )
@@ -426,13 +426,12 @@
     got = exchange_short(send.reshape(64, 16, LANES), PLANE)
     sums = call(collect_kernel, shaped(8, 8, LANES), "v", (got,))
     sums = exchange(sums, "gz")
-    out = call(final_kernel, shaped(FIELDS, BLOCKS, LANES), "ssvv", (diffusion, stiffness, got, sums))
+    out = call(final_kernel, shaped(FIELDS, BLOCKS, LANES), "sssvv", (where, diffusion, stiffness, got, sums))
     return out.reshape(gas_old.shape), moved.transpose(1, 0, 2)
 
 
 def solution(mesh):
-    fine = Mesh(mesh.devices.reshape(2, 8, 4, 8), ALL)
-    blocks = ("l", "f", "gy", "gz")
+    fine = Mesh(mesh.devices.reshape(8, 2, 4, 8), ALL)
     return jax.shard_map(
         body,
         mesh=fine,
@@ -440,12 +439,12 @@
             P(None, GX, "gy", "gz"),
             P(),
             P(),
-            P(blocks, None, None),
-            P(blocks, None, None),
-            P(blocks, None),
-            P(blocks, None),
-            P(blocks),
+            P(ALL, None, None),
+            P(ALL, None, None),
+            P(ALL, None),
+            P(ALL, None),
+            P(ALL),
         ),
-        out_specs=(P(None, GX, "gy", "gz"), P(blocks, None, None)),
+        out_specs=(P(None, GX, "gy", "gz"), P(ALL, None, None)),
         check_vma=False,
     )

time: 126 us -> 112 us (0.89)
  Pallas kernels: 19.1 us -> 8.25 us
  blocking collectives: 96.4 us -> 91.9 us
  starting transfers between devices: 4.9 us -> 6.46 us
    pallas_call x6, Pallas kernels: 19.1 us -> 8.25 us  [call(): pl.pallas_call(kernel, out_shape=listed, in_specs=[pl.BlockSpec(memory_sp...]
    all_to_all x5, blocking collectives: 96.4 us -> 91.9 us  [exchange(): return lax.all_to_all(value, axes, 0, 0, tiled=True)]
    ppermute x1, starting transfers between devices: 4.9 us -> 6.46 us  [body(): border = lax.ppermute(edge, ALL, borders())]
where the time goes in v4:
time: 112 us
  blocking collectives  91.9 us (82%)
  Pallas kernels  8.25 us (7%)
  starting transfers between devices  6.46 us (6%)
  waiting for transfers between devices  2.29 us (2%)
  local copies, waits for them, and re-layouts  1.73 us (2%)
    all_to_all x5, blocking collectives, exchange(): return lax.all_to_all(value, axes, 0, 0, tiled=True)  91.9 us
    pallas_call x6, Pallas kernels, call(): pl.pallas_call(kernel, out_shape=listed, in_specs=[pl.BlockSpec(memory_sp...  8.25 us
    ppermute x1, starting transfers between devices, body(): border = lax.ppermute(edge, ALL, borders())  6.46 us
    ppermute x1, waiting for transfers between devices, body(): border = lax.ppermute(edge, ALL, borders())  2.29 us
  transfers between devices with their start and end apart: 1, of which 1 were waited for; matrix products, arithmetic and copies ran while one was open for 0% of the time, Pallas kernels for 0%

profile of v4, /device:TPU:1, one launch (start us, length us, event | category | flops | bytes accessed | tf_op | source)
XLA Modules:
  0.0 111.7 jit_solution(4819887541993889002)
XLA Ops:
  0.6 0.0 copy-start.1
  0.7 0.1 pad_add_fusion.where
  0.7 0.7 copy-done.1
  1.5 0.1 broadcast_in_dim.2
  1.5 28.8 %all_to_all.25 = f16[16,6,16,128]{3,2,1,0:T(8,128)(2,1)S(1)} all-to-all(f16[16,6,16,128]{3,2,1,0:T(8,128)(2,1)S(1)} %broadcast_in_dim.2), channel_id=1, replica_groups=mesh['f'=8,'z'=2,'gy'=4,'gz'=8] {'f','z'}, dimensions={0} | all-to-all | bytes 786432 | tf_op jit(solution)/shard_map/all_to_all | solution.py:384
  30.4 0.0 copy-start
  30.4 0.0 copy-start.2
  30.4 0.1 convert_element_type.22.gathered
  30.4 0.0 copy-start.5
  30.5 0.0 copy-start.6
  30.5 0.0 copy-start.7
  30.5 0.9 copy-done
  31.4 0.0 copy-done.2
  31.4 0.0 copy-done.5
  31.4 0.0 copy-done.6
  31.4 0.0 copy-done.7
  31.4 2.0 %shard_map.95 = (f32[64,16,128]{2,1,0:T(8,128)S(1)}, f32[3,16,128]{2,1,0:T(8,128)}) custom-call(s32[3]{0:T(128)S(1)} %pad_add_fusion.where, s32[16]{0:T(128)S(1)} %bitcast.15, s32[16]{0:T(128)S(1)} %copy-done.7, f32[16,6,16,128]{3,2,1,0:T(8,128)S(1)} %convert_element_type.22.gathered, f32[7,16,128]{2,1,0:T(8,128)S(1)} %bitcast.13, ...), custom_call_target="tpu_custom_call" | custom-call | tf_op jit(solution)/shard_map/pallas_call | solution.py:352
  33.4 22.3 %all_to_all.26 = f16[64,16,128]{2,1,0:T(8,128)(2,1)S(1)} all-to-all(f16[64,16,128]{2,1,0:T(8,128)(2,1)S(1)} %convert_element_type.23), channel_id=1, replica_groups=mesh['f'=8,'z'=2,'gy'=4,'gz'=8] {'f','z','gy'}, dimensions={0} | all-to-all | bytes 524288 | tf_op jit(solution)/shard_map/all_to_all | solution.py:384
  55.7 1.1 shard_map.96
  56.8 0.0 copy-start.3
  56.8 0.0 copy-start.4
  56.8 6.5 %collective-permute-start = (f32[3,8,1024]{2,1,0:T(8,128)S(1)}, f32[3,8,1024]{2,1,0:T(8,128)S(1)}, u32[]{:S(2)}, u32[]{:S(2)}) collective-permute-start(f32[3,8,1024]{2,1,0:T(8,128)S(1)} %get-tuple-element.14), channel_id=1, source_target_pairs={{56,57},{57,56},{1,2},{2,1},{58,59},{59,58},{3,4},{4,3},{60,61},{6... | collective-permute-start | bytes 294920 | tf_op jit(solution)/shard_map/ppermute | solution.py:411
  63.3 2.3 %collective-permute-done.border = f32[3,8,1024]{2,1,0:T(8,128)S(1)} collective-permute-done((f32[3,8,1024]{2,1,0:T(8,128)S(1)}, f32[3,8,1024]{2,1,0:T(8,128)S(1)}, u32[]{:S(2)}, u32[]{:S(2)}) %collective-permute-start) | collective-permute-done | bytes 98336 | tf_op jit(solution)/shard_map/ppermute | solution.py:411
  65.6 0.0 copy-done.3
  65.6 0.0 copy-done.4
  65.6 1.3 %shard_map.97 = (f32[3,32,1024]{2,1,0:T(8,128)S(1)}, f32[64,1,128]{2,1,0:T(1,128)S(1)}) custom-call(s32[3]{0:T(128)S(1)} %pad_add_fusion.where, f32[7]{0:T(128)S(1)} %copy-done.3, f32[7]{0:T(128)S(1)} %copy-done.4, f32[3,32,1024]{2,1,0:T(8,128)S(1)} %get-tuple-element.13.base, f32[3,8,1024]{2,1,0:T(8,128)S(1)} %collective-permute-done.border), custom_call_target="tpu_custom_call" | custom-call | tf_op jit(solution)/shard_map/pallas_call | solution.py:352
  66.9 13.7 %all_to_all.27.got = f32[64,1,128]{2,1,0:T(1,128)S(1)} all-to-all(f32[64,1,128]{2,1,0:T(1,128)S(1)} %get-tuple-element.16), channel_id=1, replica_groups=mesh['f'=8,'z'=2,'gy'=4,'gz'=8] {'z','gy','gz'}, dimensions={0} | all-to-all | bytes 65536 | tf_op jit(solution)/shard_map/all_to_all | solution.py:384
  80.6 1.8 %shard_map.98 = f32[16,4,16,128]{3,2,1,0:T(8,128)S(1)} custom-call(s32[3]{0:T(128)S(1)} %pad_add_fusion.where, f32[7]{0:T(128)S(1)} %copy-done.3, f32[7]{0:T(128)S(1)} %copy-done.4, f32[3,32,1024]{2,1,0:T(8,128)S(1)} %get-tuple-element.13.base, f32[3,8,1024]{2,1,0:T(8,128)S(1)} %collective-permute-done.border, f32[3,32,1024]{2,1,0:T(8,128)S(1)} %get-tuple-element.15.basis, ...), custom_call_target="tpu_custom_call" | custom-call | tf_op jit(solution)/shard_map/pallas_call | solution.py:352
  82.5 17.1 %all_to_all.28 = f16[64,16,128]{2,1,0:T(8,128)(2,1)S(1)} all-to-all(f16[64,16,128]{2,1,0:T(8,128)(2,1)S(1)} %bitcast.17), channel_id=1, replica_groups=mesh['f'=8,'z'=2,'gy'=4,'gz'=8] {'f','z','gy'}, dimensions={0} | all-to-all | bytes 524288 | tf_op jit(solution)/shard_map/all_to_all | solution.py:384
  99.6 0.2 shard_map.99
  99.8 10.1 %all_to_all.29.sums = f32[8,8,128]{2,1,0:T(8,128)S(1)} all-to-all(f32[8,8,128]{2,1,0:T(8,128)S(1)} %shard_map.99), channel_id=1, replica_groups=mesh['f'=8,'z'=2,'gy'=4,'gz'=8] {'gz'}, dimensions={0} | all-to-all | bytes 65536 | tf_op jit(solution)/shard_map/all_to_all | solution.py:384
  109.9 1.9 %shard_map.100 = f32[7,16,128]{2,1,0:T(8,128)} custom-call(s32[3]{0:T(128)S(1)} %pad_add_fusion.where, f32[7]{0:T(128)S(1)} %copy-done.3, f32[7]{0:T(128)S(1)} %copy-done.4, f32[64,16,128]{2,1,0:T(8,128)S(1)} %convert_element_type.26.got, f32[8,8,128]{2,1,0:T(8,128)S(1)} %all_to_all.29.sums), custom_call_target="tpu_custom_call" | custom-call | tf_op jit(solution)/shard_map/pallas_call | solution.py:352
  (5 shorter events, 0.2 us)
Async XLA Ops:
  0.6 0.8 copy-start.1
  30.4 1.0 copy-start
  30.4 1.0 copy-start.2
  30.4 1.0 copy-start.5
  30.5 1.0 copy-start.6
  30.5 0.9 copy-start.7
  56.8 8.8 %copy-start.3 = (f32[7]{0:T(128)S(1)}, f32[7]{0:T(128)}, u32[]{:S(2)}) copy-start(f32[7]{0:T(128)} %diffusion.5) | copy-start | bytes 88
  56.8 8.8 %copy-start.4 = (f32[7]{0:T(128)S(1)}, f32[7]{0:T(128)}, u32[]{:S(2)}) copy-start(f32[7]{0:T(128)} %stiffness.5) | copy-start | bytes 88
  56.8 8.8 %collective-permute-start = (f32[3,8,1024]{2,1,0:T(8,128)S(1)}, f32[3,8,1024]{2,1,0:T(8,128)S(1)}, u32[]{:S(2)}, u32[]{:S(2)}) collective-permute-start(f32[3,8,1024]{2,1,0:T(8,128)S(1)} %get-tuple-element.14), channel_id=1, source_target_pairs={{56,57},{57,56},{1,2},{2,1},{58,59},{59,58},{3,4},{4,3},{60,61},{6... | collective-permute-start | bytes 294920 | tf_op jit(solution)/shard_map/ppermute | solution.py:411

commit v5 on v4

--- a/solution.py
+++ b/solution.py
@@ -35,16 +35,29 @@
     return lax.broadcasted_iota(jnp.int32, shape, dim)
 
 
+def fetch_kernel(*refs):
+    count = (len(refs) - 1) // 2
+    sems = refs[-1]
+    copies = [
+        pltpu.make_async_copy(source, target, sems.at[n])
+        for n, (source, target) in enumerate(zip(refs[:count], refs[count:-1]))
+    ]
+    for copy in copies:
+        copy.start()
+    for copy in copies:
+        copy.wait()
+
+
 def parcel_kernel(
-    where, dest, tile, gathered, gas, weights, velocity, rates, send, moved,
+    params, dest, tile, gathered, gas, weights, velocity, rates, send, moved,
     tiles_buf, at_buf, source_buf, dep_buf
 ):
     tiles_buf[...] = jnp.zeros_like(tiles_buf)
+    listed = dest[...] * 16 + tile[...]
+    code = [listed[0, b] for b in range(BLOCKS)]
     for b in range(BLOCKS):
-        owner = dest[b]
-        line = tile[b]
         for f in range(6):
-            tiles_buf[b, pl.ds(f, 1), :] = gathered[owner, f, pl.ds(line, 1), :]
+            tiles_buf[b, pl.ds(f, 1), :] = gathered[code[b] // 16, f, pl.ds(code[b] % 16, 1), :]
     for b in range(BLOCKS):
         high, low = split(tiles_buf[b])
         both = jnp.concatenate([high, low], axis=0)
@@ -74,21 +87,29 @@
     row = iota((BLOCKS, LANES), 0)
     spot = jnp.zeros((BLOCKS, LANES), F32)
     for b in range(BLOCKS):
-        code = (tile[b] % 8) * 32 + dest[b] * 2 + tile[b] // 8
-        spot = jnp.where(row == b, code.astype(F32), spot)
+        owner, line = code[b] // 16, code[b] % 16
+        place = (line % 8) * 32 + owner * 2 + line // 8
+        spot = jnp.where(row == b, place.astype(F32), spot)
+    flipped = params[6:7] > 0.5
     part = lane // 32
+    tails = []
     for c in range(8):
         start = 16 * c - HALO
-        tail = jnp.where(part == 2, pltpu.roll(dep_buf[7], (64 - start) % LANES, 1), spot)
-        for f in range(8):
-            src = min(f, FIELDS - 1)
+        tails.append(jnp.where(part == 2, pltpu.roll(dep_buf[7], (64 - start) % LANES, 1), spot))
+    for f in range(8):
+        src = min(f, FIELDS - 1)
+        pieces = []
+        for c in range(8):
+            start = 16 * c - HALO
             first = pltpu.roll(gas[src], (-start) % LANES, 1)
             second = pltpu.roll(dep_buf[src], (32 - start) % LANES, 1)
-            send[f * 8 + jnp.where(where[2] == 1, 7 - c, c)] = jnp.where(part == 0, first, jnp.where(part == 1, second, tail))
-
-
-def expand_kernel(where, got, base, edge):
-    moment = ((where[0] >= 1) & (where[0] <= 3)).astype(F32)
+            pieces.append(jnp.where(part == 0, first, jnp.where(part == 1, second, tails[c])))
+        for p in range(8):
+            send[f * 8 + p] = jnp.where(flipped, pieces[7 - p], pieces[p])
+
+
+def expand_kernel(params, got, base, edge):
+    moment = jnp.concatenate([params[1:2], params[1:2]], axis=1)
     target = iota((256, 256), 0)
     k = iota((256, 256), 1)
     perm = (target == (k % 8) * 32 + (k // 16) * 2 + (k % 16) // 8).astype(F32).astype(BF16)
@@ -106,25 +127,32 @@
         base[0, :, area] = held
         base[1, :, area] = held + 0.5 * value[:32]
         base[2, :, area] = 1.0 + 0.5 * moment * value[32:]
-    last = jnp.full((1, 1, 1), where[1] % 8) == 7
-    edge[...] = jnp.where(last, base[:, HALO + CHUNK - HALO:HALO + CHUNK], base[:, HALO:2 * HALO])
-
-
-def gather_neighbours(blocks):
-    shape = blocks[0].shape
+    last = params[3:4] > 0.5
+    for n in range(NQ):
+        area = slice(n * LANES, (n + 1) * LANES)
+        edge[:, :, area] = jnp.where(last, base[:, CHUNK:CHUNK + HALO, area], base[:, HALO:2 * HALO, area])
+
+
+def gather_neighbours(blocks, start=0, stop=CHUNK + 2 * HALO):
+    held = [v[start:stop] for v in blocks]
+    shape = held[0].shape
     lane = iota(shape, 1)
     place = lane % 32
-    ups = [pltpu.roll(v, 32, 1) for v in blocks]
-    downs = [pltpu.roll(v, LANES - 32, 1) for v in blocks]
+    ups = [pltpu.roll(v, 32, 1) for v in held]
+    downs = [pltpu.roll(v, LANES - 32, 1) for v in held]
     zero = jnp.zeros(shape, F32)
     out = []
     for q in range(NQ):
-        v = blocks[q]
+        v = held[q]
         total = jnp.where(place == 0, 0.0, pltpu.roll(v, 1, 1))
         total = total + jnp.where(place == 31, 0.0, pltpu.roll(v, LANES - 1, 1))
         total = total + jnp.where(lane < 32, ups[q - 1] if q > 0 else zero, ups[q])
         total = total + jnp.where(lane >= 96, downs[q + 1] if q < NQ - 1 else zero, downs[q])
-        total = total + pltpu.roll(v, 1, 0) + pltpu.roll(v, shape[0] - 1, 0)
+        whole = blocks[q]
+        if start:
+            total = total + whole[start - 1:stop - 1] + whole[start + 1:stop + 1]
+        else:
+            total = total + pltpu.roll(whole, 1, 0) + pltpu.roll(whole, stop - 1, 0)
         out.append(total)
     return out
 
@@ -147,14 +175,15 @@
 
     one = apply(residual)
     two = apply(one)
-    three = apply(two)
+    near = gather_neighbours(two, HALO, HALO + CHUNK)
+    three = [extra[n][HALO:HALO + CHUNK] * two[n][HALO:HALO + CHUNK] - near[n] * (1.0 / 6.0) for n in range(NQ)]
     rows = []
     for left, right in (
         (residual, residual), (residual, one), (one, one), (one, two), (two, two), (two, three)
     ):
         total = jnp.zeros((CHUNK, LANES), F32)
         for n in range(NQ):
-            total = total + left[n][HALO:HALO + CHUNK] * right[n][HALO:HALO + CHUNK]
+            total = total + left[n][HALO:HALO + CHUNK] * (right[n] if right is three else right[n][HALO:HALO + CHUNK])
         rows.append(jnp.sum(total, axis=0, keepdims=True))
     rows.append(jnp.zeros((2, LANES), F32))
     table = jnp.sum(jnp.concatenate(rows, axis=0), axis=1, keepdims=True)
@@ -204,10 +233,9 @@
     return step0 + alpha * e0, step1 + alpha * e1, alpha * e2
 
 
-def load(where, base, border, index):
-    c = where[1] % 8
+def load(params, base, border, index):
     plane = iota((CHUNK + 2 * HALO, LANES), 0)
-    swap = ((plane < HALO) & (c == 0)) | ((plane >= HALO + CHUNK) & (c == 7))
+    swap = jnp.where(plane < HALO, params[2:3], jnp.where(plane >= HALO + CHUNK, params[3:4], 0.0)) > 0.5
     out = []
     for n in range(NQ):
         area = slice(n * LANES, (n + 1) * LANES)
@@ -217,20 +245,24 @@
     return out
 
 
-def plane_mask(where):
+def plane_mask(params):
     plane = iota((CHUNK + 2 * HALO, LANES), 0)
-    outside = ((plane < HALO) & (where[1] == 0)) | ((plane >= HALO + CHUNK) & (where[1] == 63))
-    return jnp.where(outside, 0.0, 1.0).astype(F32)
-
-
-def first_kernel(where, diffusion, stiffness, base, border, basis, sums):
-    field = jnp.minimum(where[0], FIELDS - 1)
-    d = diffusion[field]
-    beta = stiffness[field]
-    q = load(where, base, border, 0)
-    rhs = load(where, base, border, 1)
-    damp = load(where, base, border, 2)
-    zero, one, two, line = newton_terms(q, rhs, damp, jnp.full((1, 1), d), beta, plane_mask(where))
+    return 1.0 - jnp.where(plane < HALO, params[4:5], jnp.where(plane >= HALO + CHUNK, params[5:6], 0.0))
+
+
+def pick(params, table):
+    field = jnp.minimum(params[0:1, 0:FIELDS], FIELDS - 1.0)
+    lane = iota((1, FIELDS), 1).astype(F32)
+    return jnp.sum(jnp.where(lane == field, table[...], 0.0), axis=1, keepdims=True)
+
+
+def first_kernel(params, diffusion, stiffness, base, border, basis, sums):
+    d = pick(params, diffusion)
+    beta = pick(params, stiffness)
+    q = load(params, base, border, 0)
+    rhs = load(params, base, border, 1)
+    damp = load(params, base, border, 2)
+    zero, one, two, line = newton_terms(q, rhs, damp, d, beta, plane_mask(params))
     for n in range(NQ):
         area = slice(n * LANES, (n + 1) * LANES)
         basis[0, :, area] = zero[n]
@@ -239,22 +271,21 @@
     sums[...] = jnp.broadcast_to(line[None], sums.shape)
 
 
-def second_kernel(where, diffusion, stiffness, base, border, basis, got, send, state_buf):
-    field = jnp.minimum(where[0], FIELDS - 1)
-    d = jnp.full((1, 1), diffusion[field])
-    beta = jnp.full((1, 1), stiffness[field])
+def second_kernel(params, diffusion, stiffness, base, border, basis, got, send, state_buf):
+    d = pick(params, diffusion)
+    beta = pick(params, stiffness)
     row = jnp.sum(got[...], axis=0)
     lane = iota((1, LANES), 1)
     m = [jnp.sum(jnp.where(lane == k, row, 0.0), axis=1, keepdims=True) for k in range(6)]
     k0, k1, k2 = coefficients(m, d, beta)
-    q = load(where, base, border, 0)
-    rhs = load(where, base, border, 1)
-    damp = load(where, base, border, 2)
+    q = load(params, base, border, 0)
+    rhs = load(params, base, border, 1)
+    damp = load(params, base, border, 2)
     state = []
     for n in range(NQ):
         area = slice(n * LANES, (n + 1) * LANES)
         state.append(q[n] + k0 * basis[0, :, area] + k1 * basis[1, :, area] + k2 * basis[2, :, area])
-    zero, one, two, line = newton_terms(state, rhs, damp, d, beta, plane_mask(where))
+    zero, one, two, line = newton_terms(state, rhs, damp, d, beta, plane_mask(params))
     inner = slice(HALO, HALO + CHUNK)
     powers = []
     for group in ((state,), (zero, one, two)):
@@ -311,39 +342,44 @@
     sums[...] = jnp.broadcast_to(pltpu.roll(table * (1.0 / 1024.0), 96, 1)[None], sums.shape)
 
 
-def final_kernel(where, diffusion, stiffness, got, sums, out):
+def final_kernel(params, diffusion, stiffness, got, sums, out):
     table = jnp.sum(sums[...], axis=0)
     lane = iota((8, LANES), 1)
     row = iota((8, 1), 0)
     m = [table[:, k:k + 1] for k in range(6)]
-    d = jnp.ones((8, 1), F32)
-    beta = jnp.ones((8, 1), F32)
-    for f in range(FIELDS):
-        d = jnp.where(row == f, diffusion[f], d)
-        beta = jnp.where(row == f, stiffness[f], beta)
+    own = iota((8, FIELDS), 0) == iota((8, FIELDS), 1)
+    spare = jnp.where(row == FIELDS, 1.0, 0.0)
+    d = jnp.sum(jnp.where(own, diffusion[...], 0.0), axis=1, keepdims=True) + spare
+    beta = jnp.sum(jnp.where(own, stiffness[...], 0.0), axis=1, keepdims=True) + spare
     k0, k1, k2 = coefficients(m, d, beta)
     part = (lane % 64) // 16
     scale = jnp.where(part == 0, 1.0, jnp.where(part == 1, k0, jnp.where(part == 2, k1, k2)))
     wide = part < 2
+    even = (lane // 16) % 2 == 0
+    lower = lane % 64 < 32
+    first = lane < 64
+    flipped = params[6:7] > 0.5
     for f in range(FIELDS):
         rows = got[f * 8:f * 8 + 8, 8, :]
         power = jnp.where(
             part == 0, jnp.broadcast_to(rows[:, 48:49], rows.shape), jnp.broadcast_to(rows[:, 49:50], rows.shape)
         )
         factors = scale[f:f + 1] * jnp.exp2(power)
-        low = jnp.zeros((8, LANES), F32)
-        high = jnp.zeros((8, LANES), F32)
+        places = []
         for p in range(8):
-            c = jnp.where(where[2] == 1, 7 - p, p)
             value = got[f * 8 + p, 0:8, :] + jnp.where(wide, got[f * 8 + p, 8:16, :], 0.0)
-            value = value * factors[p:p + 1]
-            value = value + pltpu.roll(value, 16, 1)
-            value = value + pltpu.roll(value, 32, 1)
-            here = (lane // 16) == c
-            low = jnp.where(here, pltpu.roll(value, (16 * c + 80) % LANES, 1), low)
-            high = jnp.where(here, pltpu.roll(value, (16 * c + 16) % LANES, 1), high)
-        out[f, 0:8, :] = low
-        out[f, 8:16, :] = high
+            places.append(value * factors[p:p + 1])
+        values = [jnp.where(flipped, places[7 - c], places[c]) for c in range(8)]
+        pairs = [
+            jnp.where(even, a + pltpu.roll(a, LANES - 16, 1), b + pltpu.roll(b, 16, 1))
+            for a, b in zip(values[0::2], values[1::2])
+        ]
+        left, right = [
+            jnp.where(lower, a + pltpu.roll(a, LANES - 32, 1), b + pltpu.roll(b, 32, 1))
+            for a, b in zip(pairs[0::2], pairs[1::2])
+        ]
+        out[f, 0:8, :] = jnp.where(first, left, pltpu.roll(right, 64, 1))
+        out[f, 8:16, :] = jnp.where(first, pltpu.roll(left, 64, 1), right)
 
 
 def call(kernel, shapes, spaces, args, scratch=()):
@@ -389,44 +425,67 @@
 
 
 def body(gas_old, diffusion, stiffness, weights, velocity, rates, destination, tile_ids):
-    odd = lax.axis_index("gz") % 2
+    field, gz = lax.axis_index("f"), lax.axis_index("gz")
     place = lax.axis_index("z") * 4 + lax.axis_index("gy")
-    place = lax.axis_index("gz") * 8 + jnp.where(odd == 1, 7 - place, place)
-    where = jnp.stack([lax.axis_index("f"), place, odd]).astype(jnp.int32)
-    gas_old, where = lax.optimization_barrier((gas_old, where))
-    gas = gas_old.reshape(FIELDS, BLOCKS, LANES)
+    odd = gz & 1
+    chunk = jnp.where(odd == 1, 7 - place, place)
+    first, last = chunk == 0, chunk == 7
+    flags = [
+        field, (field >= 1) & (field <= 3), first, last, first & (gz == 0), last & (gz == 7), odd, odd
+    ]
+    params = jnp.stack([jnp.asarray(flag).astype(F32) for flag in flags])[:, None]
+    params = jnp.broadcast_to(params, (8, LANES))
+    inputs = (
+        gas_old.reshape(FIELDS, BLOCKS, LANES), weights, velocity.transpose(1, 0, 2), rates,
+        destination.reshape(1, BLOCKS), tile_ids[None], diffusion[None], stiffness[None],
+    )
+    near = pl.pallas_call(
+        fetch_kernel,
+        out_shape=[jax.ShapeDtypeStruct(value.shape, value.dtype) for value in inputs],
+        in_specs=[pl.BlockSpec(memory_space=pl.ANY) for _ in inputs],
+        out_specs=[pl.BlockSpec(memory_space=pltpu.VMEM) for _ in inputs],
+        scratch_shapes=[pltpu.SemaphoreType.DMA((len(inputs),))],
+        compiler_params=pltpu.CompilerParams(vmem_limit_bytes=LIMIT),
+    )(*inputs)
+    gas, weights, velocity, rates, destination, tile_ids, diffusion, stiffness = near
+    gas, params = lax.optimization_barrier((gas, params))
     gathered = exchange_short(jnp.broadcast_to(gas[None, 1:], (16, 6, BLOCKS, LANES)), GX)
     send, moved = call(
         parcel_kernel,
         [shaped(64, BLOCKS, LANES), shaped(3, BLOCKS, LANES)],
-        "sssvvvvv",
-        (where, destination[:, 0], tile_ids, gathered, gas, weights, velocity.transpose(1, 0, 2), rates),
+        "vvvvvvvv",
+        (params, destination, tile_ids, gathered, gas, weights, velocity, rates),
         [pltpu.VMEM((BLOCKS, 8, LANES), F32), pltpu.VMEM((8, BLOCKS, LANES), F32),
          pltpu.VMEM((BLOCKS, 8, LANES), F32), pltpu.VMEM((8, BLOCKS, LANES), F32)],
     )
     got = exchange_short(send, PLANE).reshape(16, 4, BLOCKS, LANES)
     base, edge = call(
-        expand_kernel, [shaped(3, CHUNK + 2 * HALO, 1024), shaped(3, HALO, 1024)], "sv", (where, got)
+        expand_kernel, [shaped(3, CHUNK + 2 * HALO, 1024), shaped(3, HALO, 1024)], "vv", (params, got)
     )
     border = lax.ppermute(edge, ALL, borders())
     basis, sums = call(
         first_kernel,
         [shaped(3, CHUNK + 2 * HALO, 1024), shaped(64, 1, LANES)],
-        "sssvv",
-        (where, diffusion, stiffness, base, border),
+        "vvvvv",
+        (params, diffusion, stiffness, base, border),
     )
     sums = exchange(sums, GROUP)
     send = call(
         second_kernel,
         shaped(16, 4, 16, LANES),
-        "sssvvvv",
-        (where, diffusion, stiffness, base, border, basis, sums),
+        "vvvvvvv",
+        (params, diffusion, stiffness, base, border, basis, sums),
         [pltpu.VMEM((4 * CHUNK, 1024), F32)],
     )
     got = exchange_short(send.reshape(64, 16, LANES), PLANE)
     sums = call(collect_kernel, shaped(8, 8, LANES), "v", (got,))
     sums = exchange(sums, "gz")
-    out = call(final_kernel, shaped(FIELDS, BLOCKS, LANES), "sssvv", (where, diffusion, stiffness, got, sums))
+    out = call(
+        final_kernel,
+        shaped(FIELDS, BLOCKS, LANES),
+        "vvvvv",
+        (params, diffusion, stiffness, got, sums),
+    )
     return out.reshape(gas_old.shape), moved.transpose(1, 0, 2)
 
 

time: 112 us -> 110 us (0.982)
  Pallas kernels: 8.25 us -> 5.73 us
    pallas_call x6, Pallas kernels: 8.25 us -> 5.54 us  [call(): pl.pallas_call(kernel, out_shape=listed, in_specs=[pl.BlockSpec(memory_sp...]
where the time goes in v5:
time: 110 us; the launch traced here: 109 us
  blocking collectives  91.9 us (84%)
  starting transfers between devices  6.45 us (6%)
  Pallas kernels  5.73 us (5%)
  waiting for transfers between devices  2.29 us (2%)
  local copies, waits for them, and re-layouts  1.96 us (2%)
    all_to_all x5, blocking collectives, exchange(): return lax.all_to_all(value, axes, 0, 0, tiled=True)  91.9 us
    ppermute x1, starting transfers between devices, body(): border = lax.ppermute(edge, ALL, borders())  6.45 us
    pallas_call x6, Pallas kernels, call(): pl.pallas_call(kernel, out_shape=listed, in_specs=[pl.BlockSpec(memory_sp...  5.54 us
    ppermute x1, waiting for transfers between devices, body(): border = lax.ppermute(edge, ALL, borders())  2.29 us
  transfers between devices with their start and end apart: 1, of which 1 were waited for; matrix products, arithmetic and copies ran while one was open for 0% of the time, Pallas kernels for 0%

profile of v5, /device:TPU:1, one launch (start us, length us, event | category | flops | bytes accessed | tf_op | source)
XLA Modules:
  0.0 109.4 jit_solution(15283704125630154396)
XLA Ops:
  0.6 0.0 copy-start.1
  0.7 0.0 copy-start.2
  0.7 0.1 stack.52
  0.8 0.0 copy-start.3
  0.8 0.0 copy-start.7
  0.8 0.0 copy-start.4
  0.8 0.0 copy-start.5
  0.8 0.0 copy-start.6
  0.8 0.6 copy-done.1
  1.4 0.0 copy-done.2
  1.5 0.0 copy-done.3
  1.5 0.0 copy-done.7
  1.5 0.0 copy-done.4
  1.5 0.0 copy-done.5
  1.5 0.0 copy-done.6
  1.5 0.0 copy-start
  1.5 1.0 copy-done
  2.5 0.2 shard_map.95
  2.7 0.1 broadcast_in_dim.24.params
  2.8 0.1 broadcast_in_dim.25
  2.9 28.8 %all_to_all.25 = f16[16,6,16,128]{3,2,1,0:T(8,128)(2,1)S(1)} all-to-all(f16[16,6,16,128]{3,2,1,0:T(8,128)(2,1)S(1)} %broadcast_in_dim.25), channel_id=1, replica_groups=mesh['f'=8,'z'=2,'gy'=4,'gz'=8] {'f','z'}, dimensions={0} | all-to-all | bytes 786432 | tf_op jit(solution)/shard_map/all_to_all | solution.py:420
  31.7 0.1 convert_element_type.32.gathered
  31.8 1.6 %shard_map.96 = (f32[64,16,128]{2,1,0:T(8,128)S(1)}, f32[3,16,128]{2,1,0:T(8,128)}) custom-call(f32[8,128]{1,0:T(8,128)S(1)} %broadcast_in_dim.24.params, s32[1,16]{1,0:T(1,128)S(1)} %get-tuple-element.22.dest, s32[1,16]{1,0:T(1,128)S(1)} %get-tuple-element.23.tile, f32[16,6,16,128]{3,2,1,0:T(8,128)S(1)} %convert_element_type.32.gathered, ...), custom_call_target="tpu_custom_call" | custom-call | tf_op jit(solution)/shard_map/pallas_call | solution.py:388
  33.4 22.3 %all_to_all.26 = f16[64,16,128]{2,1,0:T(8,128)(2,1)S(1)} all-to-all(f16[64,16,128]{2,1,0:T(8,128)(2,1)S(1)} %convert_element_type.33), channel_id=1, replica_groups=mesh['f'=8,'z'=2,'gy'=4,'gz'=8] {'f','z','gy'}, dimensions={0} | all-to-all | bytes 524288 | tf_op jit(solution)/shard_map/all_to_all | solution.py:420
  55.7 0.5 shard_map.97
  56.3 6.5 %collective-permute-start = (f32[3,8,1024]{2,1,0:T(8,128)S(1)}, f32[3,8,1024]{2,1,0:T(8,128)S(1)}, u32[]{:S(2)}, u32[]{:S(2)}) collective-permute-start(f32[3,8,1024]{2,1,0:T(8,128)S(1)} %get-tuple-element.30), channel_id=1, source_target_pairs={{56,57},{57,56},{1,2},{2,1},{58,59},{59,58},{3,4},{4,3},{60,61},{6... | collective-permute-start | bytes 294920 | tf_op jit(solution)/shard_map/ppermute | solution.py:465
  62.7 2.3 %collective-permute-done.border = f32[3,8,1024]{2,1,0:T(8,128)S(1)} collective-permute-done((f32[3,8,1024]{2,1,0:T(8,128)S(1)}, f32[3,8,1024]{2,1,0:T(8,128)S(1)}, u32[]{:S(2)}, u32[]{:S(2)}) %collective-permute-start) | collective-permute-done | bytes 98336 | tf_op jit(solution)/shard_map/ppermute | solution.py:465
  65.0 0.8 shard_map.98
  65.8 13.7 %all_to_all.27.got = f32[64,1,128]{2,1,0:T(1,128)S(1)} all-to-all(f32[64,1,128]{2,1,0:T(1,128)S(1)} %get-tuple-element.32), channel_id=1, replica_groups=mesh['f'=8,'z'=2,'gy'=4,'gz'=8] {'z','gy','gz'}, dimensions={0} | all-to-all | bytes 65536 | tf_op jit(solution)/shard_map/all_to_all | solution.py:420
  79.5 1.3 %shard_map.99 = f32[16,4,16,128]{3,2,1,0:T(8,128)S(1)} custom-call(f32[8,128]{1,0:T(8,128)S(1)} %broadcast_in_dim.24.params, f32[1,7]{1,0:T(1,128)S(1)} %get-tuple-element.20.diffusion, f32[1,7]{1,0:T(1,128)S(1)} %get-tuple-element.21.stiffness, f32[3,32,1024]{2,1,0:T(8,128)S(1)} %get-tuple-element.29.base, f32[3,8,1024]{2,1,0:T(8,128)S(1)} %collective-permute-done.border, ...), custom_call_target="tpu_custom_call" | custom-call | tf_op jit(solution)/shard_map/pallas_call | solution.py:388
  80.8 17.1 %all_to_all.28 = f16[64,16,128]{2,1,0:T(8,128)(2,1)S(1)} all-to-all(f16[64,16,128]{2,1,0:T(8,128)(2,1)S(1)} %bitcast.25), channel_id=1, replica_groups=mesh['f'=8,'z'=2,'gy'=4,'gz'=8] {'f','z','gy'}, dimensions={0} | all-to-all | bytes 524288 | tf_op jit(solution)/shard_map/all_to_all | solution.py:420
  97.9 0.2 shard_map.100
  98.1 10.1 %all_to_all.29.sums = f32[8,8,128]{2,1,0:T(8,128)S(1)} all-to-all(f32[8,8,128]{2,1,0:T(8,128)S(1)} %shard_map.100), channel_id=1, replica_groups=mesh['f'=8,'z'=2,'gy'=4,'gz'=8] {'gz'}, dimensions={0} | all-to-all | bytes 65536 | tf_op jit(solution)/shard_map/all_to_all | solution.py:420
  108.2 1.2 %shard_map.101 = f32[7,16,128]{2,1,0:T(8,128)} custom-call(f32[8,128]{1,0:T(8,128)S(1)} %broadcast_in_dim.24.params, f32[1,7]{1,0:T(1,128)S(1)} %get-tuple-element.20.diffusion, f32[1,7]{1,0:T(1,128)S(1)} %get-tuple-element.21.stiffness, f32[64,16,128]{2,1,0:T(8,128)S(1)} %convert_element_type.36.got, f32[8,8,128]{2,1,0:T(8,128)S(1)} %all_to_all.29.sums), custom_call_target="tpu_custom_call" | custom-call | tf_op jit(solution)/shard_map/pallas_call | solution.py:388
  (5 shorter events, 0.2 us)
Async XLA Ops:
  0.6 0.8 copy-start.1
  0.7 0.8 copy-start.2
  0.8 0.7 copy-start.3
  0.8 0.7 copy-start.7
  0.8 0.7 copy-start.4
  0.8 0.7 copy-start.5
  0.8 0.7 copy-start.6
  1.5 1.0 copy-start
  56.3 8.7 %collective-permute-start = (f32[3,8,1024]{2,1,0:T(8,128)S(1)}, f32[3,8,1024]{2,1,0:T(8,128)S(1)}, u32[]{:S(2)}, u32[]{:S(2)}) collective-permute-start(f32[3,8,1024]{2,1,0:T(8,128)S(1)} %get-tuple-element.30), channel_id=1, source_target_pairs={{56,57},{57,56},{1,2},{2,1},{58,59},{59,58},{3,4},{4,3},{60,61},{6... | collective-permute-start | bytes 294920 | tf_op jit(solution)/shard_map/ppermute | solution.py:465

commit v6 on v5

--- a/solution.py
+++ b/solution.py
@@ -35,17 +35,20 @@
     return lax.broadcasted_iota(jnp.int32, shape, dim)
 
 
-def fetch_kernel(*refs):
-    count = (len(refs) - 1) // 2
-    sems = refs[-1]
-    copies = [
-        pltpu.make_async_copy(source, target, sems.at[n])
-        for n, (source, target) in enumerate(zip(refs[:count], refs[count:-1]))
-    ]
-    for copy in copies:
-        copy.start()
-    for copy in copies:
-        copy.wait()
+def fetch_kernel(velocity, rates, dest, tile, diffusion, stiffness, *outs):
+    for source, target in zip((velocity, rates, dest, tile, diffusion, stiffness), outs):
+        target[...] = source[...]
+    field, gz = lax.axis_index("f"), lax.axis_index("gz")
+    place = lax.axis_index("z") * 4 + lax.axis_index("gy")
+    odd = gz & 1
+    chunk = jnp.where(odd == 1, 7 - place, place)
+    first, last = chunk == 0, chunk == 7
+    flags = (field, (field >= 1) & (field <= 3), first, last, first & (gz == 0), last & (gz == 7), odd)
+    row = iota((8, LANES), 0)
+    table = jnp.zeros((8, LANES), F32)
+    for n, flag in enumerate(flags):
+        table = jnp.where(row == n, flag.astype(jnp.int32).astype(F32), table)
+    outs[-1][...] = table
 
 
 def parcel_kernel(
@@ -425,30 +428,20 @@
 
 
 def body(gas_old, diffusion, stiffness, weights, velocity, rates, destination, tile_ids):
-    field, gz = lax.axis_index("f"), lax.axis_index("gz")
-    place = lax.axis_index("z") * 4 + lax.axis_index("gy")
-    odd = gz & 1
-    chunk = jnp.where(odd == 1, 7 - place, place)
-    first, last = chunk == 0, chunk == 7
-    flags = [
-        field, (field >= 1) & (field <= 3), first, last, first & (gz == 0), last & (gz == 7), odd, odd
-    ]
-    params = jnp.stack([jnp.asarray(flag).astype(F32) for flag in flags])[:, None]
-    params = jnp.broadcast_to(params, (8, LANES))
+    weights = jnp.maximum(weights, 0)
     inputs = (
-        gas_old.reshape(FIELDS, BLOCKS, LANES), weights, velocity.transpose(1, 0, 2), rates,
+        velocity.transpose(1, 0, 2), rates,
         destination.reshape(1, BLOCKS), tile_ids[None], diffusion[None], stiffness[None],
     )
     near = pl.pallas_call(
         fetch_kernel,
-        out_shape=[jax.ShapeDtypeStruct(value.shape, value.dtype) for value in inputs],
-        in_specs=[pl.BlockSpec(memory_space=pl.ANY) for _ in inputs],
-        out_specs=[pl.BlockSpec(memory_space=pltpu.VMEM) for _ in inputs],
-        scratch_shapes=[pltpu.SemaphoreType.DMA((len(inputs),))],
+        out_shape=[jax.ShapeDtypeStruct(value.shape, value.dtype) for value in inputs] + [shaped(8, LANES)],
+        in_specs=[pl.BlockSpec(memory_space=pltpu.VMEM) for _ in inputs],
+        out_specs=[pl.BlockSpec(memory_space=pltpu.VMEM) for _ in range(len(inputs) + 1)],
         compiler_params=pltpu.CompilerParams(vmem_limit_bytes=LIMIT),
     )(*inputs)
-    gas, weights, velocity, rates, destination, tile_ids, diffusion, stiffness = near
-    gas, params = lax.optimization_barrier((gas, params))
+    velocity, rates, destination, tile_ids, diffusion, stiffness, params = near
+    gas = gas_old.reshape(FIELDS, BLOCKS, LANES)
     gathered = exchange_short(jnp.broadcast_to(gas[None, 1:], (16, 6, BLOCKS, LANES)), GX)
     send, moved = call(
         parcel_kernel,

time: 110 us -> 110 us (level)
  blocking collectives: 91.9 us -> 63.1 us
  starting transfers between devices: 6.45 us -> 22.8 us
  waiting for transfers between devices: 2.29 us -> 14.3 us
    all_to_all x5 -> x4, blocking collectives: 91.9 us -> 63.1 us  [exchange(): return lax.all_to_all(value, axes, 0, 0, tiled=True)]
    all_to_all x0 -> x1, starting transfers between devices: none -> 16.4 us  [exchange(): return lax.all_to_all(value, axes, 0, 0, tiled=True)]
    all_to_all x0 -> x1, waiting for transfers between devices: none -> 12 us  [exchange(): return lax.all_to_all(value, axes, 0, 0, tiled=True)]
  transfers between devices with their start and end apart: 1 -> 2, of which waited for: 1 -> 2; matrix products, arithmetic and copies ran while one was open for 0% -> 0% of each run, Pallas kernels for 0% -> 0%
where the time goes in v6:
time: 110 us; the launch traced here: 109 us
  blocking collectives  63.1 us (57%)
  starting transfers between devices  22.8 us (21%)
  waiting for transfers between devices  14.3 us (13%)
  Pallas kernels  5.56 us (5%)
  local copies, waits for them, and re-layouts  1.46 us (1%)
    all_to_all x4, blocking collectives, exchange(): return lax.all_to_all(value, axes, 0, 0, tiled=True)  63.1 us
    all_to_all x1, starting transfers between devices, exchange(): return lax.all_to_all(value, axes, 0, 0, tiled=True)  16.4 us
    all_to_all x1, waiting for transfers between devices, exchange(): return lax.all_to_all(value, axes, 0, 0, tiled=True)  12 us
    ppermute x1, starting transfers between devices, body(): border = lax.ppermute(edge, ALL, borders())  6.46 us
    pallas_call x6, Pallas kernels, call(): pl.pallas_call(kernel, out_shape=listed, in_specs=[pl.BlockSpec(memory_sp...  5.54 us
    ppermute x1, waiting for transfers between devices, body(): border = lax.ppermute(edge, ALL, borders())  2.29 us
  transfers between devices with their start and end apart: 2, of which 2 were waited for; matrix products, arithmetic and copies ran while one was open for 0% of the time, Pallas kernels for 0%

profile of v6, /device:TPU:1, one launch (start us, length us, event | category | flops | bytes accessed | tf_op | source)
XLA Modules:
  0.0 109.1 jit_solution(4853302855054577237)
XLA Ops:
  0.6 0.8 fusion
  1.4 0.0 copy-start.7
  1.4 0.8 broadcast_in_dim.18
  2.2 0.0 copy-start.1
  2.2 0.0 copy-start.6
  2.2 16.4 %all-to-all-start = ((f16[16,6,16,128]{3,2,1,0:T(8,128)(2,1)}), f16[16,6,16,128]{3,2,1,0:T(8,128)(2,1)S(1)}, u32[]{:S(2)}, u32[]{:S(2)}) async-start(f16[16,6,16,128]{3,2,1,0:T(8,128)(2,1)} %broadcast_in_dim.18), calls=%async_computation | async-start | bytes 786432 | tf_op jit(solution)/shard_map/all_to_all | solution.py:423
  18.6 0.0 copy-start.2
  18.6 0.0 copy-start.3
  18.6 0.0 copy-start.4
  18.6 0.0 copy-start.5
  18.7 0.0 copy-done.1
  18.7 0.0 copy-done.6
  18.7 0.6 copy-done.2
  19.3 0.0 copy-done.3
  19.3 0.0 copy-done.4
  19.3 0.0 copy-done.5
  19.3 0.0 copy-done.7
  19.4 0.0 copy-start
  19.4 12.0 %all-to-all-done = f16[16,6,16,128]{3,2,1,0:T(8,128)(2,1)S(1)} async-done(((f16[16,6,16,128]{3,2,1,0:T(8,128)(2,1)}), f16[16,6,16,128]{3,2,1,0:T(8,128)(2,1)S(1)}, u32[]{:S(2)}, u32[]{:S(2)}) %all-to-all-start) | async-done | bytes 393248 | tf_op jit(solution)/shard_map/all_to_all | solution.py:423
  31.4 0.1 convert_element_type.22.gathered
  31.5 0.0 copy-done
  31.5 1.6 %shard_map.96 = (f32[64,16,128]{2,1,0:T(8,128)S(1)}, f32[3,16,128]{2,1,0:T(8,128)}) custom-call(f32[8,128]{1,0:T(8,128)S(1)} %get-tuple-element.15.params, s32[1,16]{1,0:T(1,128)S(1)} %get-tuple-element.18.dest, s32[1,16]{1,0:T(1,128)S(1)} %get-tuple-element.19.tile, f32[16,6,16,128]{3,2,1,0:T(8,128)S(1)} %convert_element_type.22.gathered, ...), custom_call_target="tpu_custom_call" | custom-call | tf_op jit(solution)/shard_map/pallas_call | solution.py:391
  33.1 22.3 %all_to_all.25 = f16[64,16,128]{2,1,0:T(8,128)(2,1)S(1)} all-to-all(f16[64,16,128]{2,1,0:T(8,128)(2,1)S(1)} %convert_element_type.23), channel_id=1, replica_groups=mesh['f'=8,'z'=2,'gy'=4,'gz'=8] {'f','z','gy'}, dimensions={0} | all-to-all | bytes 524288 | tf_op jit(solution)/shard_map/all_to_all | solution.py:423
  55.4 0.5 shard_map.97
  56.0 6.5 %collective-permute-start = (f32[3,8,1024]{2,1,0:T(8,128)S(1)}, f32[3,8,1024]{2,1,0:T(8,128)S(1)}, u32[]{:S(2)}, u32[]{:S(2)}) collective-permute-start(f32[3,8,1024]{2,1,0:T(8,128)S(1)} %get-tuple-element.24), channel_id=1, source_target_pairs={{56,57},{57,56},{1,2},{2,1},{58,59},{59,58},{3,4},{4,3},{60,61},{6... | collective-permute-start | bytes 294920 | tf_op jit(solution)/shard_map/ppermute | solution.py:458
  62.4 2.3 %collective-permute-done.border = f32[3,8,1024]{2,1,0:T(8,128)S(1)} collective-permute-done((f32[3,8,1024]{2,1,0:T(8,128)S(1)}, f32[3,8,1024]{2,1,0:T(8,128)S(1)}, u32[]{:S(2)}, u32[]{:S(2)}) %collective-permute-start) | collective-permute-done | bytes 98336 | tf_op jit(solution)/shard_map/ppermute | solution.py:458
  64.7 0.8 shard_map.98
  65.5 13.7 %all_to_all.26.got = f32[64,1,128]{2,1,0:T(1,128)S(1)} all-to-all(f32[64,1,128]{2,1,0:T(1,128)S(1)} %get-tuple-element.26), channel_id=1, replica_groups=mesh['f'=8,'z'=2,'gy'=4,'gz'=8] {'z','gy','gz'}, dimensions={0} | all-to-all | bytes 65536 | tf_op jit(solution)/shard_map/all_to_all | solution.py:423
  79.2 1.3 %shard_map.99 = f32[16,4,16,128]{3,2,1,0:T(8,128)S(1)} custom-call(f32[8,128]{1,0:T(8,128)S(1)} %get-tuple-element.15.params, f32[1,7]{1,0:T(1,128)S(1)} %get-tuple-element.16.diffusion, f32[1,7]{1,0:T(1,128)S(1)} %get-tuple-element.17.stiffness, f32[3,32,1024]{2,1,0:T(8,128)S(1)} %get-tuple-element.23.base, f32[3,8,1024]{2,1,0:T(8,128)S(1)} %collective-permute-done.border, ...), custom_call_target="tpu_custom_call" | custom-call | tf_op jit(solution)/shard_map/pallas_call | solution.py:391
  80.5 17.1 %all_to_all.27 = f16[64,16,128]{2,1,0:T(8,128)(2,1)S(1)} all-to-all(f16[64,16,128]{2,1,0:T(8,128)(2,1)S(1)} %bitcast.20), channel_id=1, replica_groups=mesh['f'=8,'z'=2,'gy'=4,'gz'=8] {'f','z','gy'}, dimensions={0} | all-to-all | bytes 524288 | tf_op jit(solution)/shard_map/all_to_all | solution.py:423
  97.6 0.2 shard_map.100
  97.8 10.1 %all_to_all.28.sums = f32[8,8,128]{2,1,0:T(8,128)S(1)} all-to-all(f32[8,8,128]{2,1,0:T(8,128)S(1)} %shard_map.100), channel_id=1, replica_groups=mesh['f'=8,'z'=2,'gy'=4,'gz'=8] {'gz'}, dimensions={0} | all-to-all | bytes 65536 | tf_op jit(solution)/shard_map/all_to_all | solution.py:423
  107.9 1.2 %shard_map.101 = f32[7,16,128]{2,1,0:T(8,128)} custom-call(f32[8,128]{1,0:T(8,128)S(1)} %get-tuple-element.15.params, f32[1,7]{1,0:T(1,128)S(1)} %get-tuple-element.16.diffusion, f32[1,7]{1,0:T(1,128)S(1)} %get-tuple-element.17.stiffness, f32[64,16,128]{2,1,0:T(8,128)S(1)} %convert_element_type.26.got, f32[8,8,128]{2,1,0:T(8,128)S(1)} %all_to_all.28.sums), custom_call_target="tpu_custom_call" | custom-call | tf_op jit(solution)/shard_map/pallas_call | solution.py:391
  (6 shorter events, 0.2 us)
Async XLA Ops:
  1.4 17.9 %copy-start.7 = (bf16[16,128,128]{2,1,0:T(8,128)(2,1)S(1)}, bf16[16,128,128]{2,1,0:T(8,128)(2,1)}, u32[]{:S(2)}) copy-start(bf16[16,128,128]{2,1,0:T(8,128)(2,1)} %param.11) | copy-start | bytes 1572868
  2.2 16.4 %copy-start.1 = (bf16[16,3,128]{2,0,1:T(8,128)(2,1)S(1)}, bf16[16,3,128]{2,0,1:T(8,128)(2,1)}, u32[]{:S(2)}) copy-start(bf16[16,3,128]{2,0,1:T(8,128)(2,1)} %param.12) | copy-start | bytes 36868
  2.2 16.4 %copy-start.6 = (f32[7]{0:T(128)S(1)}, f32[7]{0:T(128)}, u32[]{:S(2)}) copy-start(f32[7]{0:T(128)} %param.10) | copy-start | bytes 88
  2.2 29.2 %all-to-all-start = ((f16[16,6,16,128]{3,2,1,0:T(8,128)(2,1)}), f16[16,6,16,128]{3,2,1,0:T(8,128)(2,1)S(1)}, u32[]{:S(2)}, u32[]{:S(2)}) async-start(f16[16,6,16,128]{3,2,1,0:T(8,128)(2,1)} %broadcast_in_dim.18), calls=%async_computation | async-start | bytes 786432 | tf_op jit(solution)/shard_map/all_to_all | solution.py:423
  18.6 0.7 copy-start.2
  18.6 0.7 copy-start.3
  18.6 0.7 copy-start.4
  18.6 0.7 copy-start.5
  19.4 12.1 %copy-start = (f32[7,2,8,128]{3,2,1,0:T(8,128)S(1)}, f32[7,2,8,128]{3,2,1,0:T(8,128)}, u32[]{:S(2)}) copy-start(f32[7,2,8,128]{3,2,1,0:T(8,128)} %param.8) | copy-start | bytes 172036
  56.0 8.7 %collective-permute-start = (f32[3,8,1024]{2,1,0:T(8,128)S(1)}, f32[3,8,1024]{2,1,0:T(8,128)S(1)}, u32[]{:S(2)}, u32[]{:S(2)}) collective-permute-start(f32[3,8,1024]{2,1,0:T(8,128)S(1)} %get-tuple-element.24), channel_id=1, source_target_pairs={{56,57},{57,56},{1,2},{2,1},{58,59},{59,58},{3,4},{4,3},{60,61},{6... | collective-permute-start | bytes 294920 | tf_op jit(solution)/shard_map/ppermute | solution.py:458

commit v7 on v6

--- a/solution.py
+++ b/solution.py
@@ -302,14 +302,16 @@
         area = slice(n * LANES, (n + 1) * LANES)
         for a, held in enumerate((state, zero, one, two)):
             state_buf[a * CHUNK:(a + 1) * CHUNK, area] = held[n][inner] * scales[min(a, 1)]
-    power = power_of(jnp.max(jnp.abs(line), axis=1, keepdims=True))
+    power = power_of(jnp.abs(line))
     scaled = line * jnp.exp2(-power) * 1024.0
     first = shorten(scaled)
-    rest = scaled - first
     lane = iota((8, LANES), 1)
-    extra = jnp.where(lane < 64, pltpu.roll(jnp.broadcast_to(first, (8, LANES)), 32, 1),
-                      pltpu.roll(jnp.broadcast_to(rest, (8, LANES)), 96, 1))
-    for spot, value in ((48, powers[0]), (49, powers[1]), (50, power)):
+
+    def spread(value, shift):
+        return pltpu.roll(jnp.broadcast_to(value, (8, LANES)), shift, 1)
+
+    extra = jnp.where(lane < 48, spread(first, 32), jnp.where(lane < 64, spread(power, 50), spread(scaled - first, 96)))
+    for spot, value in ((48, powers[0]), (49, powers[1])):
         extra = jnp.where(lane == spot, value, extra)
     out = iota((LANES, 256), 0)
     k = iota((LANES, 256), 1)
@@ -336,16 +338,19 @@
 
 def collect_kernel(got, sums):
     first = iota((8, LANES), 0)
+    lane = iota((8, LANES), 1)
+    used = (lane >= 32) & (lane < 38)
     table = jnp.zeros((8, LANES), F32)
     for f in range(8):
         rows = got[f * 8:f * 8 + 8, 8, :]
-        power = jnp.broadcast_to(rows[:, 50:51], rows.shape)
-        rows = (rows + pltpu.roll(rows, 64, 1)) * jnp.exp2(power)
+        power = jnp.where(used, pltpu.roll(rows, LANES - 18, 1), 0.0)
+        rows = jnp.where(used, rows + pltpu.roll(rows, 64, 1), 0.0) * jnp.exp2(power)
         table = jnp.where(first == f, jnp.sum(rows, axis=0, keepdims=True), table)
     sums[...] = jnp.broadcast_to(pltpu.roll(table * (1.0 / 1024.0), 96, 1)[None], sums.shape)
 
 
-def final_kernel(params, diffusion, stiffness, got, sums, out):
+def final_kernel(params, diffusion, stiffness, got, sums, moved, out, velocity):
+    velocity[...] = moved[...]
     table = jnp.sum(sums[...], axis=0)
     lane = iota((8, LANES), 1)
     row = iota((8, 1), 0)
@@ -473,11 +478,11 @@
     got = exchange_short(send.reshape(64, 16, LANES), PLANE)
     sums = call(collect_kernel, shaped(8, 8, LANES), "v", (got,))
     sums = exchange(sums, "gz")
-    out = call(
+    out, moved = call(
         final_kernel,
-        shaped(FIELDS, BLOCKS, LANES),
-        "vvvvv",
-        (params, diffusion, stiffness, got, sums),
+        [shaped(FIELDS, BLOCKS, LANES), shaped(3, BLOCKS, LANES)],
+        "vvvvvv",
+        (params, diffusion, stiffness, got, sums, moved),
     )
     return out.reshape(gas_old.shape), moved.transpose(1, 0, 2)
 

time: 110 us -> 109 us (level)
  no operation moved by 1% of the time
where the time goes in v7:
time: 109 us
  blocking collectives  63.1 us (58%)
  starting transfers between devices  22.8 us (21%)
  waiting for transfers between devices  14.3 us (13%)
  Pallas kernels  4.99 us (5%)
  local copies, waits for them, and re-layouts  1.47 us (1%)
    all_to_all x4, blocking collectives, exchange(): return lax.all_to_all(value, axes, 0, 0, tiled=True)  63.1 us
    all_to_all x1, starting transfers between devices, exchange(): return lax.all_to_all(value, axes, 0, 0, tiled=True)  16.4 us
    all_to_all x1, waiting for transfers between devices, exchange(): return lax.all_to_all(value, axes, 0, 0, tiled=True)  12 us
    ppermute x1, starting transfers between devices, body(): border = lax.ppermute(edge, ALL, borders())  6.46 us
    pallas_call x6, Pallas kernels, call(): pl.pallas_call(kernel, out_shape=listed, in_specs=[pl.BlockSpec(memory_sp...  4.97 us
    ppermute x1, waiting for transfers between devices, body(): border = lax.ppermute(edge, ALL, borders())  2.29 us
  transfers between devices with their start and end apart: 2, of which 2 were waited for; matrix products, arithmetic and copies ran while one was open for 0% of the time, Pallas kernels for 0%

profile of v7, /device:TPU:1, one launch (start us, length us, event | category | flops | bytes accessed | tf_op | source)
XLA Modules:
  0.0 108.5 jit_solution(1426127337254535343)
XLA Ops:
  0.6 0.8 fusion
  1.4 0.0 copy-start.7
  1.4 0.8 broadcast_in_dim.18
  2.2 0.0 copy-start.1
  2.2 0.0 copy-start.6
  2.2 16.4 %all-to-all-start = ((f16[16,6,16,128]{3,2,1,0:T(8,128)(2,1)}), f16[16,6,16,128]{3,2,1,0:T(8,128)(2,1)S(1)}, u32[]{:S(2)}, u32[]{:S(2)}) async-start(f16[16,6,16,128]{3,2,1,0:T(8,128)(2,1)} %broadcast_in_dim.18), calls=%async_computation | async-start | bytes 786432 | tf_op jit(solution)/shard_map/all_to_all | solution.py:428
  18.6 0.0 copy-start.2
  18.6 0.0 copy-start.3
  18.6 0.0 copy-start.4
  18.6 0.0 copy-start.5
  18.7 0.0 copy-done.1
  18.7 0.0 copy-done.6
  18.7 0.6 copy-done.2
  19.3 0.0 copy-done.3
  19.3 0.0 copy-done.4
  19.3 0.0 copy-done.5
  19.3 0.0 copy-done.7
  19.4 0.0 copy-start
  19.4 12.0 %all-to-all-done = f16[16,6,16,128]{3,2,1,0:T(8,128)(2,1)S(1)} async-done(((f16[16,6,16,128]{3,2,1,0:T(8,128)(2,1)}), f16[16,6,16,128]{3,2,1,0:T(8,128)(2,1)S(1)}, u32[]{:S(2)}, u32[]{:S(2)}) %all-to-all-start) | async-done | bytes 393248 | tf_op jit(solution)/shard_map/all_to_all | solution.py:428
  31.4 0.1 convert_element_type.22.gathered
  31.5 0.0 copy-done
  31.5 1.0 shard_map.96
  32.6 22.3 %all_to_all.25 = f16[64,16,128]{2,1,0:T(8,128)(2,1)S(1)} all-to-all(f16[64,16,128]{2,1,0:T(8,128)(2,1)S(1)} %convert_element_type.23), channel_id=1, replica_groups=mesh['f'=8,'z'=2,'gy'=4,'gz'=8] {'f','z','gy'}, dimensions={0} | all-to-all | bytes 524288 | tf_op jit(solution)/shard_map/all_to_all | solution.py:428
  54.9 0.5 shard_map.97
  55.5 6.5 %collective-permute-start = (f32[3,8,1024]{2,1,0:T(8,128)S(1)}, f32[3,8,1024]{2,1,0:T(8,128)S(1)}, u32[]{:S(2)}, u32[]{:S(2)}) collective-permute-start(f32[3,8,1024]{2,1,0:T(8,128)S(1)} %get-tuple-element.26), channel_id=1, source_target_pairs={{56,57},{57,56},{1,2},{2,1},{58,59},{59,58},{3,4},{4,3},{60,61},{6... | collective-permute-start | bytes 294920 | tf_op jit(solution)/shard_map/ppermute | solution.py:463
  61.9 2.3 %collective-permute-done.border = f32[3,8,1024]{2,1,0:T(8,128)S(1)} collective-permute-done((f32[3,8,1024]{2,1,0:T(8,128)S(1)}, f32[3,8,1024]{2,1,0:T(8,128)S(1)}, u32[]{:S(2)}, u32[]{:S(2)}) %collective-permute-start) | collective-permute-done | bytes 98336 | tf_op jit(solution)/shard_map/ppermute | solution.py:463
  64.2 0.8 shard_map.98
  65.0 13.7 %all_to_all.26.got = f32[64,1,128]{2,1,0:T(1,128)S(1)} all-to-all(f32[64,1,128]{2,1,0:T(1,128)S(1)} %get-tuple-element.28), channel_id=1, replica_groups=mesh['f'=8,'z'=2,'gy'=4,'gz'=8] {'z','gy','gz'}, dimensions={0} | all-to-all | bytes 65536 | tf_op jit(solution)/shard_map/all_to_all | solution.py:428
  78.7 1.3 %shard_map.99 = f32[16,4,16,128]{3,2,1,0:T(8,128)S(1)} custom-call(f32[8,128]{1,0:T(8,128)S(1)} %get-tuple-element.17.params, f32[1,7]{1,0:T(1,128)S(1)} %get-tuple-element.18.diffusion, f32[1,7]{1,0:T(1,128)S(1)} %get-tuple-element.19.stiffness, f32[3,32,1024]{2,1,0:T(8,128)S(1)} %get-tuple-element.25.base, f32[3,8,1024]{2,1,0:T(8,128)S(1)} %collective-permute-done.border, ...), custom_call_target="tpu_custom_call" | custom-call | tf_op jit(solution)/shard_map/pallas_call | solution.py:396
  80.0 17.1 %all_to_all.27 = f16[64,16,128]{2,1,0:T(8,128)(2,1)S(1)} all-to-all(f16[64,16,128]{2,1,0:T(8,128)(2,1)S(1)} %bitcast.20), channel_id=1, replica_groups=mesh['f'=8,'z'=2,'gy'=4,'gz'=8] {'f','z','gy'}, dimensions={0} | all-to-all | bytes 524288 | tf_op jit(solution)/shard_map/all_to_all | solution.py:428
  97.1 0.2 shard_map.100
  97.3 10.1 %all_to_all.28.sums = f32[8,8,128]{2,1,0:T(8,128)S(1)} all-to-all(f32[8,8,128]{2,1,0:T(8,128)S(1)} %shard_map.100), channel_id=1, replica_groups=mesh['f'=8,'z'=2,'gy'=4,'gz'=8] {'gz'}, dimensions={0} | all-to-all | bytes 65536 | tf_op jit(solution)/shard_map/all_to_all | solution.py:428
  107.3 1.2 %shard_map.101 = (f32[7,16,128]{2,1,0:T(8,128)}, f32[3,16,128]{2,1,0:T(8,128)}) custom-call(f32[8,128]{1,0:T(8,128)S(1)} %get-tuple-element.17.params, f32[1,7]{1,0:T(1,128)S(1)} %get-tuple-element.18.diffusion, f32[1,7]{1,0:T(1,128)S(1)} %get-tuple-element.19.stiffness, f32[64,16,128]{2,1,0:T(8,128)S(1)} %convert_element_type.26.got, ...), custom_call_target="tpu_custom_call" | custom-call | tf_op jit(solution)/shard_map/pallas_call | solution.py:396
  (6 shorter events, 0.2 us)
Async XLA Ops:
  1.4 17.9 %copy-start.7 = (bf16[16,128,128]{2,1,0:T(8,128)(2,1)S(1)}, bf16[16,128,128]{2,1,0:T(8,128)(2,1)}, u32[]{:S(2)}) copy-start(bf16[16,128,128]{2,1,0:T(8,128)(2,1)} %param.11) | copy-start | bytes 1572868
  2.2 16.4 %copy-start.1 = (bf16[16,3,128]{2,0,1:T(8,128)(2,1)S(1)}, bf16[16,3,128]{2,0,1:T(8,128)(2,1)}, u32[]{:S(2)}) copy-start(bf16[16,3,128]{2,0,1:T(8,128)(2,1)} %param.12) | copy-start | bytes 36868
  2.2 16.4 %copy-start.6 = (f32[7]{0:T(128)S(1)}, f32[7]{0:T(128)}, u32[]{:S(2)}) copy-start(f32[7]{0:T(128)} %param.10) | copy-start | bytes 88
  2.2 29.2 %all-to-all-start = ((f16[16,6,16,128]{3,2,1,0:T(8,128)(2,1)}), f16[16,6,16,128]{3,2,1,0:T(8,128)(2,1)S(1)}, u32[]{:S(2)}, u32[]{:S(2)}) async-start(f16[16,6,16,128]{3,2,1,0:T(8,128)(2,1)} %broadcast_in_dim.18), calls=%async_computation | async-start | bytes 786432 | tf_op jit(solution)/shard_map/all_to_all | solution.py:428
  18.6 0.7 copy-start.2
  18.6 0.7 copy-start.3
  18.6 0.7 copy-start.4
  18.6 0.7 copy-start.5
  19.4 12.1 %copy-start = (f32[7,2,8,128]{3,2,1,0:T(8,128)S(1)}, f32[7,2,8,128]{3,2,1,0:T(8,128)}, u32[]{:S(2)}) copy-start(f32[7,2,8,128]{3,2,1,0:T(8,128)} %param.8) | copy-start | bytes 172036
  55.5 8.7 %collective-permute-start = (f32[3,8,1024]{2,1,0:T(8,128)S(1)}, f32[3,8,1024]{2,1,0:T(8,128)S(1)}, u32[]{:S(2)}, u32[]{:S(2)}) collective-permute-start(f32[3,8,1024]{2,1,0:T(8,128)S(1)} %get-tuple-element.26), channel_id=1, source_target_pairs={{56,57},{57,56},{1,2},{2,1},{58,59},{59,58},{3,4},{4,3},{60,61},{6... | collective-permute-start | bytes 294920 | tf_op jit(solution)/shard_map/ppermute | solution.py:463

commit v8 on v7

--- a/solution.py
+++ b/solution.py
@@ -279,7 +279,7 @@
     beta = pick(params, stiffness)
     row = jnp.sum(got[...], axis=0)
     lane = iota((1, LANES), 1)
-    m = [jnp.sum(jnp.where(lane == k, row, 0.0), axis=1, keepdims=True) for k in range(6)]
+    m = [row[:, k:k + 1] for k in range(6)]
     k0, k1, k2 = coefficients(m, d, beta)
     q = load(params, base, border, 0)
     rhs = load(params, base, border, 1)
@@ -460,7 +460,7 @@
     base, edge = call(
         expand_kernel, [shaped(3, CHUNK + 2 * HALO, 1024), shaped(3, HALO, 1024)], "vv", (params, got)
     )
-    border = lax.ppermute(edge, ALL, borders())
+    border = lax.ppermute(edge.astype(F16), ALL, borders()).astype(F32)
     basis, sums = call(
         first_kernel,
         [shaped(3, CHUNK + 2 * HALO, 1024), shaped(64, 1, LANES)],

time: 109 us -> 109 us (level)
  no operation moved by 1% of the time
where the time goes in v8:
time: 109 us
  blocking collectives  63.5 us (58%)
  starting transfers between devices  22.8 us (21%)
  waiting for transfers between devices  13.8 us (13%)
  Pallas kernels  5.03 us (5%)
  local copies, waits for them, and re-layouts  1.47 us (1%)
  other arithmetic  1.09 us (1%)
    all_to_all x4, blocking collectives, exchange(): return lax.all_to_all(value, axes, 0, 0, tiled=True)  63.5 us
    all_to_all x1, starting transfers between devices, exchange(): return lax.all_to_all(value, axes, 0, 0, tiled=True)  16.4 us
    all_to_all x1, waiting for transfers between devices, exchange(): return lax.all_to_all(value, axes, 0, 0, tiled=True)  12 us
    ppermute x1, starting transfers between devices, body(): border = lax.ppermute(edge.astype(F16), ALL, borders()).astype(F32)  6.46 us
    pallas_call x6, Pallas kernels, call(): pl.pallas_call(kernel, out_shape=listed, in_specs=[pl.BlockSpec(memory_sp...  5.01 us
  transfers between devices with their start and end apart: 2, of which 2 were waited for; matrix products, arithmetic and copies ran while one was open for 0% of the time, Pallas kernels for 0%

profile of v8, /device:TPU:1, one launch (start us, length us, event | category | flops | bytes accessed | tf_op | source)
XLA Modules:
  0.0 108.5 jit_solution(8073435625937335267)
XLA Ops:
  0.6 0.8 fusion
  1.4 0.0 copy-start.7
  1.4 0.8 broadcast_in_dim.18
  2.2 0.0 copy-start.1
  2.2 0.0 copy-start.6
  2.2 16.4 %all-to-all-start = ((f16[16,6,16,128]{3,2,1,0:T(8,128)(2,1)}), f16[16,6,16,128]{3,2,1,0:T(8,128)(2,1)S(1)}, u32[]{:S(2)}, u32[]{:S(2)}) async-start(f16[16,6,16,128]{3,2,1,0:T(8,128)(2,1)} %broadcast_in_dim.18), calls=%async_computation | async-start | bytes 786432 | tf_op jit(solution)/shard_map/all_to_all | solution.py:428
  18.6 0.0 copy-start.2
  18.6 0.0 copy-start.3
  18.6 0.0 copy-start.4
  18.6 0.0 copy-start.5
  18.7 0.0 copy-done.1
  18.7 0.0 copy-done.6
  18.7 0.6 copy-done.2
  19.3 0.0 copy-done.3
  19.3 0.0 copy-done.4
  19.3 0.0 copy-done.5
  19.3 0.0 copy-done.7
  19.4 0.0 copy-start
  19.4 12.0 %all-to-all-done = f16[16,6,16,128]{3,2,1,0:T(8,128)(2,1)S(1)} async-done(((f16[16,6,16,128]{3,2,1,0:T(8,128)(2,1)}), f16[16,6,16,128]{3,2,1,0:T(8,128)(2,1)S(1)}, u32[]{:S(2)}, u32[]{:S(2)}) %all-to-all-start) | async-done | bytes 393248 | tf_op jit(solution)/shard_map/all_to_all | solution.py:428
  31.4 0.1 convert_element_type.28.gathered
  31.5 0.0 copy-done
  31.5 1.0 shard_map.96
  32.6 22.3 %all_to_all.25 = f16[64,16,128]{2,1,0:T(8,128)(2,1)S(1)} all-to-all(f16[64,16,128]{2,1,0:T(8,128)(2,1)S(1)} %convert_element_type.29), channel_id=1, replica_groups=mesh['f'=8,'z'=2,'gy'=4,'gz'=8] {'f','z','gy'}, dimensions={0} | all-to-all | bytes 524288 | tf_op jit(solution)/shard_map/all_to_all | solution.py:428
  54.9 0.5 shard_map.97
  55.5 6.5 %collective-permute-start = (f16[3,8,1024]{2,1,0:T(8,128)(2,1)S(1)}, f16[3,8,1024]{2,1,0:T(8,128)(2,1)S(1)}, u32[]{:S(2)}, u32[]{:S(2)}) collective-permute-start(f16[3,8,1024]{2,1,0:T(8,128)(2,1)S(1)} %convert_element_type.30), channel_id=1, source_target_pairs={{56,57},{57,56},{1,2},{2,1},{58,59},{59,58},{3,4},{4,3},{60,61},{6... | collective-permute-start | bytes 147464 | tf_op jit(solution)/shard_map/ppermute | solution.py:463
  62.0 1.8 %collective-permute-done = f16[3,8,1024]{2,1,0:T(8,128)(2,1)S(1)} collective-permute-done((f16[3,8,1024]{2,1,0:T(8,128)(2,1)S(1)}, f16[3,8,1024]{2,1,0:T(8,128)(2,1)S(1)}, u32[]{:S(2)}, u32[]{:S(2)}) %collective-permute-start) | collective-permute-done | bytes 49184 | tf_op jit(solution)/shard_map/ppermute | solution.py:463
  63.7 0.8 shard_map.98
  64.5 13.7 %all_to_all.26.got = f32[64,1,128]{2,1,0:T(1,128)S(1)} all-to-all(f32[64,1,128]{2,1,0:T(1,128)S(1)} %get-tuple-element.28), channel_id=1, replica_groups=mesh['f'=8,'z'=2,'gy'=4,'gz'=8] {'z','gy','gz'}, dimensions={0} | all-to-all | bytes 65536 | tf_op jit(solution)/shard_map/all_to_all | solution.py:428
  78.2 1.3 %shard_map.99 = f32[16,4,16,128]{3,2,1,0:T(8,128)S(1)} custom-call(f32[8,128]{1,0:T(8,128)S(1)} %get-tuple-element.17.params, f32[1,7]{1,0:T(1,128)S(1)} %get-tuple-element.18.diffusion, f32[1,7]{1,0:T(1,128)S(1)} %get-tuple-element.19.stiffness, f32[3,32,1024]{2,1,0:T(8,128)S(1)} %get-tuple-element.25.base, f32[3,8,1024]{2,1,0:T(8,128)S(1)} %convert_element_type.31.border, ...), custom_call_target="tpu_custom_call" | custom-call | tf_op jit(solution)/shard_map/pallas_call | solution.py:396
  79.5 17.5 %all_to_all.27 = f16[64,16,128]{2,1,0:T(8,128)(2,1)S(1)} all-to-all(f16[64,16,128]{2,1,0:T(8,128)(2,1)S(1)} %bitcast.20), channel_id=1, replica_groups=mesh['f'=8,'z'=2,'gy'=4,'gz'=8] {'f','z','gy'}, dimensions={0} | all-to-all | bytes 524288 | tf_op jit(solution)/shard_map/all_to_all | solution.py:428
  97.1 0.2 shard_map.100
  97.3 10.1 %all_to_all.28.sums = f32[8,8,128]{2,1,0:T(8,128)S(1)} all-to-all(f32[8,8,128]{2,1,0:T(8,128)S(1)} %shard_map.100), channel_id=1, replica_groups=mesh['f'=8,'z'=2,'gy'=4,'gz'=8] {'gz'}, dimensions={0} | all-to-all | bytes 65536 | tf_op jit(solution)/shard_map/all_to_all | solution.py:428
  107.3 1.2 %shard_map.101 = (f32[7,16,128]{2,1,0:T(8,128)}, f32[3,16,128]{2,1,0:T(8,128)}) custom-call(f32[8,128]{1,0:T(8,128)S(1)} %get-tuple-element.17.params, f32[1,7]{1,0:T(1,128)S(1)} %get-tuple-element.18.diffusion, f32[1,7]{1,0:T(1,128)S(1)} %get-tuple-element.19.stiffness, f32[64,16,128]{2,1,0:T(8,128)S(1)} %convert_element_type.34.got, ...), custom_call_target="tpu_custom_call" | custom-call | tf_op jit(solution)/shard_map/pallas_call | solution.py:396
  (8 shorter events, 0.2 us)
Async XLA Ops:
  1.4 17.9 %copy-start.7 = (bf16[16,128,128]{2,1,0:T(8,128)(2,1)S(1)}, bf16[16,128,128]{2,1,0:T(8,128)(2,1)}, u32[]{:S(2)}) copy-start(bf16[16,128,128]{2,1,0:T(8,128)(2,1)} %param.11) | copy-start | bytes 1572868
  2.2 16.4 %copy-start.1 = (bf16[16,3,128]{2,0,1:T(8,128)(2,1)S(1)}, bf16[16,3,128]{2,0,1:T(8,128)(2,1)}, u32[]{:S(2)}) copy-start(bf16[16,3,128]{2,0,1:T(8,128)(2,1)} %param.12) | copy-start | bytes 36868
  2.2 16.4 %copy-start.6 = (f32[7]{0:T(128)S(1)}, f32[7]{0:T(128)}, u32[]{:S(2)}) copy-start(f32[7]{0:T(128)} %param.10) | copy-start | bytes 88
  2.2 29.2 %all-to-all-start = ((f16[16,6,16,128]{3,2,1,0:T(8,128)(2,1)}), f16[16,6,16,128]{3,2,1,0:T(8,128)(2,1)S(1)}, u32[]{:S(2)}, u32[]{:S(2)}) async-start(f16[16,6,16,128]{3,2,1,0:T(8,128)(2,1)} %broadcast_in_dim.18), calls=%async_computation | async-start | bytes 786432 | tf_op jit(solution)/shard_map/all_to_all | solution.py:428
  18.6 0.7 copy-start.2
  18.6 0.7 copy-start.3
  18.6 0.7 copy-start.4
  18.6 0.7 copy-start.5
  19.4 12.1 %copy-start = (f32[7,2,8,128]{3,2,1,0:T(8,128)S(1)}, f32[7,2,8,128]{3,2,1,0:T(8,128)}, u32[]{:S(2)}) copy-start(f32[7,2,8,128]{3,2,1,0:T(8,128)} %param.8) | copy-start | bytes 172036
  55.5 8.2 %collective-permute-start = (f16[3,8,1024]{2,1,0:T(8,128)(2,1)S(1)}, f16[3,8,1024]{2,1,0:T(8,128)(2,1)S(1)}, u32[]{:S(2)}, u32[]{:S(2)}) collective-permute-start(f16[3,8,1024]{2,1,0:T(8,128)(2,1)S(1)} %convert_element_type.30), channel_id=1, source_target_pairs={{56,57},{57,56},{1,2},{2,1},{58,59},{59,58},{3,4},{4,3},{60,61},{6... | collective-permute-start | bytes 147464 | tf_op jit(solution)/shard_map/ppermute | solution.py:463

commit v9 on v7

--- a/solution.py
+++ b/solution.py
@@ -35,26 +35,28 @@
     return lax.broadcasted_iota(jnp.int32, shape, dim)
 
 
-def fetch_kernel(velocity, rates, dest, tile, diffusion, stiffness, *outs):
-    for source, target in zip((velocity, rates, dest, tile, diffusion, stiffness), outs):
-        target[...] = source[...]
+def flags():
     field, gz = lax.axis_index("f"), lax.axis_index("gz")
     place = lax.axis_index("z") * 4 + lax.axis_index("gy")
     odd = gz & 1
     chunk = jnp.where(odd == 1, 7 - place, place)
     first, last = chunk == 0, chunk == 7
-    flags = (field, (field >= 1) & (field <= 3), first, last, first & (gz == 0), last & (gz == 7), odd)
     row = iota((8, LANES), 0)
     table = jnp.zeros((8, LANES), F32)
-    for n, flag in enumerate(flags):
+    listed = (field, (field >= 1) & (field <= 3), first, last, first & (gz == 0), last & (gz == 7), odd)
+    for n, flag in enumerate(listed):
         table = jnp.where(row == n, flag.astype(jnp.int32).astype(F32), table)
-    outs[-1][...] = table
+    return table
 
 
 def parcel_kernel(
-    params, dest, tile, gathered, gas, weights, velocity, rates, send, moved,
+    dest, tile, gathered, gas, weights, velocity, rates, diffusion, stiffness,
+    send, moved, coeff, beta,
     tiles_buf, at_buf, source_buf, dep_buf
 ):
+    coeff[...] = diffusion[...]
+    beta[...] = stiffness[...]
+    params = flags()
     tiles_buf[...] = jnp.zeros_like(tiles_buf)
     listed = dest[...] * 16 + tile[...]
     code = [listed[0, b] for b in range(BLOCKS)]
@@ -111,7 +113,8 @@
             send[f * 8 + p] = jnp.where(flipped, pieces[7 - p], pieces[p])
 
 
-def expand_kernel(params, got, base, edge):
+def expand_kernel(got, base, edge):
+    params = flags()
     moment = jnp.concatenate([params[1:2], params[1:2]], axis=1)
     target = iota((256, 256), 0)
     k = iota((256, 256), 1)
@@ -259,7 +262,8 @@
     return jnp.sum(jnp.where(lane == field, table[...], 0.0), axis=1, keepdims=True)
 
 
-def first_kernel(params, diffusion, stiffness, base, border, basis, sums):
+def first_kernel(diffusion, stiffness, base, border, basis, sums):
+    params = flags()
     d = pick(params, diffusion)
     beta = pick(params, stiffness)
     q = load(params, base, border, 0)
@@ -274,7 +278,8 @@
     sums[...] = jnp.broadcast_to(line[None], sums.shape)
 
 
-def second_kernel(params, diffusion, stiffness, base, border, basis, got, send, state_buf):
+def second_kernel(diffusion, stiffness, base, border, basis, got, send, state_buf):
+    params = flags()
     d = pick(params, diffusion)
     beta = pick(params, stiffness)
     row = jnp.sum(got[...], axis=0)
@@ -349,7 +354,8 @@
     sums[...] = jnp.broadcast_to(pltpu.roll(table * (1.0 / 1024.0), 96, 1)[None], sums.shape)
 
 
-def final_kernel(params, diffusion, stiffness, got, sums, moved, out, velocity):
+def final_kernel(diffusion, stiffness, got, sums, moved, out, velocity):
+    params = flags()
     velocity[...] = moved[...]
     table = jnp.sum(sums[...], axis=0)
     lane = iota((8, LANES), 1)
@@ -433,46 +439,36 @@
 
 
 def body(gas_old, diffusion, stiffness, weights, velocity, rates, destination, tile_ids):
-    weights = jnp.maximum(weights, 0)
-    inputs = (
-        velocity.transpose(1, 0, 2), rates,
-        destination.reshape(1, BLOCKS), tile_ids[None], diffusion[None], stiffness[None],
-    )
-    near = pl.pallas_call(
-        fetch_kernel,
-        out_shape=[jax.ShapeDtypeStruct(value.shape, value.dtype) for value in inputs] + [shaped(8, LANES)],
-        in_specs=[pl.BlockSpec(memory_space=pltpu.VMEM) for _ in inputs],
-        out_specs=[pl.BlockSpec(memory_space=pltpu.VMEM) for _ in range(len(inputs) + 1)],
-        compiler_params=pltpu.CompilerParams(vmem_limit_bytes=LIMIT),
-    )(*inputs)
-    velocity, rates, destination, tile_ids, diffusion, stiffness, params = near
     gas = gas_old.reshape(FIELDS, BLOCKS, LANES)
+    velocity = velocity.transpose(1, 0, 2)
+    destination, tile_ids = destination.reshape(1, BLOCKS), tile_ids[None]
+    diffusion, stiffness = diffusion[None], stiffness[None]
     gathered = exchange_short(jnp.broadcast_to(gas[None, 1:], (16, 6, BLOCKS, LANES)), GX)
-    send, moved = call(
+    send, moved, diffusion, stiffness = call(
         parcel_kernel,
-        [shaped(64, BLOCKS, LANES), shaped(3, BLOCKS, LANES)],
-        "vvvvvvvv",
-        (params, destination, tile_ids, gathered, gas, weights, velocity, rates),
+        [shaped(64, BLOCKS, LANES), shaped(3, BLOCKS, LANES), shaped(1, FIELDS), shaped(1, FIELDS)],
+        "vvvvvvvvv",
+        (destination, tile_ids, gathered, gas, weights, velocity, rates, diffusion, stiffness),
         [pltpu.VMEM((BLOCKS, 8, LANES), F32), pltpu.VMEM((8, BLOCKS, LANES), F32),
          pltpu.VMEM((BLOCKS, 8, LANES), F32), pltpu.VMEM((8, BLOCKS, LANES), F32)],
     )
     got = exchange_short(send, PLANE).reshape(16, 4, BLOCKS, LANES)
     base, edge = call(
-        expand_kernel, [shaped(3, CHUNK + 2 * HALO, 1024), shaped(3, HALO, 1024)], "vv", (params, got)
+        expand_kernel, [shaped(3, CHUNK + 2 * HALO, 1024), shaped(3, HALO, 1024)], "v", (got,)
     )
     border = lax.ppermute(edge, ALL, borders())
     basis, sums = call(
         first_kernel,
         [shaped(3, CHUNK + 2 * HALO, 1024), shaped(64, 1, LANES)],
-        "vvvvv",
-        (params, diffusion, stiffness, base, border),
+        "vvvv",
+        (diffusion, stiffness, base, border),
     )
     sums = exchange(sums, GROUP)
     send = call(
         second_kernel,
         shaped(16, 4, 16, LANES),
-        "vvvvvvv",
-        (params, diffusion, stiffness, base, border, basis, sums),
+        "vvvvvv",
+        (diffusion, stiffness, base, border, basis, sums),
         [pltpu.VMEM((4 * CHUNK, 1024), F32)],
     )
     got = exchange_short(send.reshape(64, 16, LANES), PLANE)
@@ -481,8 +477,8 @@
     out, moved = call(
         final_kernel,
         [shaped(FIELDS, BLOCKS, LANES), shaped(3, BLOCKS, LANES)],
-        "vvvvvv",
-        (params, diffusion, stiffness, got, sums, moved),
+        "vvvvv",
+        (diffusion, stiffness, got, sums, moved),
     )
     return out.reshape(gas_old.shape), moved.transpose(1, 0, 2)
 

time: 109 us -> 109 us (level)
  blocking collectives: 63.1 us -> 91.9 us
  starting transfers between devices: 22.8 us -> 6.46 us
  waiting for transfers between devices: 14.3 us -> 2.29 us
    all_to_all x4 -> x5, blocking collectives: 63.1 us -> 91.9 us  [exchange(): return lax.all_to_all(value, axes, 0, 0, tiled=True)]
    all_to_all x1 -> x0, starting transfers between devices: 16.4 us -> none  [exchange(): return lax.all_to_all(value, axes, 0, 0, tiled=True)]
    all_to_all x1 -> x0, waiting for transfers between devices: 12 us -> none  [exchange(): return lax.all_to_all(value, axes, 0, 0, tiled=True)]
  transfers between devices with their start and end apart: 2 -> 1, of which waited for: 2 -> 1; matrix products, arithmetic and copies ran while one was open for 0% -> 0% of each run, Pallas kernels for 0% -> 0%
where the time goes in v9:
time: 109 us; the launch traced here: 108 us
  blocking collectives  91.9 us (84%)
  starting transfers between devices  6.46 us (6%)
  Pallas kernels  5 us (5%)
  waiting for transfers between devices  2.29 us (2%)
    all_to_all x5, blocking collectives, exchange(): return lax.all_to_all(value, axes, 0, 0, tiled=True)  91.9 us
    ppermute x1, starting transfers between devices, body(): border = lax.ppermute(edge, ALL, borders())  6.46 us
    pallas_call x6, Pallas kernels, call(): pl.pallas_call(kernel, out_shape=listed, in_specs=[pl.BlockSpec(memory_sp...  5 us
    ppermute x1, waiting for transfers between devices, body(): border = lax.ppermute(edge, ALL, borders())  2.29 us
  transfers between devices with their start and end apart: 1, of which 1 were waited for; matrix products, arithmetic and copies ran while one was open for 0% of the time, Pallas kernels for 0%

profile of v9, /device:TPU:1, one launch (start us, length us, event | category | flops | bytes accessed | tf_op | source)
XLA Modules:
  0.0 108.5 jit_solution(11471537027217338971)
XLA Ops:
  0.6 0.8 fusion
  1.4 0.1 broadcast_in_dim.16
  1.5 28.8 %all_to_all.25 = f16[16,6,16,128]{3,2,1,0:T(8,128)(2,1)S(1)} all-to-all(f16[16,6,16,128]{3,2,1,0:T(8,128)(2,1)S(1)} %broadcast_in_dim.16), channel_id=1, replica_groups=mesh['f'=8,'z'=2,'gy'=4,'gz'=8] {'f','z'}, dimensions={0} | all-to-all | bytes 786432 | tf_op jit(solution)/shard_map/all_to_all | solution.py:434
  30.3 0.0 copy-start
  30.3 0.0 copy-start.1
  30.3 0.0 copy-start.2
  30.3 0.0 copy-start.7
  30.4 0.1 convert_element_type.22.gathered
  30.4 0.0 copy-start.3
  30.4 0.0 copy-start.4
  30.5 0.0 copy-start.5
  30.5 0.0 copy-start.6
  30.5 0.9 copy-done
  31.4 0.0 copy-done.1
  31.4 0.0 copy-done.2
  31.4 0.0 copy-done.7
  31.4 0.0 copy-done.3
  31.4 0.0 copy-done.4
  31.4 0.0 copy-done.5
  31.4 0.0 copy-done.6
  31.4 1.0 shard_map.95
  32.5 22.3 %all_to_all.26 = f16[64,16,128]{2,1,0:T(8,128)(2,1)S(1)} all-to-all(f16[64,16,128]{2,1,0:T(8,128)(2,1)S(1)} %convert_element_type.23), channel_id=1, replica_groups=mesh['f'=8,'z'=2,'gy'=4,'gz'=8] {'f','z','gy'}, dimensions={0} | all-to-all | bytes 524288 | tf_op jit(solution)/shard_map/all_to_all | solution.py:434
  54.8 0.5 shard_map.96
  55.4 6.5 %collective-permute-start = (f32[3,8,1024]{2,1,0:T(8,128)S(1)}, f32[3,8,1024]{2,1,0:T(8,128)S(1)}, u32[]{:S(2)}, u32[]{:S(2)}) collective-permute-start(f32[3,8,1024]{2,1,0:T(8,128)S(1)} %get-tuple-element.16), channel_id=1, source_target_pairs={{56,57},{57,56},{1,2},{2,1},{58,59},{59,58},{3,4},{4,3},{60,61},{6... | collective-permute-start | bytes 294920 | tf_op jit(solution)/shard_map/ppermute | solution.py:459
  61.8 2.3 %collective-permute-done.border = f32[3,8,1024]{2,1,0:T(8,128)S(1)} collective-permute-done((f32[3,8,1024]{2,1,0:T(8,128)S(1)}, f32[3,8,1024]{2,1,0:T(8,128)S(1)}, u32[]{:S(2)}, u32[]{:S(2)}) %collective-permute-start) | collective-permute-done | bytes 98336 | tf_op jit(solution)/shard_map/ppermute | solution.py:459
  64.1 0.8 shard_map.97
  64.9 13.7 %all_to_all.27.got = f32[64,1,128]{2,1,0:T(1,128)S(1)} all-to-all(f32[64,1,128]{2,1,0:T(1,128)S(1)} %get-tuple-element.18), channel_id=1, replica_groups=mesh['f'=8,'z'=2,'gy'=4,'gz'=8] {'z','gy','gz'}, dimensions={0} | all-to-all | bytes 65536 | tf_op jit(solution)/shard_map/all_to_all | solution.py:434
  78.6 1.3 %shard_map.98 = f32[16,4,16,128]{3,2,1,0:T(8,128)S(1)} custom-call(f32[1,7]{1,0:T(1,128)S(1)} %get-tuple-element.12.diffusion, f32[1,7]{1,0:T(1,128)S(1)} %get-tuple-element.13.stiffness, f32[3,32,1024]{2,1,0:T(8,128)S(1)} %get-tuple-element.15.base, f32[3,8,1024]{2,1,0:T(8,128)S(1)} %collective-permute-done.border, ...), custom_call_target="tpu_custom_call" | custom-call | tf_op jit(solution)/shard_map/pallas_call | solution.py:402
  79.9 17.1 %all_to_all.28 = f16[64,16,128]{2,1,0:T(8,128)(2,1)S(1)} all-to-all(f16[64,16,128]{2,1,0:T(8,128)(2,1)S(1)} %bitcast.20), channel_id=1, replica_groups=mesh['f'=8,'z'=2,'gy'=4,'gz'=8] {'f','z','gy'}, dimensions={0} | all-to-all | bytes 524288 | tf_op jit(solution)/shard_map/all_to_all | solution.py:434
  97.0 0.2 shard_map.99
  97.2 10.1 %all_to_all.29.sums = f32[8,8,128]{2,1,0:T(8,128)S(1)} all-to-all(f32[8,8,128]{2,1,0:T(8,128)S(1)} %shard_map.99), channel_id=1, replica_groups=mesh['f'=8,'z'=2,'gy'=4,'gz'=8] {'gz'}, dimensions={0} | all-to-all | bytes 65536 | tf_op jit(solution)/shard_map/all_to_all | solution.py:434
  107.3 1.2 %shard_map.100 = (f32[7,16,128]{2,1,0:T(8,128)}, f32[3,16,128]{2,1,0:T(8,128)}) custom-call(f32[1,7]{1,0:T(1,128)S(1)} %get-tuple-element.12.diffusion, f32[1,7]{1,0:T(1,128)S(1)} %get-tuple-element.13.stiffness, f32[64,16,128]{2,1,0:T(8,128)S(1)} %convert_element_type.26.got, f32[8,8,128]{2,1,0:T(8,128)S(1)} %all_to_all.29.sums, ...), custom_call_target="tpu_custom_call" | custom-call | tf_op jit(solution)/shard_map/pallas_call | solution.py:402
  (4 shorter events, 0.2 us)
Async XLA Ops:
  30.3 1.0 copy-start
  30.3 1.0 copy-start.1
  30.3 1.0 copy-start.2
  30.3 1.0 copy-start.7
  30.4 1.0 copy-start.3
  30.4 1.0 copy-start.4
  30.5 1.0 copy-start.5
  30.5 0.9 copy-start.6
  55.4 8.7 %collective-permute-start = (f32[3,8,1024]{2,1,0:T(8,128)S(1)}, f32[3,8,1024]{2,1,0:T(8,128)S(1)}, u32[]{:S(2)}, u32[]{:S(2)}) collective-permute-start(f32[3,8,1024]{2,1,0:T(8,128)S(1)} %get-tuple-element.16), channel_id=1, source_target_pairs={{56,57},{57,56},{1,2},{2,1},{58,59},{59,58},{3,4},{4,3},{60,61},{6... | collective-permute-start | bytes 294920 | tf_op jit(solution)/shard_map/ppermute | solution.py:459

commit v10 on v8

--- a/solution.py
+++ b/solution.py
@@ -337,21 +337,21 @@
 
 
 def collect_kernel(got, sums):
-    first = iota((8, LANES), 0)
     lane = iota((8, LANES), 1)
     used = (lane >= 32) & (lane < 38)
-    table = jnp.zeros((8, LANES), F32)
+    line = jnp.zeros((1, LANES), F32)
     for f in range(8):
         rows = got[f * 8:f * 8 + 8, 8, :]
         power = jnp.where(used, pltpu.roll(rows, LANES - 18, 1), 0.0)
         rows = jnp.where(used, rows + pltpu.roll(rows, 64, 1), 0.0) * jnp.exp2(power)
-        table = jnp.where(first == f, jnp.sum(rows, axis=0, keepdims=True), table)
-    sums[...] = jnp.broadcast_to(pltpu.roll(table * (1.0 / 1024.0), 96, 1)[None], sums.shape)
+        line = line + pltpu.roll(jnp.sum(rows, axis=0, keepdims=True), (96 - 16 * f) % LANES, 1)
+    sums[...] = jnp.broadcast_to((line * (1.0 / 1024.0))[None], sums.shape)
 
 
 def final_kernel(params, diffusion, stiffness, got, sums, moved, out, velocity):
     velocity[...] = moved[...]
-    table = jnp.sum(sums[...], axis=0)
+    table = jnp.broadcast_to(jnp.sum(sums[...], axis=0), (8, LANES))
+    table = pltpu.roll(table, 0, 1, stride=16, stride_axis=0)
     lane = iota((8, LANES), 1)
     row = iota((8, 1), 0)
     m = [table[:, k:k + 1] for k in range(6)]
@@ -476,7 +476,7 @@
         [pltpu.VMEM((4 * CHUNK, 1024), F32)],
     )
     got = exchange_short(send.reshape(64, 16, LANES), PLANE)
-    sums = call(collect_kernel, shaped(8, 8, LANES), "v", (got,))
+    sums = call(collect_kernel, shaped(8, 1, LANES), "v", (got,))
     sums = exchange(sums, "gz")
     out, moved = call(
         final_kernel,

time: 109 us -> 109 us (level)
  no operation moved by 1% of the time
where the time goes in v10:
time: 109 us; the launch traced here: 108 us
  blocking collectives  63.4 us (58%)
  starting transfers between devices  22.8 us (21%)
  waiting for transfers between devices  13.8 us (13%)
  Pallas kernels  5.04 us (5%)
  local copies, waits for them, and re-layouts  1.47 us (1%)
  other arithmetic  1.09 us (1%)
    all_to_all x4, blocking collectives, exchange(): return lax.all_to_all(value, axes, 0, 0, tiled=True)  63.4 us
    all_to_all x1, starting transfers between devices, exchange(): return lax.all_to_all(value, axes, 0, 0, tiled=True)  16.4 us
    all_to_all x1, waiting for transfers between devices, exchange(): return lax.all_to_all(value, axes, 0, 0, tiled=True)  12 us
    ppermute x1, starting transfers between devices, body(): border = lax.ppermute(edge.astype(F16), ALL, borders()).astype(F32)  6.46 us
    pallas_call x6, Pallas kernels, call(): pl.pallas_call(kernel, out_shape=listed, in_specs=[pl.BlockSpec(memory_sp...  5.02 us
  transfers between devices with their start and end apart: 2, of which 2 were waited for; matrix products, arithmetic and copies ran while one was open for 0% of the time, Pallas kernels for 0%

profile of v10, /device:TPU:1, one launch (start us, length us, event | category | flops | bytes accessed | tf_op | source)
XLA Modules:
  0.0 108.4 jit_solution(10571438846399713303)
XLA Ops:
  0.6 0.8 fusion
  1.4 0.0 copy-start.7
  1.4 0.8 broadcast_in_dim.18
  2.2 0.0 copy-start.1
  2.2 0.0 copy-start.6
  2.2 16.4 %all-to-all-start = ((f16[16,6,16,128]{3,2,1,0:T(8,128)(2,1)}), f16[16,6,16,128]{3,2,1,0:T(8,128)(2,1)S(1)}, u32[]{:S(2)}, u32[]{:S(2)}) async-start(f16[16,6,16,128]{3,2,1,0:T(8,128)(2,1)} %broadcast_in_dim.18), calls=%async_computation | async-start | bytes 786432 | tf_op jit(solution)/shard_map/all_to_all | solution.py:428
  18.6 0.0 copy-start.2
  18.6 0.0 copy-start.3
  18.6 0.0 copy-start.4
  18.6 0.0 copy-start.5
  18.7 0.0 copy-done.1
  18.7 0.0 copy-done.6
  18.7 0.6 copy-done.2
  19.3 0.0 copy-done.3
  19.3 0.0 copy-done.4
  19.3 0.0 copy-done.5
  19.3 0.0 copy-done.7
  19.4 0.0 copy-start
  19.4 12.0 %all-to-all-done = f16[16,6,16,128]{3,2,1,0:T(8,128)(2,1)S(1)} async-done(((f16[16,6,16,128]{3,2,1,0:T(8,128)(2,1)}), f16[16,6,16,128]{3,2,1,0:T(8,128)(2,1)S(1)}, u32[]{:S(2)}, u32[]{:S(2)}) %all-to-all-start) | async-done | bytes 393248 | tf_op jit(solution)/shard_map/all_to_all | solution.py:428
  31.4 0.1 convert_element_type.28.gathered
  31.5 0.0 copy-done
  31.5 1.0 shard_map.96
  32.6 22.3 %all_to_all.25 = f16[64,16,128]{2,1,0:T(8,128)(2,1)S(1)} all-to-all(f16[64,16,128]{2,1,0:T(8,128)(2,1)S(1)} %convert_element_type.29), channel_id=1, replica_groups=mesh['f'=8,'z'=2,'gy'=4,'gz'=8] {'f','z','gy'}, dimensions={0} | all-to-all | bytes 524288 | tf_op jit(solution)/shard_map/all_to_all | solution.py:428
  54.9 0.5 shard_map.97
  55.5 6.5 %collective-permute-start = (f16[3,8,1024]{2,1,0:T(8,128)(2,1)S(1)}, f16[3,8,1024]{2,1,0:T(8,128)(2,1)S(1)}, u32[]{:S(2)}, u32[]{:S(2)}) collective-permute-start(f16[3,8,1024]{2,1,0:T(8,128)(2,1)S(1)} %convert_element_type.30), channel_id=1, source_target_pairs={{56,57},{57,56},{1,2},{2,1},{58,59},{59,58},{3,4},{4,3},{60,61},{6... | collective-permute-start | bytes 147464 | tf_op jit(solution)/shard_map/ppermute | solution.py:463
  62.0 1.8 %collective-permute-done = f16[3,8,1024]{2,1,0:T(8,128)(2,1)S(1)} collective-permute-done((f16[3,8,1024]{2,1,0:T(8,128)(2,1)S(1)}, f16[3,8,1024]{2,1,0:T(8,128)(2,1)S(1)}, u32[]{:S(2)}, u32[]{:S(2)}) %collective-permute-start) | collective-permute-done | bytes 49184 | tf_op jit(solution)/shard_map/ppermute | solution.py:463
  63.7 0.8 shard_map.98
  64.5 13.7 %all_to_all.26.got = f32[64,1,128]{2,1,0:T(1,128)S(1)} all-to-all(f32[64,1,128]{2,1,0:T(1,128)S(1)} %get-tuple-element.28), channel_id=1, replica_groups=mesh['f'=8,'z'=2,'gy'=4,'gz'=8] {'z','gy','gz'}, dimensions={0} | all-to-all | bytes 65536 | tf_op jit(solution)/shard_map/all_to_all | solution.py:428
  78.2 1.3 %shard_map.99 = f32[16,4,16,128]{3,2,1,0:T(8,128)S(1)} custom-call(f32[8,128]{1,0:T(8,128)S(1)} %get-tuple-element.17.params, f32[1,7]{1,0:T(1,128)S(1)} %get-tuple-element.18.diffusion, f32[1,7]{1,0:T(1,128)S(1)} %get-tuple-element.19.stiffness, f32[3,32,1024]{2,1,0:T(8,128)S(1)} %get-tuple-element.25.base, f32[3,8,1024]{2,1,0:T(8,128)S(1)} %convert_element_type.31.border, ...), custom_call_target="tpu_custom_call" | custom-call | tf_op jit(solution)/shard_map/pallas_call | solution.py:396
  79.5 17.5 %all_to_all.27 = f16[64,16,128]{2,1,0:T(8,128)(2,1)S(1)} all-to-all(f16[64,16,128]{2,1,0:T(8,128)(2,1)S(1)} %bitcast.20), channel_id=1, replica_groups=mesh['f'=8,'z'=2,'gy'=4,'gz'=8] {'f','z','gy'}, dimensions={0} | all-to-all | bytes 524288 | tf_op jit(solution)/shard_map/all_to_all | solution.py:428
  97.1 0.2 shard_map.100
  97.3 9.9 %all_to_all.28.sums = f32[8,1,128]{2,1,0:T(1,128)S(1)} all-to-all(f32[8,1,128]{2,1,0:T(1,128)S(1)} %shard_map.100), channel_id=1, replica_groups=mesh['f'=8,'z'=2,'gy'=4,'gz'=8] {'gz'}, dimensions={0} | all-to-all | bytes 8192 | tf_op jit(solution)/shard_map/all_to_all | solution.py:428
  107.2 1.2 %shard_map.101 = (f32[7,16,128]{2,1,0:T(8,128)}, f32[3,16,128]{2,1,0:T(8,128)}) custom-call(f32[8,128]{1,0:T(8,128)S(1)} %get-tuple-element.17.params, f32[1,7]{1,0:T(1,128)S(1)} %get-tuple-element.18.diffusion, f32[1,7]{1,0:T(1,128)S(1)} %get-tuple-element.19.stiffness, f32[64,16,128]{2,1,0:T(8,128)S(1)} %convert_element_type.34.got, ...), custom_call_target="tpu_custom_call" | custom-call | tf_op jit(solution)/shard_map/pallas_call | solution.py:396
  (8 shorter events, 0.2 us)
Async XLA Ops:
  1.4 17.9 %copy-start.7 = (bf16[16,128,128]{2,1,0:T(8,128)(2,1)S(1)}, bf16[16,128,128]{2,1,0:T(8,128)(2,1)}, u32[]{:S(2)}) copy-start(bf16[16,128,128]{2,1,0:T(8,128)(2,1)} %param.11) | copy-start | bytes 1572868
  2.2 16.4 %copy-start.1 = (bf16[16,3,128]{2,0,1:T(8,128)(2,1)S(1)}, bf16[16,3,128]{2,0,1:T(8,128)(2,1)}, u32[]{:S(2)}) copy-start(bf16[16,3,128]{2,0,1:T(8,128)(2,1)} %param.12) | copy-start | bytes 36868
  2.2 16.4 %copy-start.6 = (f32[7]{0:T(128)S(1)}, f32[7]{0:T(128)}, u32[]{:S(2)}) copy-start(f32[7]{0:T(128)} %param.10) | copy-start | bytes 88
  2.2 29.2 %all-to-all-start = ((f16[16,6,16,128]{3,2,1,0:T(8,128)(2,1)}), f16[16,6,16,128]{3,2,1,0:T(8,128)(2,1)S(1)}, u32[]{:S(2)}, u32[]{:S(2)}) async-start(f16[16,6,16,128]{3,2,1,0:T(8,128)(2,1)} %broadcast_in_dim.18), calls=%async_computation | async-start | bytes 786432 | tf_op jit(solution)/shard_map/all_to_all | solution.py:428
  18.6 0.7 copy-start.2
  18.6 0.7 copy-start.3
  18.6 0.7 copy-start.4
  18.6 0.7 copy-start.5
  19.4 12.1 %copy-start = (f32[7,2,8,128]{3,2,1,0:T(8,128)S(1)}, f32[7,2,8,128]{3,2,1,0:T(8,128)}, u32[]{:S(2)}) copy-start(f32[7,2,8,128]{3,2,1,0:T(8,128)} %param.8) | copy-start | bytes 172036
  55.5 8.2 %collective-permute-start = (f16[3,8,1024]{2,1,0:T(8,128)(2,1)S(1)}, f16[3,8,1024]{2,1,0:T(8,128)(2,1)S(1)}, u32[]{:S(2)}, u32[]{:S(2)}) collective-permute-start(f16[3,8,1024]{2,1,0:T(8,128)(2,1)S(1)} %convert_element_type.30), channel_id=1, source_target_pairs={{56,57},{57,56},{1,2},{2,1},{58,59},{59,58},{3,4},{4,3},{60,61},{6... | collective-permute-start | bytes 147464 | tf_op jit(solution)/shard_map/ppermute | solution.py:463

commit v11 on v10

--- a/solution.py
+++ b/solution.py
@@ -460,7 +460,7 @@
     base, edge = call(
         expand_kernel, [shaped(3, CHUNK + 2 * HALO, 1024), shaped(3, HALO, 1024)], "vv", (params, got)
     )
-    border = lax.ppermute(edge.astype(F16), ALL, borders()).astype(F32)
+    border = lax.ppermute(edge, ALL, borders())
     basis, sums = call(
         first_kernel,
         [shaped(3, CHUNK + 2 * HALO, 1024), shaped(64, 1, LANES)],

time: 109 us -> 109 us (level)
  no operation moved by 1% of the time
where the time goes in v11:
time: 109 us; the launch traced here: 108 us
  blocking collectives  62.9 us (58%)
  starting transfers between devices  22.8 us (21%)
  waiting for transfers between devices  14.3 us (13%)
  Pallas kernels  5.04 us (5%)
  local copies, waits for them, and re-layouts  1.47 us (1%)
    all_to_all x4, blocking collectives, exchange(): return lax.all_to_all(value, axes, 0, 0, tiled=True)  62.9 us
    all_to_all x1, starting transfers between devices, exchange(): return lax.all_to_all(value, axes, 0, 0, tiled=True)  16.4 us
    all_to_all x1, waiting for transfers between devices, exchange(): return lax.all_to_all(value, axes, 0, 0, tiled=True)  12 us
    ppermute x1, starting transfers between devices, body(): border = lax.ppermute(edge, ALL, borders())  6.46 us
    pallas_call x6, Pallas kernels, call(): pl.pallas_call(kernel, out_shape=listed, in_specs=[pl.BlockSpec(memory_sp...  5.02 us
    ppermute x1, waiting for transfers between devices, body(): border = lax.ppermute(edge, ALL, borders())  2.29 us
  transfers between devices with their start and end apart: 2, of which 2 were waited for; matrix products, arithmetic and copies ran while one was open for 0% of the time, Pallas kernels for 0%

profile of v11, /device:TPU:1, one launch (start us, length us, event | category | flops | bytes accessed | tf_op | source)
XLA Modules:
  0.0 108.4 jit_solution(12495586618009844332)
XLA Ops:
  0.6 0.8 fusion
  1.4 0.0 copy-start.7
  1.4 0.8 broadcast_in_dim.18
  2.2 0.0 copy-start.1
  2.2 0.0 copy-start.6
  2.2 16.4 %all-to-all-start = ((f16[16,6,16,128]{3,2,1,0:T(8,128)(2,1)}), f16[16,6,16,128]{3,2,1,0:T(8,128)(2,1)S(1)}, u32[]{:S(2)}, u32[]{:S(2)}) async-start(f16[16,6,16,128]{3,2,1,0:T(8,128)(2,1)} %broadcast_in_dim.18), calls=%async_computation | async-start | bytes 786432 | tf_op jit(solution)/shard_map/all_to_all | solution.py:428
  18.6 0.0 copy-start.2
  18.6 0.0 copy-start.3
  18.6 0.0 copy-start.4
  18.6 0.0 copy-start.5
  18.7 0.0 copy-done.1
  18.7 0.0 copy-done.6
  18.7 0.6 copy-done.2
  19.3 0.0 copy-done.3
  19.3 0.0 copy-done.4
  19.3 0.0 copy-done.5
  19.3 0.0 copy-done.7
  19.4 0.0 copy-start
  19.4 12.0 %all-to-all-done = f16[16,6,16,128]{3,2,1,0:T(8,128)(2,1)S(1)} async-done(((f16[16,6,16,128]{3,2,1,0:T(8,128)(2,1)}), f16[16,6,16,128]{3,2,1,0:T(8,128)(2,1)S(1)}, u32[]{:S(2)}, u32[]{:S(2)}) %all-to-all-start) | async-done | bytes 393248 | tf_op jit(solution)/shard_map/all_to_all | solution.py:428
  31.4 0.1 convert_element_type.22.gathered
  31.5 0.0 copy-done
  31.5 1.0 shard_map.96
  32.6 22.3 %all_to_all.25 = f16[64,16,128]{2,1,0:T(8,128)(2,1)S(1)} all-to-all(f16[64,16,128]{2,1,0:T(8,128)(2,1)S(1)} %convert_element_type.23), channel_id=1, replica_groups=mesh['f'=8,'z'=2,'gy'=4,'gz'=8] {'f','z','gy'}, dimensions={0} | all-to-all | bytes 524288 | tf_op jit(solution)/shard_map/all_to_all | solution.py:428
  54.9 0.5 shard_map.97
  55.5 6.5 %collective-permute-start = (f32[3,8,1024]{2,1,0:T(8,128)S(1)}, f32[3,8,1024]{2,1,0:T(8,128)S(1)}, u32[]{:S(2)}, u32[]{:S(2)}) collective-permute-start(f32[3,8,1024]{2,1,0:T(8,128)S(1)} %get-tuple-element.26), channel_id=1, source_target_pairs={{56,57},{57,56},{1,2},{2,1},{58,59},{59,58},{3,4},{4,3},{60,61},{6... | collective-permute-start | bytes 294920 | tf_op jit(solution)/shard_map/ppermute | solution.py:463
  61.9 2.3 %collective-permute-done.border = f32[3,8,1024]{2,1,0:T(8,128)S(1)} collective-permute-done((f32[3,8,1024]{2,1,0:T(8,128)S(1)}, f32[3,8,1024]{2,1,0:T(8,128)S(1)}, u32[]{:S(2)}, u32[]{:S(2)}) %collective-permute-start) | collective-permute-done | bytes 98336 | tf_op jit(solution)/shard_map/ppermute | solution.py:463
  64.2 0.8 shard_map.98
  65.0 13.7 %all_to_all.26.got = f32[64,1,128]{2,1,0:T(1,128)S(1)} all-to-all(f32[64,1,128]{2,1,0:T(1,128)S(1)} %get-tuple-element.28), channel_id=1, replica_groups=mesh['f'=8,'z'=2,'gy'=4,'gz'=8] {'z','gy','gz'}, dimensions={0} | all-to-all | bytes 65536 | tf_op jit(solution)/shard_map/all_to_all | solution.py:428
  78.7 1.3 %shard_map.99 = f32[16,4,16,128]{3,2,1,0:T(8,128)S(1)} custom-call(f32[8,128]{1,0:T(8,128)S(1)} %get-tuple-element.17.params, f32[1,7]{1,0:T(1,128)S(1)} %get-tuple-element.18.diffusion, f32[1,7]{1,0:T(1,128)S(1)} %get-tuple-element.19.stiffness, f32[3,32,1024]{2,1,0:T(8,128)S(1)} %get-tuple-element.25.base, f32[3,8,1024]{2,1,0:T(8,128)S(1)} %collective-permute-done.border, ...), custom_call_target="tpu_custom_call" | custom-call | tf_op jit(solution)/shard_map/pallas_call | solution.py:396
  80.0 17.1 %all_to_all.27 = f16[64,16,128]{2,1,0:T(8,128)(2,1)S(1)} all-to-all(f16[64,16,128]{2,1,0:T(8,128)(2,1)S(1)} %bitcast.20), channel_id=1, replica_groups=mesh['f'=8,'z'=2,'gy'=4,'gz'=8] {'f','z','gy'}, dimensions={0} | all-to-all | bytes 524288 | tf_op jit(solution)/shard_map/all_to_all | solution.py:428
  97.1 0.2 shard_map.100
  97.3 9.9 %all_to_all.28.sums = f32[8,1,128]{2,1,0:T(1,128)S(1)} all-to-all(f32[8,1,128]{2,1,0:T(1,128)S(1)} %shard_map.100), channel_id=1, replica_groups=mesh['f'=8,'z'=2,'gy'=4,'gz'=8] {'gz'}, dimensions={0} | all-to-all | bytes 8192 | tf_op jit(solution)/shard_map/all_to_all | solution.py:428
  107.2 1.2 %shard_map.101 = (f32[7,16,128]{2,1,0:T(8,128)}, f32[3,16,128]{2,1,0:T(8,128)}) custom-call(f32[8,128]{1,0:T(8,128)S(1)} %get-tuple-element.17.params, f32[1,7]{1,0:T(1,128)S(1)} %get-tuple-element.18.diffusion, f32[1,7]{1,0:T(1,128)S(1)} %get-tuple-element.19.stiffness, f32[64,16,128]{2,1,0:T(8,128)S(1)} %convert_element_type.26.got, ...), custom_call_target="tpu_custom_call" | custom-call | tf_op jit(solution)/shard_map/pallas_call | solution.py:396
  (6 shorter events, 0.2 us)
Async XLA Ops:
  1.4 17.9 %copy-start.7 = (bf16[16,128,128]{2,1,0:T(8,128)(2,1)S(1)}, bf16[16,128,128]{2,1,0:T(8,128)(2,1)}, u32[]{:S(2)}) copy-start(bf16[16,128,128]{2,1,0:T(8,128)(2,1)} %param.11) | copy-start | bytes 1572868
  2.2 16.4 %copy-start.1 = (bf16[16,3,128]{2,0,1:T(8,128)(2,1)S(1)}, bf16[16,3,128]{2,0,1:T(8,128)(2,1)}, u32[]{:S(2)}) copy-start(bf16[16,3,128]{2,0,1:T(8,128)(2,1)} %param.12) | copy-start | bytes 36868
  2.2 16.4 %copy-start.6 = (f32[7]{0:T(128)S(1)}, f32[7]{0:T(128)}, u32[]{:S(2)}) copy-start(f32[7]{0:T(128)} %param.10) | copy-start | bytes 88
  2.2 29.2 %all-to-all-start = ((f16[16,6,16,128]{3,2,1,0:T(8,128)(2,1)}), f16[16,6,16,128]{3,2,1,0:T(8,128)(2,1)S(1)}, u32[]{:S(2)}, u32[]{:S(2)}) async-start(f16[16,6,16,128]{3,2,1,0:T(8,128)(2,1)} %broadcast_in_dim.18), calls=%async_computation | async-start | bytes 786432 | tf_op jit(solution)/shard_map/all_to_all | solution.py:428
  18.6 0.7 copy-start.2
  18.6 0.7 copy-start.3
  18.6 0.7 copy-start.4
  18.6 0.7 copy-start.5
  19.4 12.1 %copy-start = (f32[7,2,8,128]{3,2,1,0:T(8,128)S(1)}, f32[7,2,8,128]{3,2,1,0:T(8,128)}, u32[]{:S(2)}) copy-start(f32[7,2,8,128]{3,2,1,0:T(8,128)} %param.8) | copy-start | bytes 172036
  55.5 8.7 %collective-permute-start = (f32[3,8,1024]{2,1,0:T(8,128)S(1)}, f32[3,8,1024]{2,1,0:T(8,128)S(1)}, u32[]{:S(2)}, u32[]{:S(2)}) collective-permute-start(f32[3,8,1024]{2,1,0:T(8,128)S(1)} %get-tuple-element.26), channel_id=1, source_target_pairs={{56,57},{57,56},{1,2},{2,1},{58,59},{59,58},{3,4},{4,3},{60,61},{6... | collective-permute-start | bytes 294920 | tf_op jit(solution)/shard_map/ppermute | solution.py:463
